TPU v7x, 768 devices: a whole 4x8x12 slice. The times are simulated.
768 devices in a mesh: comp: 2 (over core), gx: 24 (over z_hi, y), gy: 16 (over z_lo, x).
Axes of the slice: x: 4, y: 8, z: 12 (z_hi: 3, z_lo: 4; z = z_hi * 4 + z_lo), core: 2. Of those that a mesh axis runs over, the one named last changes fastest.
Arguments:
- ocean_state: float32 [2, 8, 8, 96, 2048], P('comp', None, None, 'gx', 'gy'), may hold values from -4 to 4
- land_sea: int32 [96, 2048], P('gx', 'gy'), may hold values 0 or 1
- depth_levels: int32 [96, 2048], P('gx', 'gy'), may hold values from 1 to 8
- photic_production_factors: float32 [8], replicated, may hold values from 0.1 to 0.5
- species_decay_factors: float32 [8], replicated, may hold values from 0.05 to 0.3
Outputs:
- advanced: float32 [2, 8, 8, 96, 2048], P('comp', None, None, 'gx', 'gy')
All inputs are finite; a program needn't handle non-finite values. No bound on the sum of `land_sea` on one device may be relied on, other than what follows from the above.
Results may differ from a plain program's by a relative error of at most 0.0003.
Values sent between devices are 32-bit elements; how exact they have to be, the bound alone decides.
No kernel may reach another device: no remote copies, remote signals or barrier semaphores. Data moves between devices by JAX's collectives and lax.ppermute only.
A program may use at most 32 MiB of HBM per device.

v0:
```python
import jax
import jax.numpy as jnp
from jax import lax
from jax.sharding import PartitionSpec as P

DYN_STEPS = 4
TRACER_STEPS = 2


CORIOLIS = 0.2
PRESSURE = 0.01


def with_halo(cells, sides, width):
    for axis, dim in sides:
        count = lax.axis_size(axis)
        ends = count - 1
        head = lax.slice_in_dim(cells, 0, width, axis=dim)
        tail = lax.slice_in_dim(cells, cells.shape[dim] - width, cells.shape[dim], axis=dim)
        cells = jnp.concatenate(
            [
                lax.ppermute(tail, axis, [(i, (i + 1) % count) for i in range(ends)]),
                cells,
                lax.ppermute(head, axis, [((i + 1) % count, i) for i in range(ends)]),
            ],
            axis=dim,
        )
    return cells


def shifted(shard, axis, by):
    count = lax.axis_size(axis)
    pairs = [(i, i + by) for i in range(count) if 0 <= i + by < count]
    return lax.ppermute(shard, axis, pairs)


def minmod(left_diff, right_diff):
    return (
        0.5
        * (jnp.sign(left_diff) + jnp.sign(right_diff))
        * jnp.minimum(jnp.abs(left_diff), jnp.abs(right_diff))
    )


def limited(far_low, near_low, near_high, far_high, face_speed):
    jump_mid = near_high - near_low
    left_value = near_low + 0.5 * minmod(jump_mid, near_low - far_low)
    right_value = near_high - 0.5 * minmod(jump_mid, far_high - near_high)
    return jnp.maximum(face_speed, 0.0) * left_value + jnp.minimum(face_speed, 0.0) * right_value


def advect(quantity, zonal_current, meridional_current, marine_site_indicator):
    rows_x = quantity.shape[-2] - 4
    rows_y = quantity.shape[-1] - 4
    strip = quantity[..., 2 : rows_y + 2]
    face_speed = 0.5 * (
        zonal_current[..., 0 : rows_x + 1, 1 : rows_y + 1]
        + zonal_current[..., 1 : rows_x + 2, 1 : rows_y + 1]
    )
    face_speed = (
        face_speed
        * marine_site_indicator[..., 0 : rows_x + 1, 1 : rows_y + 1]
        * marine_site_indicator[..., 1 : rows_x + 2, 1 : rows_y + 1]
    )
    face_flux = limited(
        strip[..., 0 : rows_x + 1, :],
        strip[..., 1 : rows_x + 2, :],
        strip[..., 2 : rows_x + 3, :],
        strip[..., 3 : rows_x + 4, :],
        face_speed,
    )
    change = face_flux[..., :-1, :] - face_flux[..., 1:, :]
    strip = quantity[..., 2 : rows_x + 2, :]
    face_speed = 0.5 * (
        meridional_current[..., 1 : rows_x + 1, 0 : rows_y + 1]
        + meridional_current[..., 1 : rows_x + 1, 1 : rows_y + 2]
    )
    face_speed = (
        face_speed
        * marine_site_indicator[..., 1 : rows_x + 1, 0 : rows_y + 1]
        * marine_site_indicator[..., 1 : rows_x + 1, 1 : rows_y + 2]
    )
    face_flux = limited(
        strip[..., 0 : rows_y + 1],
        strip[..., 1 : rows_y + 2],
        strip[..., 2 : rows_y + 3],
        strip[..., 3 : rows_y + 4],
        face_speed,
    )
    return change + face_flux[..., :-1] - face_flux[..., 1:]


def vertical_mix(quantity, vertical_stirring_coefficient):
    below_values = jnp.concatenate([quantity[..., 1:, :, :], quantity[..., -1:, :, :]], axis=-3)
    face_flux = vertical_stirring_coefficient * (below_values - quantity)
    from_above = jnp.concatenate(
        [jnp.zeros_like(face_flux[..., :1, :, :]), face_flux[..., :-1, :, :]], axis=-3
    )
    return face_flux - from_above


def lateral_spreading_coefficient(
    seawater_heat_state, dissolved_salt_content, marine_site_indicator
):
    seawater_mass_per_volume = 0.8 * dissolved_salt_content - 0.2 * seawater_heat_state
    jump_down = seawater_mass_per_volume[1:] - seawater_mass_per_volume[:-1]
    vertical_stirring_coefficient = (
        (0.02 + 0.1 / (1.0 + 4.0 * jump_down * jump_down))
        * marine_site_indicator[1:]
        * marine_site_indicator[:-1]
    )
    return jnp.concatenate(
        [vertical_stirring_coefficient, jnp.zeros_like(vertical_stirring_coefficient[:1])], axis=0
    )


def absorption(chlorophyll, marine_site_indicator):
    return (0.04 + 0.05 * chlorophyll * chlorophyll) * marine_site_indicator


def heating(absorb):
    lower_light = jnp.exp(-jnp.cumsum(absorb, axis=0))
    upper_light = jnp.concatenate([jnp.ones_like(lower_light[:1]), lower_light[:-1]], axis=0)
    return 0.5 * (upper_light - lower_light)


def dynamics_step(padded_with_halo_rim, marine_site_indicator, heat_rate):
    prognostic = padded_with_halo_rim[:4]
    interior = prognostic[..., 2:-2, 2:-2]
    wet_inner = marine_site_indicator[:, 2:-2, 2:-2]
    advected = advect(
        prognostic,
        padded_with_halo_rim[0, :, 1:-1, 1:-1],
        padded_with_halo_rim[1, :, 1:-1, 1:-1],
        marine_site_indicator[:, 1:-1, 1:-1],
    )
    seawater_mass_per_volume = (
        0.8 * padded_with_halo_rim[3] - 0.2 * padded_with_halo_rim[2]
    ) * marine_site_indicator
    pressure = jnp.cumsum(seawater_mass_per_volume, axis=0)
    slope_x = 0.5 * (pressure[:, 3:-1, 2:-2] - pressure[:, 1:-3, 2:-2])
    slope_y = 0.5 * (pressure[:, 2:-2, 3:-1] - pressure[:, 2:-2, 1:-3])
    vertical_stirring_coefficient = lateral_spreading_coefficient(
        interior[2], interior[3], wet_inner
    )
    forcing = jnp.stack(
        [
            CORIOLIS * interior[1] - PRESSURE * slope_x,
            -CORIOLIS * interior[0] - PRESSURE * slope_y,
            heat_rate,
            jnp.zeros_like(heat_rate),
        ]
    )
    tendency = (
        advected + vertical_mix(interior, vertical_stirring_coefficient) + forcing
    ) * wet_inner
    updated = (
        interior + 1.5 * tendency - 0.5 * padded_with_halo_rim[4:, :, 2:-2, 2:-2]
    ) * wet_inner
    return jnp.concatenate([updated, tendency], axis=0)


def step_biogeochem_species(
    padded_with_halo_rim,
    zonal_current,
    meridional_current,
    seawater_heat_state,
    vertical_stirring_coefficient,
    marine_site_indicator,
    species_production,
    species_decay_factor,
):
    interior = padded_with_halo_rim[:, :, 2:-2, 2:-2]
    wet_inner = marine_site_indicator[:, 2:-2, 2:-2]
    advected = advect(
        padded_with_halo_rim,
        zonal_current,
        meridional_current,
        marine_site_indicator[:, 1:-1, 1:-1],
    )
    solar_irradiance = jnp.exp(-jnp.cumsum(absorption(interior[0], wet_inner), axis=0))
    net_species_factor = (
        species_production[:, None, None, None]
        * (solar_irradiance * jnp.exp(0.1 * seawater_heat_state))[None]
        - species_decay_factor[:, None, None, None]
    )
    return (
        interior
        + advected
        + vertical_mix(interior, vertical_stirring_coefficient)
        + net_species_factor * interior
    ) * wet_inner


def wet_cells(land_sea, depth_levels, levels):
    level_index = lax.broadcasted_iota(jnp.int32, (levels,) + land_sea.shape, 0)
    return jnp.where((land_sea[None] == 1) & (level_index < depth_levels[None]), 1.0, 0.0).astype(
        jnp.float32
    )


def trim_rim(values, margin):
    if margin == 0:
        return values
    return values[..., margin : values.shape[-2] - margin, margin : values.shape[-1] - margin]


def local(ocean_state, land_sea, depth_levels, photic_production_factors, species_decay_factors):
    fields = ocean_state[0]
    levels = fields.shape[1]
    is_dynamics = lax.axis_index("comp") == 0
    own_wet = wet_cells(land_sea, depth_levels, levels)
    rim_width = 2
    joined = jnp.concatenate([fields, own_wet[None]], axis=0)
    extended = with_halo(joined, (("gx", 2), ("gy", 3)), rim_width)
    marine_site_indicator = extended[-1]
    padded_with_halo_rim = extended[:-1]

    def dynamics_message():
        edge_fields = trim_rim(padded_with_halo_rim[:2], rim_width - 1)
        middle = trim_rim(padded_with_halo_rim[2:4], rim_width)
        vertical_stirring_coefficient = lateral_spreading_coefficient(
            middle[0], middle[1], trim_rim(marine_site_indicator, rim_width)
        )
        return (edge_fields, jnp.stack([middle[0], vertical_stirring_coefficient]))

    def quiet_message():
        edge_fields = jnp.zeros((2, levels, fields.shape[2] + 2, fields.shape[3] + 2), jnp.float32)
        return (edge_fields, jnp.zeros((2,) + fields.shape[1:], jnp.float32))

    sent_edge, sent_column = lax.cond(is_dynamics, dynamics_message, quiet_message)
    edge_in, column_in = shifted((sent_edge, sent_column), "comp", 1)

    def tracer_message():
        absorb = absorption(
            trim_rim(padded_with_halo_rim[0], 2), trim_rim(marine_site_indicator, 2)
        )
        return absorb

    def quiet_profile():
        return jnp.zeros_like(trim_rim(marine_site_indicator, 2))

    outgoing = lax.cond(is_dynamics, quiet_profile, tracer_message)
    incoming = shifted(outgoing, "comp", -1)
    heat_rate = lax.cond(is_dynamics, lambda: heating(incoming), lambda: incoming)

    def tracer_update(source):
        return step_biogeochem_species(
            trim_rim(source, rim_width - 2),
            edge_in[0],
            edge_in[1],
            column_in[0],
            column_in[1],
            trim_rim(marine_site_indicator, rim_width - 2),
            photic_production_factors,
            species_decay_factors,
        )

    current = fields
    for step_index in range(DYN_STEPS):
        if step_index > 0:
            padded_with_halo_rim = with_halo(current, (("gx", 2), ("gy", 3)), 2)
        source = padded_with_halo_rim
        previous = current
        if step_index < TRACER_STEPS:
            current = lax.cond(
                is_dynamics,
                lambda: dynamics_step(source, marine_site_indicator, heat_rate),
                lambda: tracer_update(source),
            )
        else:
            current = lax.cond(
                is_dynamics,
                lambda: dynamics_step(source, marine_site_indicator, heat_rate),
                lambda: previous,
            )
    return current[None]


def solution(mesh):
    placed = (P("comp", None, None, "gx", "gy"), P("gx", "gy"), P("gx", "gy"), P(), P())
    return jax.shard_map(
        local,
        mesh=mesh,
        in_specs=placed,
        out_specs=P("comp", None, None, "gx", "gy"),
        check_vma=False,
    )
```

profile of v0, /device:TPU:62, one launch (start us, length us, event | category | flops | bytes accessed | tf_op | source)
XLA Modules:
  0.0 148.4 jit_solution(829587441575413401)
XLA Ops:
  1.9 10.1 %collective-permute-start = (f32[9,8,2,128]{3,2,1,0:T(2,128)S(1)}, f32[9,8,2,128]{3,2,1,0:T(2,128)S(1)}, u32[]{:S(2)}, u32[]{:S(2)}) collective-permute-start(f32[9,8,2,128]{3,2,1,0:T(2,128)S(1)} %get-tuple-element.195), channel_id=1, source_target_pairs={{0,16},{16,32},{32,48},{48,64},{64,80},{80,96},{96,112},{112,128},... | collective-permute-start | bytes 221192 | tf_op jit(solution)/shard_map/ppermute | solution.py:22
  12.0 1.9 %collective-permute-start.1 = (f32[9,8,2,128]{3,2,1,0:T(2,128)S(1)}, f32[9,8,2,128]{3,2,1,0:T(2,128)S(1)}, u32[]{:S(2)}, u32[]{:S(2)}) collective-permute-start(f32[9,8,2,128]{3,2,1,0:T(2,128)S(1)} %get-tuple-element.196), channel_id=1, source_target_pairs={{16,0},{32,16},{48,32},{64,48},{80,64},{96,80},{112,96},{128,112},... | collective-permute-start | bytes 221192 | tf_op jit(solution)/shard_map/ppermute | solution.py:24
  13.9 11.1 %collective-permute-done.1 = f32[9,8,2,128]{3,2,1,0:T(2,128)S(1)} collective-permute-done((f32[9,8,2,128]{3,2,1,0:T(2,128)S(1)}, f32[9,8,2,128]{3,2,1,0:T(2,128)S(1)}, u32[]{:S(2)}, u32[]{:S(2)}) %collective-permute-start.1) | collective-permute-done | bytes 73760 | tf_op jit(solution)/shard_map/ppermute | solution.py:24
  25.3 4.3 %collective-permute-start.2 = (f32[9,8,8,2]{3,2,1,0:T(8,128)S(1)}, f32[9,8,8,2]{3,2,1,0:T(8,128)S(1)}, u32[]{:S(2)}, u32[]{:S(2)}) collective-permute-start(f32[9,8,8,2]{3,2,1,0:T(8,128)S(1)} %get-tuple-element.187), channel_id=1, source_target_pairs={{0,1},{1,2},{2,3},{3,4},{4,5},{5,6},{6,7},{7,8},{8,9},{9,10},{10,1... | collective-permute-start | bytes 13832 | tf_op jit(solution)/shard_map/ppermute | solution.py:22
  29.6 1.9 %collective-permute-start.3 = (f32[9,8,8,2]{3,2,1,0:T(8,128)S(1)}, f32[9,8,8,2]{3,2,1,0:T(8,128)S(1)}, u32[]{:S(2)}, u32[]{:S(2)}) collective-permute-start(f32[9,8,8,2]{3,2,1,0:T(8,128)S(1)} %get-tuple-element.188), channel_id=1, source_target_pairs={{1,0},{2,1},{3,2},{4,3},{5,4},{6,5},{7,6},{8,7},{9,8},{10,9},{11,1... | collective-permute-start | bytes 13832 | tf_op jit(solution)/shard_map/ppermute | solution.py:24
  31.5 2.4 %collective-permute-done.2 = f32[9,8,8,2]{3,2,1,0:T(8,128)S(1)} collective-permute-done((f32[9,8,8,2]{3,2,1,0:T(8,128)S(1)}, f32[9,8,8,2]{3,2,1,0:T(8,128)S(1)}, u32[]{:S(2)}, u32[]{:S(2)}) %collective-permute-start.2) | collective-permute-done | bytes 4640 | tf_op jit(solution)/shard_map/ppermute | solution.py:22
  33.9 6.4 %collective-permute-done.3 = f32[9,8,8,2]{3,2,1,0:T(8,128)S(1)} collective-permute-done((f32[9,8,8,2]{3,2,1,0:T(8,128)S(1)}, f32[9,8,8,2]{3,2,1,0:T(8,128)S(1)}, u32[]{:S(2)}, u32[]{:S(2)}) %collective-permute-start.3) | collective-permute-done | bytes 4640 | tf_op jit(solution)/shard_map/ppermute | solution.py:24
  47.9 3.4 %conditional.10 = (f32[8,8,4,128]{3,2,1,0:T(4,128)S(1)}) conditional(s32[]{:T(128)} %convert_element_type.2, (f32[8,8,8,132]{3,2,1,0:T(8,128)S(1)}, f32[2,8,6,130]{3,2,1,0:T(8,128)S(1)}, f32[8,8,132]{2,1,0:T(8,128)S(1)}, f32[2,8,4,128]{3,2,1,0:T(4,128)S(1)}, f32[8]{0:T(128)S(1)}, /*index=5*/f32[8]{0:T(128)S(1)}) %tuple.115, ...), branch_computations={%region_7.9_spmd, %region_9.11_spmd} | conditional | flops 2347200 | bytes 5210008 | solution.py:266
  51.4 1.9 %collective-permute-start.7 = (f32[8,8,2,128]{3,2,1,0:T(2,128)S(1)}, f32[8,8,2,128]{3,2,1,0:T(2,128)S(1)}, u32[]{:S(2)}, u32[]{:S(2)}) collective-permute-start(f32[8,8,2,128]{3,2,1,0:T(2,128)S(1)} %get-tuple-element.201), channel_id=1, source_target_pairs={{0,16},{16,32},{32,48},{48,64},{64,80},{80,96},{96,112},{112,128},... | collective-permute-start | bytes 196616 | tf_op jit(solution)/shard_map/ppermute | solution.py:22
  53.3 3.9 %collective-permute-start.8 = (f32[8,8,2,128]{3,2,1,0:T(2,128)S(1)}, f32[8,8,2,128]{3,2,1,0:T(2,128)S(1)}, u32[]{:S(2)}, u32[]{:S(2)}) collective-permute-start(f32[8,8,2,128]{3,2,1,0:T(2,128)S(1)} %get-tuple-element.202), channel_id=1, source_target_pairs={{16,0},{32,16},{48,32},{64,48},{80,64},{96,80},{112,96},{128,112},... | collective-permute-start | bytes 196616 | tf_op jit(solution)/shard_map/ppermute | solution.py:24
  57.5 8.7 %collective-permute-done.8 = f32[8,8,2,128]{3,2,1,0:T(2,128)S(1)} collective-permute-done((f32[8,8,2,128]{3,2,1,0:T(2,128)S(1)}, f32[8,8,2,128]{3,2,1,0:T(2,128)S(1)}, u32[]{:S(2)}, u32[]{:S(2)}) %collective-permute-start.8) | collective-permute-done | bytes 65568 | tf_op jit(solution)/shard_map/ppermute | solution.py:24
  66.4 1.9 %collective-permute-start.9 = (f32[8,8,8,2]{3,2,1,0:T(8,128)S(1)}, f32[8,8,8,2]{3,2,1,0:T(8,128)S(1)}, u32[]{:S(2)}, u32[]{:S(2)}) collective-permute-start(f32[8,8,8,2]{3,2,1,0:T(8,128)S(1)} %get-tuple-element.193), channel_id=1, source_target_pairs={{0,1},{1,2},{2,3},{3,4},{4,5},{5,6},{6,7},{7,8},{8,9},{9,10},{10,1... | collective-permute-start | bytes 12296 | tf_op jit(solution)/shard_map/ppermute | solution.py:22
  68.4 3.9 %collective-permute-start.10 = (f32[8,8,8,2]{3,2,1,0:T(8,128)S(1)}, f32[8,8,8,2]{3,2,1,0:T(8,128)S(1)}, u32[]{:S(2)}, u32[]{:S(2)}) collective-permute-start(f32[8,8,8,2]{3,2,1,0:T(8,128)S(1)} %get-tuple-element.194), channel_id=1, source_target_pairs={{1,0},{2,1},{3,2},{4,3},{5,4},{6,5},{7,6},{8,7},{9,8},{10,9},{11,1... | collective-permute-start | bytes 12296 | tf_op jit(solution)/shard_map/ppermute | solution.py:24
  72.3 2.4 %collective-permute-done.9 = f32[8,8,8,2]{3,2,1,0:T(8,128)S(1)} collective-permute-done((f32[8,8,8,2]{3,2,1,0:T(8,128)S(1)}, f32[8,8,8,2]{3,2,1,0:T(8,128)S(1)}, u32[]{:S(2)}, u32[]{:S(2)}) %collective-permute-start.9) | collective-permute-done | bytes 4128 | tf_op jit(solution)/shard_map/ppermute | solution.py:22
  74.7 4.0 %collective-permute-done.10 = f32[8,8,8,2]{3,2,1,0:T(8,128)S(1)} collective-permute-done((f32[8,8,8,2]{3,2,1,0:T(8,128)S(1)}, f32[8,8,8,2]{3,2,1,0:T(8,128)S(1)}, u32[]{:S(2)}, u32[]{:S(2)}) %collective-permute-start.10) | collective-permute-done | bytes 4128 | tf_op jit(solution)/shard_map/ppermute | solution.py:24
  79.3 3.3 %conditional.11 = (f32[8,8,4,128]{3,2,1,0:T(4,128)S(1)}) conditional(s32[]{:T(128)} %convert_element_type.2, (f32[2,8,6,130]{3,2,1,0:T(8,128)S(1)}, f32[8,8,132]{2,1,0:T(8,128)S(1)}, f32[8,8,8,128]{3,2,1,0:T(8,128)S(1)}, f32[8,8,8,132]{3,2,1,0:T(8,128)S(1)}, f32[8,8,4,128]{3,2,1,0:T(4,128)S(1)}, /*index=5*/f32[2,8,4,128]{3,2,1,0:T(4,128)S(1)}, ...), branch_computations={%region_11.13_spmd, %region_13.15_spmd} | conditional | flops 2347200 | bytes 4046664 | solution.py:266
  82.7 2.5 %collective-permute-start.11 = (f32[8,8,2,128]{3,2,1,0:T(2,128)S(1)}, f32[8,8,2,128]{3,2,1,0:T(2,128)S(1)}, u32[]{:S(2)}, u32[]{:S(2)}) collective-permute-start(f32[8,8,2,128]{3,2,1,0:T(2,128)S(1)} %get-tuple-element.199), channel_id=1, source_target_pairs={{0,16},{16,32},{32,48},{48,64},{64,80},{80,96},{96,112},{112,128},... | collective-permute-start | bytes 196616 | tf_op jit(solution)/shard_map/ppermute | solution.py:22
  85.2 3.3 %collective-permute-start.12 = (f32[8,8,2,128]{3,2,1,0:T(2,128)S(1)}, f32[8,8,2,128]{3,2,1,0:T(2,128)S(1)}, u32[]{:S(2)}, u32[]{:S(2)}) collective-permute-start(f32[8,8,2,128]{3,2,1,0:T(2,128)S(1)} %get-tuple-element.200), channel_id=1, source_target_pairs={{16,0},{32,16},{48,32},{64,48},{80,64},{96,80},{112,96},{128,112},... | collective-permute-start | bytes 196616 | tf_op jit(solution)/shard_map/ppermute | solution.py:24
  88.8 10.0 %collective-permute-done.12 = f32[8,8,2,128]{3,2,1,0:T(2,128)S(1)} collective-permute-done((f32[8,8,2,128]{3,2,1,0:T(2,128)S(1)}, f32[8,8,2,128]{3,2,1,0:T(2,128)S(1)}, u32[]{:S(2)}, u32[]{:S(2)}) %collective-permute-start.12) | collective-permute-done | bytes 65568 | tf_op jit(solution)/shard_map/ppermute | solution.py:24
  99.0 1.9 %collective-permute-start.13 = (f32[8,8,8,2]{3,2,1,0:T(8,128)S(1)}, f32[8,8,8,2]{3,2,1,0:T(8,128)S(1)}, u32[]{:S(2)}, u32[]{:S(2)}) collective-permute-start(f32[8,8,8,2]{3,2,1,0:T(8,128)S(1)} %get-tuple-element.191), channel_id=1, source_target_pairs={{0,1},{1,2},{2,3},{3,4},{4,5},{5,6},{6,7},{7,8},{8,9},{9,10},{10,1... | collective-permute-start | bytes 12296 | tf_op jit(solution)/shard_map/ppermute | solution.py:22
  101.0 3.9 %collective-permute-start.14 = (f32[8,8,8,2]{3,2,1,0:T(8,128)S(1)}, f32[8,8,8,2]{3,2,1,0:T(8,128)S(1)}, u32[]{:S(2)}, u32[]{:S(2)}) collective-permute-start(f32[8,8,8,2]{3,2,1,0:T(8,128)S(1)} %get-tuple-element.192), channel_id=1, source_target_pairs={{1,0},{2,1},{3,2},{4,3},{5,4},{6,5},{7,6},{8,7},{9,8},{10,9},{11,1... | collective-permute-start | bytes 12296 | tf_op jit(solution)/shard_map/ppermute | solution.py:24
  104.9 2.4 %collective-permute-done.13 = f32[8,8,8,2]{3,2,1,0:T(8,128)S(1)} collective-permute-done((f32[8,8,8,2]{3,2,1,0:T(8,128)S(1)}, f32[8,8,8,2]{3,2,1,0:T(8,128)S(1)}, u32[]{:S(2)}, u32[]{:S(2)}) %collective-permute-start.13) | collective-permute-done | bytes 4128 | tf_op jit(solution)/shard_map/ppermute | solution.py:22
  107.3 4.0 %collective-permute-done.14 = f32[8,8,8,2]{3,2,1,0:T(8,128)S(1)} collective-permute-done((f32[8,8,8,2]{3,2,1,0:T(8,128)S(1)}, f32[8,8,8,2]{3,2,1,0:T(8,128)S(1)}, u32[]{:S(2)}, u32[]{:S(2)}) %collective-permute-start.14) | collective-permute-done | bytes 4128 | tf_op jit(solution)/shard_map/ppermute | solution.py:24
  111.9 3.6 %conditional.12 = (f32[8,8,4,128]{3,2,1,0:T(4,128)S(1)}) conditional(s32[]{:T(128)} %convert_element_type.2, f32[8,8,4,128]{3,2,1,0:T(4,128)S(1)} %get-tuple-element.216, (f32[8,8,8,132]{3,2,1,0:T(8,128)S(1)}, f32[8,8,132]{2,1,0:T(8,128)S(1)}, f32[8,4,128]{2,1,0:T(4,128)S(1)}, f32[8,8,4,128]{3,2,1,0:T(4,128)S(1)}) %tuple.58), branch_computations={%region_15.16_spmd, %region_16.18_spmd} | conditional | flops 1437632 | bytes 3770756 | solution.py:272
  115.5 1.9 %collective-permute-start.15 = (f32[8,8,2,128]{3,2,1,0:T(2,128)S(1)}, f32[8,8,2,128]{3,2,1,0:T(2,128)S(1)}, u32[]{:S(2)}, u32[]{:S(2)}) collective-permute-start(f32[8,8,2,128]{3,2,1,0:T(2,128)S(1)} %get-tuple-element.197), channel_id=1, source_target_pairs={{0,16},{16,32},{32,48},{48,64},{64,80},{80,96},{96,112},{112,128},... | collective-permute-start | bytes 196616 | tf_op jit(solution)/shard_map/ppermute | solution.py:22
  117.4 3.9 %collective-permute-start.16 = (f32[8,8,2,128]{3,2,1,0:T(2,128)S(1)}, f32[8,8,2,128]{3,2,1,0:T(2,128)S(1)}, u32[]{:S(2)}, u32[]{:S(2)}) collective-permute-start(f32[8,8,2,128]{3,2,1,0:T(2,128)S(1)} %get-tuple-element.198), channel_id=1, source_target_pairs={{16,0},{32,16},{48,32},{64,48},{80,64},{96,80},{112,96},{128,112},... | collective-permute-start | bytes 196616 | tf_op jit(solution)/shard_map/ppermute | solution.py:24
  121.7 7.9 %collective-permute-done.16 = f32[8,8,2,128]{3,2,1,0:T(2,128)S(1)} collective-permute-done((f32[8,8,2,128]{3,2,1,0:T(2,128)S(1)}, f32[8,8,2,128]{3,2,1,0:T(2,128)S(1)}, u32[]{:S(2)}, u32[]{:S(2)}) %collective-permute-start.16) | collective-permute-done | bytes 65568 | tf_op jit(solution)/shard_map/ppermute | solution.py:24
  129.8 3.6 %collective-permute-start.17 = (f32[8,8,8,2]{3,2,1,0:T(8,128)S(1)}, f32[8,8,8,2]{3,2,1,0:T(8,128)S(1)}, u32[]{:S(2)}, u32[]{:S(2)}) collective-permute-start(f32[8,8,8,2]{3,2,1,0:T(8,128)S(1)} %get-tuple-element.189), channel_id=1, source_target_pairs={{0,1},{1,2},{2,3},{3,4},{4,5},{5,6},{6,7},{7,8},{8,9},{9,10},{10,1... | collective-permute-start | bytes 12296 | tf_op jit(solution)/shard_map/ppermute | solution.py:22
  133.5 2.2 %collective-permute-start.18 = (f32[8,8,8,2]{3,2,1,0:T(8,128)S(1)}, f32[8,8,8,2]{3,2,1,0:T(8,128)S(1)}, u32[]{:S(2)}, u32[]{:S(2)}) collective-permute-start(f32[8,8,8,2]{3,2,1,0:T(8,128)S(1)} %get-tuple-element.190), channel_id=1, source_target_pairs={{1,0},{2,1},{3,2},{4,3},{5,4},{6,5},{7,6},{8,7},{9,8},{10,9},{11,1... | collective-permute-start | bytes 12296 | tf_op jit(solution)/shard_map/ppermute | solution.py:24
  135.7 2.4 %collective-permute-done.17 = f32[8,8,8,2]{3,2,1,0:T(8,128)S(1)} collective-permute-done((f32[8,8,8,2]{3,2,1,0:T(8,128)S(1)}, f32[8,8,8,2]{3,2,1,0:T(8,128)S(1)}, u32[]{:S(2)}, u32[]{:S(2)}) %collective-permute-start.17) | collective-permute-done | bytes 4128 | tf_op jit(solution)/shard_map/ppermute | solution.py:22
  138.1 5.7 %collective-permute-done.18 = f32[8,8,8,2]{3,2,1,0:T(8,128)S(1)} collective-permute-done((f32[8,8,8,2]{3,2,1,0:T(8,128)S(1)}, f32[8,8,8,2]{3,2,1,0:T(8,128)S(1)}, u32[]{:S(2)}, u32[]{:S(2)}) %collective-permute-start.18) | collective-permute-done | bytes 4128 | tf_op jit(solution)/shard_map/ppermute | solution.py:24
  144.4 3.4 %conditional.13 = (f32[1,8,8,4,128]{4,3,2,1,0:T(4,128)S(1)}) conditional(s32[]{:T(128)} %convert_element_type.2, f32[8,8,4,128]{3,2,1,0:T(4,128)S(1)} %get-tuple-element.217, (f32[8,8,8,132]{3,2,1,0:T(8,128)S(1)}, f32[8,8,132]{2,1,0:T(8,128)S(1)}, f32[8,4,128]{2,1,0:T(4,128)S(1)}, f32[8,8,4,128]{3,2,1,0:T(4,128)S(1)}) %tuple.101), branch_computations={%region_18.19_spmd, %region_19.21_spmd} | conditional | flops 1437632 | bytes 3770756 | solution.py:272
  (152 shorter events, 26.8 us)
Async XLA Ops:
  0.0 0.7 copy-start.14
  0.7 24.3 %copy-start.1 = (f32[1,8,8,4,128]{4,3,2,1,0:T(4,128)S(1)}, f32[1,8,8,4,128]{4,3,2,1,0:T(4,128)}, u32[]{:S(2)}) copy-start(f32[1,8,8,4,128]{4,3,2,1,0:T(4,128)} %param.19) | copy-start | bytes 393220
  1.9 12.1 %collective-permute-start = (f32[9,8,2,128]{3,2,1,0:T(2,128)S(1)}, f32[9,8,2,128]{3,2,1,0:T(2,128)S(1)}, u32[]{:S(2)}, u32[]{:S(2)}) collective-permute-start(f32[9,8,2,128]{3,2,1,0:T(2,128)S(1)} %get-tuple-element.195), channel_id=1, source_target_pairs={{0,16},{16,32},{32,48},{48,64},{64,80},{80,96},{96,112},{112,128},... | collective-permute-start | bytes 221192 | tf_op jit(solution)/shard_map/ppermute | solution.py:22
  12.0 13.1 %collective-permute-start.1 = (f32[9,8,2,128]{3,2,1,0:T(2,128)S(1)}, f32[9,8,2,128]{3,2,1,0:T(2,128)S(1)}, u32[]{:S(2)}, u32[]{:S(2)}) collective-permute-start(f32[9,8,2,128]{3,2,1,0:T(2,128)S(1)} %get-tuple-element.196), channel_id=1, source_target_pairs={{16,0},{32,16},{48,32},{64,48},{80,64},{96,80},{112,96},{128,112},... | collective-permute-start | bytes 221192 | tf_op jit(solution)/shard_map/ppermute | solution.py:24
  25.3 8.6 %collective-permute-start.2 = (f32[9,8,8,2]{3,2,1,0:T(8,128)S(1)}, f32[9,8,8,2]{3,2,1,0:T(8,128)S(1)}, u32[]{:S(2)}, u32[]{:S(2)}) collective-permute-start(f32[9,8,8,2]{3,2,1,0:T(8,128)S(1)} %get-tuple-element.187), channel_id=1, source_target_pairs={{0,1},{1,2},{2,3},{3,4},{4,5},{5,6},{6,7},{7,8},{8,9},{9,10},{10,1... | collective-permute-start | bytes 13832 | tf_op jit(solution)/shard_map/ppermute | solution.py:22
  29.6 10.7 %collective-permute-start.3 = (f32[9,8,8,2]{3,2,1,0:T(8,128)S(1)}, f32[9,8,8,2]{3,2,1,0:T(8,128)S(1)}, u32[]{:S(2)}, u32[]{:S(2)}) collective-permute-start(f32[9,8,8,2]{3,2,1,0:T(8,128)S(1)} %get-tuple-element.188), channel_id=1, source_target_pairs={{1,0},{2,1},{3,2},{4,3},{5,4},{6,5},{7,6},{8,7},{9,8},{10,9},{11,1... | collective-permute-start | bytes 13832 | tf_op jit(solution)/shard_map/ppermute | solution.py:24
  41.5 5.8 %collective-permute-start.4 = (f32[2,8,6,130]{3,2,1,0:T(8,128)S(1)}, f32[2,8,6,130]{3,2,1,0:T(8,128)S(1)}, u32[]{:S(2)}, u32[]{:S(2)}) collective-permute-start(f32[2,8,6,130]{3,2,1,0:T(8,128)S(1)} %get-tuple-element.130), channel_id=1, source_target_pairs={{0,384},{1,385},{2,386},{3,387},{4,388},{5,389},{6,390},{7,391},{8... | collective-permute-start | bytes 149768 | tf_op jit(solution)/shard_map/ppermute | solution.py:34
  42.8 4.5 %collective-permute-start.5 = (f32[2,8,4,128]{3,2,1,0:T(4,128)S(1)}, f32[2,8,4,128]{3,2,1,0:T(4,128)S(1)}, u32[]{:S(2)}, u32[]{:S(2)}) collective-permute-start(f32[2,8,4,128]{3,2,1,0:T(4,128)S(1)} %get-tuple-element.131), channel_id=1, source_target_pairs={{0,384},{1,385},{2,386},{3,387},{4,388},{5,389},{6,390},{7,391},{8... | collective-permute-start | bytes 98312 | tf_op jit(solution)/shard_map/ppermute | solution.py:34
  44.1 3.1 %collective-permute-start.6 = (f32[8,4,128]{2,1,0:T(4,128)S(1)}, f32[8,4,128]{2,1,0:T(4,128)S(1)}, u32[]{:S(2)}, u32[]{:S(2)}) collective-permute-start(f32[8,4,128]{2,1,0:T(4,128)S(1)} %get-tuple-element.213), channel_id=1, source_target_pairs={{384,0},{385,1},{386,2},{387,3},{388,4},{389,5},{390,6},{391,7},{3... | collective-permute-start | bytes 49160 | tf_op jit(solution)/shard_map/ppermute | solution.py:34
  47.2 0.7 copy-start.12
  47.2 0.7 copy-start.13
  50.2 0.8 copy-start.5
  50.2 0.9 slice-start.1
  51.4 6.2 %collective-permute-start.7 = (f32[8,8,2,128]{3,2,1,0:T(2,128)S(1)}, f32[8,8,2,128]{3,2,1,0:T(2,128)S(1)}, u32[]{:S(2)}, u32[]{:S(2)}) collective-permute-start(f32[8,8,2,128]{3,2,1,0:T(2,128)S(1)} %get-tuple-element.201), channel_id=1, source_target_pairs={{0,16},{16,32},{32,48},{48,64},{64,80},{80,96},{96,112},{112,128},... | collective-permute-start | bytes 196616 | tf_op jit(solution)/shard_map/ppermute | solution.py:22
  53.3 12.9 %collective-permute-start.8 = (f32[8,8,2,128]{3,2,1,0:T(2,128)S(1)}, f32[8,8,2,128]{3,2,1,0:T(2,128)S(1)}, u32[]{:S(2)}, u32[]{:S(2)}) collective-permute-start(f32[8,8,2,128]{3,2,1,0:T(2,128)S(1)} %get-tuple-element.202), channel_id=1, source_target_pairs={{16,0},{32,16},{48,32},{64,48},{80,64},{96,80},{112,96},{128,112},... | collective-permute-start | bytes 196616 | tf_op jit(solution)/shard_map/ppermute | solution.py:24
  66.4 8.3 %collective-permute-start.9 = (f32[8,8,8,2]{3,2,1,0:T(8,128)S(1)}, f32[8,8,8,2]{3,2,1,0:T(8,128)S(1)}, u32[]{:S(2)}, u32[]{:S(2)}) collective-permute-start(f32[8,8,8,2]{3,2,1,0:T(8,128)S(1)} %get-tuple-element.193), channel_id=1, source_target_pairs={{0,1},{1,2},{2,3},{3,4},{4,5},{5,6},{6,7},{7,8},{8,9},{9,10},{10,1... | collective-permute-start | bytes 12296 | tf_op jit(solution)/shard_map/ppermute | solution.py:22
  68.4 10.4 %collective-permute-start.10 = (f32[8,8,8,2]{3,2,1,0:T(8,128)S(1)}, f32[8,8,8,2]{3,2,1,0:T(8,128)S(1)}, u32[]{:S(2)}, u32[]{:S(2)}) collective-permute-start(f32[8,8,8,2]{3,2,1,0:T(8,128)S(1)} %get-tuple-element.194), channel_id=1, source_target_pairs={{1,0},{2,1},{3,2},{4,3},{5,4},{6,5},{7,6},{8,7},{9,8},{10,9},{11,1... | collective-permute-start | bytes 12296 | tf_op jit(solution)/shard_map/ppermute | solution.py:24
  81.5 0.8 copy-start.7
  81.5 0.9 slice-start.2
  82.7 6.2 %collective-permute-start.11 = (f32[8,8,2,128]{3,2,1,0:T(2,128)S(1)}, f32[8,8,2,128]{3,2,1,0:T(2,128)S(1)}, u32[]{:S(2)}, u32[]{:S(2)}) collective-permute-start(f32[8,8,2,128]{3,2,1,0:T(2,128)S(1)} %get-tuple-element.199), channel_id=1, source_target_pairs={{0,16},{16,32},{32,48},{48,64},{64,80},{80,96},{96,112},{112,128},... | collective-permute-start | bytes 196616 | tf_op jit(solution)/shard_map/ppermute | solution.py:22
  85.2 13.6 %collective-permute-start.12 = (f32[8,8,2,128]{3,2,1,0:T(2,128)S(1)}, f32[8,8,2,128]{3,2,1,0:T(2,128)S(1)}, u32[]{:S(2)}, u32[]{:S(2)}) collective-permute-start(f32[8,8,2,128]{3,2,1,0:T(2,128)S(1)} %get-tuple-element.200), channel_id=1, source_target_pairs={{16,0},{32,16},{48,32},{64,48},{80,64},{96,80},{112,96},{128,112},... | collective-permute-start | bytes 196616 | tf_op jit(solution)/shard_map/ppermute | solution.py:24
  99.0 8.3 %collective-permute-start.13 = (f32[8,8,8,2]{3,2,1,0:T(8,128)S(1)}, f32[8,8,8,2]{3,2,1,0:T(8,128)S(1)}, u32[]{:S(2)}, u32[]{:S(2)}) collective-permute-start(f32[8,8,8,2]{3,2,1,0:T(8,128)S(1)} %get-tuple-element.191), channel_id=1, source_target_pairs={{0,1},{1,2},{2,3},{3,4},{4,5},{5,6},{6,7},{7,8},{8,9},{9,10},{10,1... | collective-permute-start | bytes 12296 | tf_op jit(solution)/shard_map/ppermute | solution.py:22
  101.0 10.4 %collective-permute-start.14 = (f32[8,8,8,2]{3,2,1,0:T(8,128)S(1)}, f32[8,8,8,2]{3,2,1,0:T(8,128)S(1)}, u32[]{:S(2)}, u32[]{:S(2)}) collective-permute-start(f32[8,8,8,2]{3,2,1,0:T(8,128)S(1)} %get-tuple-element.192), channel_id=1, source_target_pairs={{1,0},{2,1},{3,2},{4,3},{5,4},{6,5},{7,6},{8,7},{9,8},{10,9},{11,1... | collective-permute-start | bytes 12296 | tf_op jit(solution)/shard_map/ppermute | solution.py:24
  114.4 0.8 copy-start.9
  114.4 0.9 slice-start.3
  115.5 6.2 %collective-permute-start.15 = (f32[8,8,2,128]{3,2,1,0:T(2,128)S(1)}, f32[8,8,2,128]{3,2,1,0:T(2,128)S(1)}, u32[]{:S(2)}, u32[]{:S(2)}) collective-permute-start(f32[8,8,2,128]{3,2,1,0:T(2,128)S(1)} %get-tuple-element.197), channel_id=1, source_target_pairs={{0,16},{16,32},{32,48},{48,64},{64,80},{80,96},{96,112},{112,128},... | collective-permute-start | bytes 196616 | tf_op jit(solution)/shard_map/ppermute | solution.py:22
  117.4 12.2 %collective-permute-start.16 = (f32[8,8,2,128]{3,2,1,0:T(2,128)S(1)}, f32[8,8,2,128]{3,2,1,0:T(2,128)S(1)}, u32[]{:S(2)}, u32[]{:S(2)}) collective-permute-start(f32[8,8,2,128]{3,2,1,0:T(2,128)S(1)} %get-tuple-element.198), channel_id=1, source_target_pairs={{16,0},{32,16},{48,32},{64,48},{80,64},{96,80},{112,96},{128,112},... | collective-permute-start | bytes 196616 | tf_op jit(solution)/shard_map/ppermute | solution.py:24
  129.8 8.3 %collective-permute-start.17 = (f32[8,8,8,2]{3,2,1,0:T(8,128)S(1)}, f32[8,8,8,2]{3,2,1,0:T(8,128)S(1)}, u32[]{:S(2)}, u32[]{:S(2)}) collective-permute-start(f32[8,8,8,2]{3,2,1,0:T(8,128)S(1)} %get-tuple-element.189), channel_id=1, source_target_pairs={{0,1},{1,2},{2,3},{3,4},{4,5},{5,6},{6,7},{7,8},{8,9},{9,10},{10,1... | collective-permute-start | bytes 12296 | tf_op jit(solution)/shard_map/ppermute | solution.py:22
  133.5 10.4 %collective-permute-start.18 = (f32[8,8,8,2]{3,2,1,0:T(8,128)S(1)}, f32[8,8,8,2]{3,2,1,0:T(8,128)S(1)}, u32[]{:S(2)}, u32[]{:S(2)}) collective-permute-start(f32[8,8,8,2]{3,2,1,0:T(8,128)S(1)} %get-tuple-element.190), channel_id=1, source_target_pairs={{1,0},{2,1},{3,2},{4,3},{5,4},{6,5},{7,6},{8,7},{9,8},{10,9},{11,1... | collective-permute-start | bytes 12296 | tf_op jit(solution)/shard_map/ppermute | solution.py:24
  146.7 0.8 copy-start.11
  146.7 0.9 slice-start.4
  147.8 0.7 copy-start
  (4 other events, 2.5 us)
where the time goes:
time: 149 us; the launch traced here: 148 us
  waiting for transfers between devices  70.2 us (47%)
  starting transfers between devices  57.2 us (38%)
  other arithmetic  11.1 us (7%)
  local copies, waits for them, and re-layouts  8.71 us (6%)
    ppermute x8, waiting for transfers between devices, with_halo(): lax.ppermute(head, axis, [((i + 1) % count, i) for i in range(ends)])  57.9 us
    ppermute x8, starting transfers between devices, with_halo(): lax.ppermute(tail, axis, [(i, (i + 1) % count) for i in range(ends)])  28.3 us
    ppermute x8, starting transfers between devices, with_halo(): lax.ppermute(head, axis, [((i + 1) % count, i) for i in range(ends)])  25 us
    ppermute x8, waiting for transfers between devices, with_halo(): lax.ppermute(tail, axis, [(i, (i + 1) % count) for i in range(ends)])  10.5 us
    cond x16, local copies, waits for them, and re-layouts  4.66 us
    ppermute x3, starting transfers between devices, shifted(): return lax.ppermute(shard, axis, pairs)  3.88 us
  transfers between devices with their start and end apart: 19, of which 16 were waited for; matrix products, arithmetic and copies ran while one was open for 0% of the time, Pallas kernels for 0%

commit v1 on v0

v1 whole, which is shorter than its diff:
```python
import functools

import jax
import jax.numpy as jnp
from jax import lax
from jax.experimental import pallas as pl
from jax.experimental.pallas import tpu as pltpu
from jax.sharding import PartitionSpec as P

DYN_STEPS = 4
TRACER_STEPS = 2
CORIOLIS = 0.2
PRESSURE = 0.01

LEVELS = 8
LANES = 128
FIELDS = 8
PROG = 4
ROWS = 4
HALO = 8
MAIN = 2 * FIELDS * ROWS
EDGE = 2 * ROWS
NEAR = MAIN + EDGE + 1
FAR_G = PROG * ROWS
FAR_CHL = FAR_G + PROG * 2
FAR_EDGE = FAR_CHL + 2
FAR = FAR_EDGE + EDGE + 1
DYN_ROWS = 5 * ROWS
TRC_ROWS = 3 * ROWS
TILE = (LEVELS, LANES)


def lanes():
    return lax.broadcasted_iota(jnp.int32, TILE, 1)


def level_index():
    return lax.broadcasted_iota(jnp.int32, TILE, 0)


def edge_source(comp):
    first = jnp.where(comp == 0, LANES - HALO, 0)
    lane = lanes()
    return (lane >= first) & (lane < first + HALO)


def wet_count(land_ref, depth_ref):
    return jnp.where(land_ref[...] == 1, depth_ref[...], 0).astype(jnp.float32)


def row_of(own_ref, comp, field, row):
    return own_ref[comp, field, pl.ds(row, LEVELS, stride=ROWS), :]


def pack_columns(comp_ref, own_ref, land_ref, depth_ref, out_ref):
    source = edge_source(comp_ref[0])
    for c in range(2):
        for r in range(ROWS):
            total = None
            for f in range(FIELDS):
                part = jnp.where(source, row_of(own_ref, c, f, r), 0.0)
                part = pltpu.roll(part, (16 * f + HALO) % LANES, 1)
                total = part if total is None else total + part
            out_ref[c * ROWS + r] = total
    count = wet_count(land_ref, depth_ref)
    out_ref[EDGE] = jnp.zeros(TILE, jnp.float32)
    out_ref[EDGE, 0:ROWS, :] = jnp.where(source[0:ROWS], count, 0.0)


def pack_rows(comp_ref, own_ref, land_ref, depth_ref, side_ref, near_ref, far_ref):
    first = jnp.where(comp_ref[0] == 0, 2, 0)
    for c in range(2):
        for f in range(FIELDS):
            for r in range(ROWS):
                tile = row_of(own_ref, c, f, r)
                near_ref[(c * FIELDS + f) * ROWS + r] = tile
                if c == 0 and f < PROG:
                    far_ref[f * ROWS + r] = tile
    for k in range(2):
        for f in range(PROG):
            far_ref[FAR_G + f * 2 + k] = row_of(own_ref, 0, PROG + f, first + k)
        far_ref[FAR_CHL + k] = row_of(own_ref, 1, 0, first + k)
    for t in range(EDGE):
        both = side_ref[0, t] + side_ref[1, t]
        near_ref[MAIN + t] = both
        far_ref[FAR_EDGE + t] = both
    count = wet_count(land_ref, depth_ref)
    outer = side_ref[0, EDGE, 0:ROWS, :] + side_ref[1, EDGE, 0:ROWS, :]
    near_ref[MAIN + EDGE, 0:ROWS, :] = count
    near_ref[MAIN + EDGE, ROWS : 2 * ROWS, :] = outer
    far_ref[FAR_EDGE + EDGE, 0:ROWS, :] = count
    far_ref[FAR_EDGE + EDGE, ROWS : 2 * ROWS, :] = outer


def next_column(pair):
    here, beyond = pair
    last = lanes() == LANES - 1
    a, b = pltpu.roll(here, LANES - 1, 1), pltpu.roll(beyond, LANES - 1, 1)
    return jnp.where(last, b, a), jnp.where(last, a, b)


def previous_column(pair):
    here, beyond = pair
    start = lanes() == 0
    a, b = pltpu.roll(here, 1, 1), pltpu.roll(beyond, 1, 1)
    return jnp.where(start, b, a), jnp.where(start, a, b)


def both(function, *pairs):
    return tuple(function(*values) for values in zip(*pairs))


def half_minmod(a, b):
    return 0.5 * (jnp.maximum(jnp.minimum(a, b), 0.0) + jnp.minimum(jnp.maximum(a, b), 0.0))


def level_sum(values):
    level = level_index()
    for by in (1, 2, 4):
        values = values + jnp.where(level >= by, pltpu.roll(values, by, 0), 0.0)
    return values


def below(values):
    return pltpu.roll(values, LEVELS - 1, 0)


def above(values):
    return pltpu.roll(values, 1, 0)


def density(temperature, salinity):
    return 0.8 * salinity - 0.2 * temperature


def stirring(rho, column_wet):
    jump = below(rho) - rho
    return (0.02 + 0.1 / (1.0 + 4.0 * jump * jump)) * column_wet


def column_mix(quantity, mixing):
    flux = mixing * (below(quantity) - quantity)
    return flux - above(flux)


def across(quantity, shifted, plus, minus):
    jump = both(lambda n, q: n - q, shifted, quantity)
    slope = both(half_minmod, jump, previous_column(jump))
    low = both(lambda q, s: q + s, quantity, slope)
    high = next_column(both(lambda q, s: q - s, quantity, slope))
    flux = both(lambda p, lo, m, hi: p * lo + m * hi, plus, low, minus, high)
    return both(lambda before, after: before - after, previous_column(flux), flux)


def split(speed):
    return jnp.maximum(speed, 0.0), jnp.minimum(speed, 0.0)


def face_start(ref, fields, row):
    out = []
    for f in fields:
        here = [ref[f, row, t] for t in range(2)]
        jump = [ref[f, row + 1, t] - here[t] for t in range(2)]
        left = [here[t] + half_minmod(jump[t], here[t] - ref[f, row - 1, t]) for t in range(2)]
        out.append((tuple(jump), tuple(left)))
    return out


def face_step(ref, field, row, jump, left, plus, minus):
    jumps, lefts, fluxes = [], [], []
    for t in range(2):
        near = ref[field, row + 1, t]
        ahead = ref[field, row + 2, t] - near
        slope = half_minmod(ahead, jump[t])
        fluxes.append(plus[t] * left[t] + minus[t] * (near - slope))
        jumps.append(ahead)
        lefts.append(near + slope)
    return tuple(jumps), tuple(lefts), tuple(fluxes)


def load_wet(count_ref, index, row, wet_ref, at):
    level = level_index().astype(jnp.float32)
    for t in range(2):
        count = count_ref[index + (slice(t * ROWS + row, t * ROWS + row + 1), slice(None))]
        wet_ref[at, t] = jnp.where(level < count, 1.0, 0.0)


def unpack_edge(edge, field):
    return pltpu.roll(edge, (2 * LANES - HALO - 16 * field) % LANES, 1)


def masks(wet_ref, facex_ref, facey_ref, facez_ref, rows):
    not_last = level_index() < LEVELS - 1

    def body(i, carry):
        here = (wet_ref[i, 0], wet_ref[i, 1])
        beside = next_column(here)
        for t in range(2):
            facey_ref[i, t] = 0.5 * here[t] * beside[t]
            facez_ref[i, t] = jnp.where(not_last, here[t] * below(here[t]), 0.0)
        return carry

    lax.fori_loop(0, rows, body, 0)

    def body_x(i, carry):
        for t in range(2):
            facex_ref[i, t] = 0.5 * wet_ref[i, t] * wet_ref[i + 1, t]
        return carry

    lax.fori_loop(0, rows - 1, body_x, 0)


def dynamics(own_ref, near_ref, far_ref, out_ref, q_ref, g_ref, heat_ref, wet_ref, facex_ref, facey_ref, facez_ref):
    blocks = ((far_ref, (0,)), (near_ref, (0,)), (own_ref, ()), (near_ref, (1,)), (far_ref, (1,)))
    for b, (ref, lead) in enumerate(blocks):
        far = b in (0, 4)
        edge_at = FAR_EDGE if far else MAIN
        for r in range(ROWS):
            row = b * ROWS + r
            load_wet(ref, lead + (edge_at + EDGE,), r, wet_ref, row)
            edge = ref[lead + (edge_at + r,)]
            for f in range(PROG):
                q_ref[0, f, row, 0] = ref[lead + (f * ROWS + r,)]
                q_ref[0, f, row, 1] = unpack_edge(edge, f)
            k = r - 2 if b == 0 else r
            if not 2 <= row < DYN_ROWS - 2:
                continue
            for f in range(PROG):
                at = FAR_G + f * 2 + k if far else (PROG + f) * ROWS + r
                g_ref[f, row, 0] = ref[lead + (at,)]
                g_ref[f, row, 1] = unpack_edge(edge, PROG + f)
            chl_at = FAR_CHL + k if far else FIELDS * ROWS + r
            chl_edge = ref[lead + (edge_at + ROWS + r,)]
            chl = (ref[lead + (chl_at,)], unpack_edge(chl_edge, 0))
            for t in range(2):
                absorb = (0.04 + 0.05 * chl[t] * chl[t]) * wet_ref[row, t]
                lower = jnp.exp(-level_sum(absorb))
                upper = jnp.where(level_index() == 0, 1.0, above(lower))
                heat_ref[row, t] = 0.5 * (upper - lower)
    masks(wet_ref, facex_ref, facey_ref, facez_ref, DYN_ROWS)

    def column(src, row):
        rho = [density(src[2, row, t], src[3, row, t]) for t in range(2)]
        pressure = [level_sum(rho[t] * wet_ref[row, t]) for t in range(2)]
        return tuple(rho), tuple(pressure)

    for step in range(DYN_STEPS):
        src, dst = q_ref.at[step % 2], q_ref.at[(step + 1) % 2]
        first, end = 2 * (step + 1), DYN_ROWS - 2 * (step + 1)
        last_step = step == DYN_STEPS - 1

        def speed_x(row):
            return [split(facex_ref[row, t] * (src[0, row, t] + src[0, row + 1, t])) for t in range(2)]

        started = face_start(src, range(PROG), first - 1)
        speeds = speed_x(first - 1)
        streams = tuple(
            face_step(src, f, first - 1, *started[f], [s[0] for s in speeds], [s[1] for s in speeds])
            for f in range(PROG)
        )
        _, before = column(src, first - 1)
        rho, pressure = column(src, first)

        def body(i, carry, src=src, dst=dst, speed_x=speed_x, last_step=last_step):
            streams, before, rho, pressure = carry
            rho_after, after = column(src, i + 1)
            wet = [wet_ref[i, t] for t in range(2)]
            here = [(src[f, i, 0], src[f, i, 1]) for f in range(PROG)]
            shifted = [next_column(h) for h in here]
            speeds = speed_x(i)
            plus_x, minus_x = [s[0] for s in speeds], [s[1] for s in speeds]
            speeds = [split(facey_ref[i, t] * (here[1][t] + shifted[1][t])) for t in range(2)]
            plus_y, minus_y = [s[0] for s in speeds], [s[1] for s in speeds]
            mixing = [stirring(rho[t], facez_ref[i, t]) for t in range(2)]
            east, west = next_column(pressure), previous_column(pressure)
            new = []
            for f in range(PROG):
                jump, left, entering = streams[f]
                jump, left, leaving = face_step(src, f, i, jump, left, plus_x, minus_x)
                new.append((jump, left, leaving))
                sideways = across(here[f], shifted[f], plus_y, minus_y)
                for t in range(1 if last_step else 2):
                    tendency = entering[t] - leaving[t] + sideways[t] + column_mix(here[f][t], mixing[t])
                    if f == 0:
                        tendency += CORIOLIS * here[1][t] - (0.5 * PRESSURE) * (after[t] - before[t])
                    elif f == 1:
                        tendency += -CORIOLIS * here[0][t] - (0.5 * PRESSURE) * (east[t] - west[t])
                    elif f == 2:
                        tendency += heat_ref[i, t]
                    tendency = tendency * wet[t]
                    updated = (here[f][t] + 1.5 * tendency - 0.5 * g_ref[f, i, t]) * wet[t]
                    if last_step:
                        rows = pl.ds(i - 2 * ROWS, LEVELS, stride=ROWS)
                        out_ref[f, rows, :] = updated
                        out_ref[PROG + f, rows, :] = tendency
                    else:
                        dst[f, i, t] = updated
                        g_ref[f, i, t] = tendency
            return tuple(new), pressure, rho_after, after

        lax.fori_loop(first, end, body, (streams, before, rho, pressure))


def tracers(
    growth_ref, decay_ref, own_ref, near_ref, out_ref,
    c_ref, flow_ref, speed_ref, mix_ref, warm_ref, light_ref, wet_ref, facex_ref, facey_ref, facez_ref,
):
    blocks = ((near_ref, (0,)), (own_ref, ()), (near_ref, (1,)))
    for b, (ref, lead) in enumerate(blocks):
        for r in range(ROWS):
            row = b * ROWS + r
            load_wet(ref, lead + (MAIN + EDGE,), r, wet_ref, row)
            edge = ref[lead + (MAIN + ROWS + r,)]
            for f in range(FIELDS):
                c_ref[0, f, row, 0] = ref[lead + ((FIELDS + f) * ROWS + r,)]
                c_ref[0, f, row, 1] = unpack_edge(edge, f)
            edge = ref[lead + (MAIN + r,)]
            for f in range(PROG):
                flow_ref[f, row, 0] = ref[lead + (f * ROWS + r,)]
                flow_ref[f, row, 1] = unpack_edge(edge, f)
    masks(wet_ref, facex_ref, facey_ref, facez_ref, TRC_ROWS)

    def prepare(i, carry):
        beside = next_column((flow_ref[1, i, 0], flow_ref[1, i, 1]))
        for t in range(2):
            plus, minus = split(facex_ref[i, t] * (flow_ref[0, i, t] + flow_ref[0, i + 1, t]))
            speed_ref[0, i, t] = plus
            speed_ref[1, i, t] = minus
            plus, minus = split(facey_ref[i, t] * (flow_ref[1, i, t] + beside[t]))
            speed_ref[2, i, t] = plus
            speed_ref[3, i, t] = minus
            mix_ref[i, t] = stirring(density(flow_ref[2, i, t], flow_ref[3, i, t]), facez_ref[i, t])
            warm_ref[i, t] = jnp.exp(0.1 * flow_ref[2, i, t])
        return carry

    lax.fori_loop(1, TRC_ROWS - 2, prepare, 0)

    group = 4
    for step in range(TRACER_STEPS):
        src, dst = c_ref.at[step % 2], c_ref.at[(step + 1) % 2]
        first, end = 2 * (step + 1), TRC_ROWS - 2 * (step + 1)
        last_step = step == TRACER_STEPS - 1

        def shade(i, carry, src=src):
            for t in range(2):
                chl = src[0, i, t]
                absorb = (0.04 + 0.05 * chl * chl) * wet_ref[i, t]
                light_ref[i, t] = jnp.exp(-level_sum(absorb)) * warm_ref[i, t]
            return carry

        lax.fori_loop(first, end, shade, 0)

        def some(n, carry, src=src, dst=dst, first=first, end=end, last_step=last_step):
            fields = [n * group + k for k in range(group)]

            def pair(ref, *index):
                return (ref[index + (0,)], ref[index + (1,)])

            started = face_start(src, fields, first - 1)
            plus, minus = pair(speed_ref, 0, first - 1), pair(speed_ref, 1, first - 1)
            streams = tuple(
                face_step(src, f, first - 1, *started[k], plus, minus) for k, f in enumerate(fields)
            )

            def body(i, streams):
                plus_x, minus_x = pair(speed_ref, 0, i), pair(speed_ref, 1, i)
                plus_y, minus_y = pair(speed_ref, 2, i), pair(speed_ref, 3, i)
                new = []
                for k, f in enumerate(fields):
                    jump, left, entering = streams[k]
                    jump, left, leaving = face_step(src, f, i, jump, left, plus_x, minus_x)
                    new.append((jump, left, leaving))
                    here = pair(src, f, i)
                    sideways = across(here, next_column(here), plus_y, minus_y)
                    for t in range(1 if last_step else 2):
                        net = growth_ref[f] * light_ref[i, t] - decay_ref[f]
                        change = entering[t] - leaving[t] + sideways[t] + column_mix(here[t], mix_ref[i, t])
                        updated = (here[t] + change + net * here[t]) * wet_ref[i, t]
                        if last_step:
                            out_ref[f, pl.ds(i - ROWS, LEVELS, stride=ROWS), :] = updated
                        else:
                            dst[f, i, t] = updated
                return tuple(new)

            lax.fori_loop(first, end, body, streams)
            return carry

        lax.fori_loop(0, FIELDS // group, some, 0)


def advance(
    comp_ref, growth_ref, decay_ref, own_ref, near_ref, far_ref, out_ref,
    q_ref, g_ref, heat_ref, c_ref, flow_ref, speed_ref, mix_ref, warm_ref, light_ref,
    wet_ref, facex_ref, facey_ref, facez_ref,
):
    @pl.when(comp_ref[0] == 0)
    def _():
        dynamics(own_ref, near_ref, far_ref, out_ref, q_ref, g_ref, heat_ref, wet_ref, facex_ref, facey_ref, facez_ref)

    @pl.when(comp_ref[0] == 1)
    def _():
        tracers(
            growth_ref, decay_ref, own_ref, near_ref, out_ref,
            c_ref, flow_ref, speed_ref, mix_ref, warm_ref, light_ref, wet_ref, facex_ref, facey_ref, facez_ref,
        )


def call(kernel, smem, vmem, outs, scratch=(), flops=0):
    out_shape = tuple(jax.ShapeDtypeStruct(s, jnp.float32) for s in outs)
    size = 4 * sum(a.size for a in vmem) + 4 * sum(s.size for s in out_shape)
    result = pl.pallas_call(
        kernel,
        out_shape=out_shape,
        in_specs=[pl.BlockSpec(memory_space=pltpu.SMEM)] * len(smem)
        + [pl.BlockSpec(memory_space=pltpu.VMEM)] * len(vmem),
        out_specs=tuple(pl.BlockSpec(memory_space=pltpu.VMEM) for _ in outs),
        scratch_shapes=[pltpu.VMEM(s + TILE, jnp.float32) for s in scratch],
        compiler_params=pltpu.CompilerParams(vmem_limit_bytes=24 * 1024 * 1024),
        cost_estimate=pl.CostEstimate(flops=flops, bytes_accessed=size, transcendentals=0),
    )(*smem, *vmem)
    return result


def neighbours(gx, gy, by_x, by_y):
    pairs = []
    for c, way in ((0, 1), (1, -1)):
        for i in range(gx):
            for j in range(gy):
                a, b = i + way * by_x, j + way * by_y
                if 0 <= a < gx and 0 <= b < gy:
                    pairs.append(((c * gx + i) * gy + j, (c * gx + a) * gy + b))
    return pairs


def local(ocean_state, land_sea, depth_levels, growth, decay):
    axes = ("comp", "gx", "gy")
    gx, gy = lax.axis_size("gx"), lax.axis_size("gy")
    comp = lax.axis_index("comp").astype(jnp.int32).reshape(1)
    fields = ocean_state.reshape(FIELDS, LEVELS * ROWS, LANES)
    own = lax.all_gather(fields, "comp")
    (columns,) = call(pack_columns, [comp], [own, land_sea, depth_levels], [(EDGE + 1,) + TILE])
    columns = lax.ppermute(columns, axes, neighbours(gx, gy, 0, 1))
    sides = lax.all_gather(columns, "comp")
    near, far = call(
        pack_rows, [comp], [own, land_sea, depth_levels, sides], [(NEAR,) + TILE, (FAR,) + TILE]
    )
    near_in = lax.ppermute(near, axes, neighbours(gx, gy, 1, 0))
    far_in = lax.ppermute(far, axes, neighbours(gx, gy, 2, 0))
    near_in, far_in = lax.all_gather((near_in, far_in), "comp")
    scratch = [
        (2, PROG, DYN_ROWS, 2),
        (PROG, DYN_ROWS, 2),
        (DYN_ROWS, 2),
        (2, FIELDS, TRC_ROWS, 2),
        (PROG, TRC_ROWS, 2),
        (4, TRC_ROWS, 2),
        (TRC_ROWS, 2),
        (TRC_ROWS, 2),
        (TRC_ROWS, 2),
        (DYN_ROWS, 2),
        (DYN_ROWS, 2),
        (DYN_ROWS, 2),
        (DYN_ROWS, 2),
    ]
    (out,) = call(
        advance, [comp, growth, decay], [near, near_in, far_in],
        [(FIELDS, LEVELS * ROWS, LANES)], scratch, flops=20_000_000,
    )
    return out.reshape(ocean_state.shape)


def solution(mesh):
    placed = (P("comp", None, None, "gx", "gy"), P("gx", "gy"), P("gx", "gy"), P(), P())
    return jax.shard_map(
        local,
        mesh=mesh,
        in_specs=placed,
        out_specs=P("comp", None, None, "gx", "gy"),
        check_vma=False,
    )
```

time: 149 us -> 61.9 us (0.42)
  the two profiles are of different devices: /device:TPU:62 before, /device:TPU:112 now
where the time goes in v1:
time: 61.9 us; the launch traced here: 61.7 us
  blocking collectives  21.3 us (34%)
  starting transfers between devices  17.1 us (28%)
  Pallas kernels  15.4 us (25%)
  waiting for transfers between devices  7.17 us (12%)
  local copies, waits for them, and re-layouts  0.68 us (1%)
    all_gather x2, blocking collectives, local(): near_in, far_in = lax.all_gather((near_in, far_in), 'comp')  17.1 us
    pallas_call x3, Pallas kernels, call(): pl.pallas_call(kernel, out_shape=out_shape, in_specs=[pl.BlockSpec(memory...  15.4 us
    ppermute x1, starting transfers between devices, local(): far_in = lax.ppermute(far, axes, neighbours(gx, gy, 2, 0))  11.1 us
    ppermute x1, waiting for transfers between devices, local(): columns = lax.ppermute(columns, axes, neighbours(gx, gy, 0, 1))  4.55 us
    ppermute x1, starting transfers between devices, local(): columns = lax.ppermute(columns, axes, neighbours(gx, gy, 0, 1))  3.4 us
    ppermute x1, waiting for transfers between devices, local(): far_in = lax.ppermute(far, axes, neighbours(gx, gy, 2, 0))  2.62 us
    ppermute x1, starting transfers between devices, local(): near_in = lax.ppermute(near, axes, neighbours(gx, gy, 1, 0))  2.59 us
    all_gather x1, blocking collectives, local(): own = lax.all_gather(fields, 'comp')  2.32 us
  transfers between devices with their start and end apart: 3, of which 2 were waited for; matrix products, arithmetic and copies ran while one was open for 0% of the time, Pallas kernels for 0%

profile of v1, /device:TPU:112, one launch (start us, length us, event | category | flops | bytes accessed | tf_op | source)
XLA Modules:
  0.0 61.7 jit_solution(16835811869247586697)
XLA Ops:
  0.0 0.0 copy-start
  0.0 0.0 copy-start.1
  0.0 2.3 %all_gather.21.own_ref = f32[2,8,32,128]{3,2,1,0:T(8,128)S(1)} all-gather(f32[1,8,32,128]{3,2,1,0:T(8,128)} %bitcast.9), channel_id=1, replica_groups=mesh['comp'=2,'gx'=24,'gy'=16] {'comp'}, dimensions={0}, use_global_device_ids=true | all-gather | bytes 393216 | tf_op jit(solution)/shard_map/all_gather | solution.py:440
  2.3 0.0 copy-done
  2.3 0.0 copy-done.1
  2.3 0.1 shard_map.55
  2.5 3.4 %collective-permute-start = (f32[9,8,128]{2,1,0:T(8,128)S(1)}, f32[9,8,128]{2,1,0:T(8,128)S(1)}, u32[]{:S(2)}, u32[]{:S(2)}) collective-permute-start(f32[9,8,128]{2,1,0:T(8,128)S(1)} %shard_map.55), channel_id=1, source_target_pairs={{0,1},{1,2},{2,3},{3,4},{4,5},{5,6},{6,7},{7,8},{8,9},{9,10},{10,1... | collective-permute-start | bytes 110600 | tf_op jit(solution)/shard_map/ppermute | solution.py:442
  5.9 4.6 %collective-permute-done = f32[9,8,128]{2,1,0:T(8,128)S(1)} collective-permute-done((f32[9,8,128]{2,1,0:T(8,128)S(1)}, f32[9,8,128]{2,1,0:T(8,128)S(1)}, u32[]{:S(2)}, u32[]{:S(2)}) %collective-permute-start) | collective-permute-done | bytes 36896 | tf_op jit(solution)/shard_map/ppermute | solution.py:442
  10.4 1.8 %all-gather = f32[18,8,128]{2,1,0:T(8,128)S(1)} all-gather(f32[9,8,128]{2,1,0:T(8,128)S(1)} %collective-permute-done), channel_id=2, replica_groups=mesh['comp'=2,'gx'=24,'gy'=16] {'comp'}, dimensions={0}, use_global_device_ids=true | all-gather | bytes 110592 | tf_op jit(solution)/shard_map/all_gather | solution.py:443
  12.3 2.6 %collective-permute-start.1 = (f32[73,8,128]{2,1,0:T(8,128)S(1)}, f32[73,8,128]{2,1,0:T(8,128)S(1)}, u32[]{:S(2)}, u32[]{:S(2)}) collective-permute-start(f32[73,8,128]{2,1,0:T(8,128)S(1)} %get-tuple-element.7.own_ref), channel_id=1, source_target_pairs={{0,16},{1,17},{2,18},{3,19},{4,20},{5,21},{6,22},{7,23},{8,24},{9,... | collective-permute-start | bytes 897032 | tf_op jit(solution)/shard_map/ppermute | solution.py:447
  14.9 11.1 %collective-permute-start.2 = (f32[35,8,128]{2,1,0:T(8,128)S(1)}, f32[35,8,128]{2,1,0:T(8,128)S(1)}, u32[]{:S(2)}, u32[]{:S(2)}) collective-permute-start(f32[35,8,128]{2,1,0:T(8,128)S(1)} %get-tuple-element.8), channel_id=1, source_target_pairs={{0,32},{1,33},{2,34},{3,35},{4,36},{5,37},{6,38},{7,39},{8,40},{9,... | collective-permute-start | bytes 430088 | tf_op jit(solution)/shard_map/ppermute | solution.py:448
  26.1 2.6 %collective-permute-done.2 = f32[35,8,128]{2,1,0:T(8,128)S(1)} collective-permute-done((f32[35,8,128]{2,1,0:T(8,128)S(1)}, f32[35,8,128]{2,1,0:T(8,128)S(1)}, u32[]{:S(2)}, u32[]{:S(2)}) %collective-permute-start.2) | collective-permute-done | bytes 143392 | tf_op jit(solution)/shard_map/ppermute | solution.py:448
  28.7 14.9 %all-gather.2 = f32[70,8,128]{2,1,0:T(8,128)S(1)} all-gather(f32[35,8,128]{2,1,0:T(8,128)S(1)} %collective-permute-done.2), channel_id=4, replica_groups=mesh['comp'=2,'gx'=24,'gy'=16] {'comp'}, dimensions={0}, use_global_device_ids=true | all-gather | bytes 430080 | tf_op jit(solution)/shard_map/all_gather | solution.py:449
  43.6 0.0 collective-permute-done.1
  43.6 2.2 %all-gather.1 = f32[146,8,128]{2,1,0:T(8,128)S(1)} all-gather(f32[73,8,128]{2,1,0:T(8,128)S(1)} %collective-permute-done.1), channel_id=3, replica_groups=mesh['comp'=2,'gx'=24,'gy'=16] {'comp'}, dimensions={0}, use_global_device_ids=true | all-gather | bytes 897024 | tf_op jit(solution)/shard_map/all_gather | solution.py:449
  45.8 0.0 copy-start.2
  45.8 0.0 copy-start.3
  45.8 0.7 %copy-done.2 = f32[8]{0:T(128)S(1)} copy-done((f32[8]{0:T(128)S(1)}, f32[8]{0:T(128)}, u32[]{:S(2)}) %copy-start.2) | copy-done | bytes 56
  46.4 0.0 copy-done.3
  46.5 15.2 %shard_map.57 = f32[8,32,128]{2,1,0:T(8,128)} custom-call(s32[1]{0:T(128)} %bitcast.comp_ref, f32[8]{0:T(128)S(1)} %copy-done.2, f32[8]{0:T(128)S(1)} %copy-done.3, f32[73,8,128]{2,1,0:T(8,128)S(1)} %get-tuple-element.7.own_ref, f32[2,73,8,128]{3,2,1,0:T(8,128)S(1)} %bitcast.6, f32[2,35,8,128]{3,2,1,0:T(8,128)S(1)} %bitcast.7), custom_call_target="tpu_custom_call" | custom-call | flops 20000000 | bytes 1314816 | tf_op jit(solution)/shard_map/pallas_call | solution.py:411
  (1 shorter events, 0.0 us)
Async XLA Ops:
  0.0 2.3 %copy-start = (s32[4,128]{1,0:T(4,128)S(1)}, s32[4,128]{1,0:T(4,128)}, u32[]{:S(2)}) copy-start(s32[4,128]{1,0:T(4,128)} %land_ref.3) | copy-start | bytes 6148
  0.0 2.3 %copy-start.1 = (s32[4,128]{1,0:T(4,128)S(1)}, s32[4,128]{1,0:T(4,128)}, u32[]{:S(2)}) copy-start(s32[4,128]{1,0:T(4,128)} %depth_ref.3) | copy-start | bytes 6148
  2.5 8.0 %collective-permute-start = (f32[9,8,128]{2,1,0:T(8,128)S(1)}, f32[9,8,128]{2,1,0:T(8,128)S(1)}, u32[]{:S(2)}, u32[]{:S(2)}) collective-permute-start(f32[9,8,128]{2,1,0:T(8,128)S(1)} %shard_map.55), channel_id=1, source_target_pairs={{0,1},{1,2},{2,3},{3,4},{4,5},{5,6},{6,7},{7,8},{8,9},{9,10},{10,1... | collective-permute-start | bytes 110600 | tf_op jit(solution)/shard_map/ppermute | solution.py:442
  12.3 31.2 %collective-permute-start.1 = (f32[73,8,128]{2,1,0:T(8,128)S(1)}, f32[73,8,128]{2,1,0:T(8,128)S(1)}, u32[]{:S(2)}, u32[]{:S(2)}) collective-permute-start(f32[73,8,128]{2,1,0:T(8,128)S(1)} %get-tuple-element.7.own_ref), channel_id=1, source_target_pairs={{0,16},{1,17},{2,18},{3,19},{4,20},{5,21},{6,22},{7,23},{8,24},{9,... | collective-permute-start | bytes 897032 | tf_op jit(solution)/shard_map/ppermute | solution.py:447
  14.9 13.8 %collective-permute-start.2 = (f32[35,8,128]{2,1,0:T(8,128)S(1)}, f32[35,8,128]{2,1,0:T(8,128)S(1)}, u32[]{:S(2)}, u32[]{:S(2)}) collective-permute-start(f32[35,8,128]{2,1,0:T(8,128)S(1)} %get-tuple-element.8), channel_id=1, source_target_pairs={{0,32},{1,33},{2,34},{3,35},{4,36},{5,37},{6,38},{7,39},{8,40},{9,... | collective-permute-start | bytes 430088 | tf_op jit(solution)/shard_map/ppermute | solution.py:448
  45.8 0.7 %copy-start.2 = (f32[8]{0:T(128)S(1)}, f32[8]{0:T(128)}, u32[]{:S(2)}) copy-start(f32[8]{0:T(128)} %growth_ref.1) | copy-start | bytes 100
  45.8 0.7 %copy-start.3 = (f32[8]{0:T(128)S(1)}, f32[8]{0:T(128)}, u32[]{:S(2)}) copy-start(f32[8]{0:T(128)} %decay_ref.1) | copy-start | bytes 100

commit v2 on v1

--- a/solution.py
+++ b/solution.py
@@ -20,14 +20,21 @@
 HALO = 8
 MAIN = 2 * FIELDS * ROWS
 EDGE = 2 * ROWS
-NEAR = MAIN + EDGE + 1
+SIDE = EDGE + 1
 FAR_G = PROG * ROWS
 FAR_CHL = FAR_G + PROG * 2
 FAR_EDGE = FAR_CHL + 2
-FAR = FAR_EDGE + EDGE + 1
+FAR_CHL_EDGE = FAR_EDGE + ROWS
+FAR_WET = FAR_CHL_EDGE + 2
+FAR = FAR_WET + 1
+IN_SIDE = MAIN
+IN_FAR = MAIN + SIDE
+IN = IN_FAR + FAR
 DYN_ROWS = 5 * ROWS
 TRC_ROWS = 3 * ROWS
 TILE = (LEVELS, LANES)
+DYN_UNROLL = 4
+TRC_UNROLL = 4
 
 
 def lanes():
@@ -52,7 +59,7 @@
     return own_ref[comp, field, pl.ds(row, LEVELS, stride=ROWS), :]
 
 
-def pack_columns(comp_ref, own_ref, land_ref, depth_ref, out_ref):
+def pack_columns(comp_ref, growth_ref, decay_ref, own_ref, land_ref, depth_ref, out_ref, rates_ref):
     source = edge_source(comp_ref[0])
     for c in range(2):
         for r in range(ROWS):
@@ -65,31 +72,85 @@
     count = wet_count(land_ref, depth_ref)
     out_ref[EDGE] = jnp.zeros(TILE, jnp.float32)
     out_ref[EDGE, 0:ROWS, :] = jnp.where(source[0:ROWS], count, 0.0)
-
-
-def pack_rows(comp_ref, own_ref, land_ref, depth_ref, side_ref, near_ref, far_ref):
+    for f in range(FIELDS):
+        rates_ref[0, f : f + 1, :] = jnp.full((1, LANES), growth_ref[f])
+        rates_ref[1, f : f + 1, :] = jnp.full((1, LANES), decay_ref[f])
+
+
+def pack_rows(comp_ref, own_ref, land_ref, depth_ref, columns_ref, side_ref, far_ref):
     first = jnp.where(comp_ref[0] == 0, 2, 0)
-    for c in range(2):
-        for f in range(FIELDS):
-            for r in range(ROWS):
-                tile = row_of(own_ref, c, f, r)
-                near_ref[(c * FIELDS + f) * ROWS + r] = tile
-                if c == 0 and f < PROG:
-                    far_ref[f * ROWS + r] = tile
+    for f in range(PROG):
+        for r in range(ROWS):
+            far_ref[f * ROWS + r] = row_of(own_ref, 0, f, r)
     for k in range(2):
         for f in range(PROG):
             far_ref[FAR_G + f * 2 + k] = row_of(own_ref, 0, PROG + f, first + k)
         far_ref[FAR_CHL + k] = row_of(own_ref, 1, 0, first + k)
+        at = ROWS + first + k
+        far_ref[FAR_CHL_EDGE + k] = columns_ref[0, at] + columns_ref[1, at]
     for t in range(EDGE):
-        both = side_ref[0, t] + side_ref[1, t]
-        near_ref[MAIN + t] = both
-        far_ref[FAR_EDGE + t] = both
+        joined = columns_ref[0, t] + columns_ref[1, t]
+        side_ref[t] = joined
+        if t < ROWS:
+            far_ref[FAR_EDGE + t] = joined
     count = wet_count(land_ref, depth_ref)
-    outer = side_ref[0, EDGE, 0:ROWS, :] + side_ref[1, EDGE, 0:ROWS, :]
-    near_ref[MAIN + EDGE, 0:ROWS, :] = count
-    near_ref[MAIN + EDGE, ROWS : 2 * ROWS, :] = outer
-    far_ref[FAR_EDGE + EDGE, 0:ROWS, :] = count
-    far_ref[FAR_EDGE + EDGE, ROWS : 2 * ROWS, :] = outer
+    outer = columns_ref[0, EDGE, 0:ROWS, :] + columns_ref[1, EDGE, 0:ROWS, :]
+    for ref, at in ((side_ref, EDGE), (far_ref, FAR_WET)):
+        ref[at, 0:ROWS, :] = count
+        ref[at, ROWS : 2 * ROWS, :] = outer
+
+
+def join(main_ref, side_ref, far_ref, out_ref):
+    at = 0
+    for ref in (main_ref, side_ref, far_ref):
+        size = ref.shape[0]
+        out_ref[at : at + size, :] = ref[...]
+        at += size
+
+
+class Block:
+    def __init__(self, main, edge, wet, g_rows=range(ROWS)):
+        self.main, self.edge, self.wet, self.g_rows = main, edge, wet, g_rows
+
+
+def own_block(own_ref, side_ref):
+    return Block(
+        lambda c, f, r: row_of(own_ref, c, f, r),
+        lambda c, r: side_ref[c * ROWS + r],
+        lambda row: side_ref[EDGE, row : row + 1, :],
+    )
+
+
+def near_block(in_ref, way):
+    def tile(index):
+        return in_ref[way, (IN_SIDE + index) * LEVELS : (IN_SIDE + index + 1) * LEVELS, :]
+
+    at = (IN_SIDE + EDGE) * LEVELS
+    return Block(
+        lambda c, f, r: in_ref[way, pl.ds((c * FIELDS + f) * LEVELS * ROWS + r, LEVELS, stride=ROWS), :],
+        lambda c, r: tile(c * ROWS + r),
+        lambda row: in_ref[way, at + row : at + row + 1, :],
+    )
+
+
+def far_block(in_ref, way):
+    first = 2 if way == 0 else 0
+
+    def tile(index):
+        return in_ref[way, (IN_FAR + index) * LEVELS : (IN_FAR + index + 1) * LEVELS, :]
+
+    def main(c, f, r):
+        if c == 1:
+            return tile(FAR_CHL + r - first)
+        return tile(f * ROWS + r if f < PROG else FAR_G + (f - PROG) * 2 + r - first)
+
+    at = (IN_FAR + FAR_WET) * LEVELS
+    return Block(
+        main,
+        lambda c, r: tile(FAR_EDGE + r if c == 0 else FAR_CHL_EDGE + r - first),
+        lambda row: in_ref[way, at + row : at + row + 1, :],
+        range(first, first + 2),
+    )
 
 
 def next_column(pair):
@@ -143,13 +204,13 @@
     return flux - above(flux)
 
 
-def across(quantity, shifted, plus, minus):
-    jump = both(lambda n, q: n - q, shifted, quantity)
-    slope = both(half_minmod, jump, previous_column(jump))
+def across(quantity, shifted, out_speed, in_speed):
+    slope = both(lambda n, q, p: half_minmod(n - q, q - p), shifted, quantity, previous_column(quantity))
     low = both(lambda q, s: q + s, quantity, slope)
-    high = next_column(both(lambda q, s: q - s, quantity, slope))
-    flux = both(lambda p, lo, m, hi: p * lo + m * hi, plus, low, minus, high)
-    return both(lambda before, after: before - after, previous_column(flux), flux)
+    high = both(lambda q, s: q - s, quantity, slope)
+    leaving = both(lambda s, lo, hi: s[0] * lo + s[1] * hi, out_speed, low, next_column(high))
+    entering = both(lambda s, lo, hi: s[0] * lo + s[1] * hi, in_speed, previous_column(low), high)
+    return both(lambda before, after: before - after, entering, leaving)
 
 
 def split(speed):
@@ -178,11 +239,10 @@
     return tuple(jumps), tuple(lefts), tuple(fluxes)
 
 
-def load_wet(count_ref, index, row, wet_ref, at):
+def load_wet(block, r, wet_ref, row):
     level = level_index().astype(jnp.float32)
     for t in range(2):
-        count = count_ref[index + (slice(t * ROWS + row, t * ROWS + row + 1), slice(None))]
-        wet_ref[at, t] = jnp.where(level < count, 1.0, 0.0)
+        wet_ref[row, t] = jnp.where(level < block.wet(t * ROWS + r), 1.0, 0.0)
 
 
 def unpack_edge(edge, field):
@@ -200,7 +260,7 @@
             facez_ref[i, t] = jnp.where(not_last, here[t] * below(here[t]), 0.0)
         return carry
 
-    lax.fori_loop(0, rows, body, 0)
+    lax.fori_loop(0, rows, body, 0, unroll=4)
 
     def body_x(i, carry):
         for t in range(2):
@@ -210,28 +270,28 @@
     lax.fori_loop(0, rows - 1, body_x, 0)
 
 
-def dynamics(own_ref, near_ref, far_ref, out_ref, q_ref, g_ref, heat_ref, wet_ref, facex_ref, facey_ref, facez_ref):
-    blocks = ((far_ref, (0,)), (near_ref, (0,)), (own_ref, ()), (near_ref, (1,)), (far_ref, (1,)))
-    for b, (ref, lead) in enumerate(blocks):
-        far = b in (0, 4)
-        edge_at = FAR_EDGE if far else MAIN
+def dynamics(own_ref, side_ref, in_ref, out_ref, q_ref, g_ref, heat_ref, wet_ref, facex_ref, facey_ref, facez_ref):
+    blocks = (
+        far_block(in_ref, 0),
+        near_block(in_ref, 0),
+        own_block(own_ref, side_ref),
+        near_block(in_ref, 1),
+        far_block(in_ref, 1),
+    )
+    for b, block in enumerate(blocks):
         for r in range(ROWS):
             row = b * ROWS + r
-            load_wet(ref, lead + (edge_at + EDGE,), r, wet_ref, row)
-            edge = ref[lead + (edge_at + r,)]
+            load_wet(block, r, wet_ref, row)
+            edge = block.edge(0, r)
             for f in range(PROG):
-                q_ref[0, f, row, 0] = ref[lead + (f * ROWS + r,)]
+                q_ref[0, f, row, 0] = block.main(0, f, r)
                 q_ref[0, f, row, 1] = unpack_edge(edge, f)
-            k = r - 2 if b == 0 else r
-            if not 2 <= row < DYN_ROWS - 2:
+            if r not in block.g_rows:
                 continue
             for f in range(PROG):
-                at = FAR_G + f * 2 + k if far else (PROG + f) * ROWS + r
-                g_ref[f, row, 0] = ref[lead + (at,)]
+                g_ref[f, row, 0] = block.main(0, PROG + f, r)
                 g_ref[f, row, 1] = unpack_edge(edge, PROG + f)
-            chl_at = FAR_CHL + k if far else FIELDS * ROWS + r
-            chl_edge = ref[lead + (edge_at + ROWS + r,)]
-            chl = (ref[lead + (chl_at,)], unpack_edge(chl_edge, 0))
+            chl = (block.main(1, 0, r), unpack_edge(block.edge(1, r), 0))
             for t in range(2):
                 absorb = (0.04 + 0.05 * chl[t] * chl[t]) * wet_ref[row, t]
                 lower = jnp.exp(-level_sum(absorb))
@@ -269,8 +329,9 @@
             shifted = [next_column(h) for h in here]
             speeds = speed_x(i)
             plus_x, minus_x = [s[0] for s in speeds], [s[1] for s in speeds]
-            speeds = [split(facey_ref[i, t] * (here[1][t] + shifted[1][t])) for t in range(2)]
-            plus_y, minus_y = [s[0] for s in speeds], [s[1] for s in speeds]
+            speed = tuple(facey_ref[i, t] * (here[1][t] + shifted[1][t]) for t in range(2))
+            out_y = both(split, speed)
+            in_y = both(split, previous_column(speed))
             mixing = [stirring(rho[t], facez_ref[i, t]) for t in range(2)]
             east, west = next_column(pressure), previous_column(pressure)
             new = []
@@ -278,7 +339,7 @@
                 jump, left, entering = streams[f]
                 jump, left, leaving = face_step(src, f, i, jump, left, plus_x, minus_x)
                 new.append((jump, left, leaving))
-                sideways = across(here[f], shifted[f], plus_y, minus_y)
+                sideways = across(here[f], shifted[f], out_y, in_y)
                 for t in range(1 if last_step else 2):
                     tendency = entering[t] - leaving[t] + sideways[t] + column_mix(here[f][t], mixing[t])
                     if f == 0:
@@ -298,37 +359,38 @@
                         g_ref[f, i, t] = tendency
             return tuple(new), pressure, rho_after, after
 
-        lax.fori_loop(first, end, body, (streams, before, rho, pressure))
+        lax.fori_loop(first, end, body, (streams, before, rho, pressure), unroll=DYN_UNROLL)
 
 
 def tracers(
-    growth_ref, decay_ref, own_ref, near_ref, out_ref,
+    rates_ref, own_ref, side_ref, in_ref, out_ref,
     c_ref, flow_ref, speed_ref, mix_ref, warm_ref, light_ref, wet_ref, facex_ref, facey_ref, facez_ref,
 ):
-    blocks = ((near_ref, (0,)), (own_ref, ()), (near_ref, (1,)))
-    for b, (ref, lead) in enumerate(blocks):
+    blocks = (near_block(in_ref, 0), own_block(own_ref, side_ref), near_block(in_ref, 1))
+    for b, block in enumerate(blocks):
         for r in range(ROWS):
             row = b * ROWS + r
-            load_wet(ref, lead + (MAIN + EDGE,), r, wet_ref, row)
-            edge = ref[lead + (MAIN + ROWS + r,)]
+            load_wet(block, r, wet_ref, row)
+            edge = block.edge(1, r)
             for f in range(FIELDS):
-                c_ref[0, f, row, 0] = ref[lead + ((FIELDS + f) * ROWS + r,)]
+                c_ref[0, f, row, 0] = block.main(1, f, r)
                 c_ref[0, f, row, 1] = unpack_edge(edge, f)
-            edge = ref[lead + (MAIN + r,)]
+            edge = block.edge(0, r)
             for f in range(PROG):
-                flow_ref[f, row, 0] = ref[lead + (f * ROWS + r,)]
+                flow_ref[f, row, 0] = block.main(0, f, r)
                 flow_ref[f, row, 1] = unpack_edge(edge, f)
     masks(wet_ref, facex_ref, facey_ref, facez_ref, TRC_ROWS)
 
     def prepare(i, carry):
-        beside = next_column((flow_ref[1, i, 0], flow_ref[1, i, 1]))
+        north = (flow_ref[1, i, 0], flow_ref[1, i, 1])
+        speed = tuple(facey_ref[i, t] * (north[t] + n) for t, n in enumerate(next_column(north)))
+        before = previous_column(speed)
         for t in range(2):
             plus, minus = split(facex_ref[i, t] * (flow_ref[0, i, t] + flow_ref[0, i + 1, t]))
             speed_ref[0, i, t] = plus
             speed_ref[1, i, t] = minus
-            plus, minus = split(facey_ref[i, t] * (flow_ref[1, i, t] + beside[t]))
-            speed_ref[2, i, t] = plus
-            speed_ref[3, i, t] = minus
+            speed_ref[2, i, t] = speed[t]
+            speed_ref[3, i, t] = before[t]
             mix_ref[i, t] = stirring(density(flow_ref[2, i, t], flow_ref[3, i, t]), facez_ref[i, t])
             warm_ref[i, t] = jnp.exp(0.1 * flow_ref[2, i, t])
         return carry
@@ -348,7 +410,7 @@
                 light_ref[i, t] = jnp.exp(-level_sum(absorb)) * warm_ref[i, t]
             return carry
 
-        lax.fori_loop(first, end, shade, 0)
+        lax.fori_loop(first, end, shade, 0, unroll=4)
 
         def some(n, carry, src=src, dst=dst, first=first, end=end, last_step=last_step):
             fields = [n * group + k for k in range(group)]
@@ -362,18 +424,20 @@
                 face_step(src, f, first - 1, *started[k], plus, minus) for k, f in enumerate(fields)
             )
 
+            rates = [(rates_ref[0, pl.ds(f, 1), :], rates_ref[1, pl.ds(f, 1), :]) for f in fields]
+
             def body(i, streams):
                 plus_x, minus_x = pair(speed_ref, 0, i), pair(speed_ref, 1, i)
-                plus_y, minus_y = pair(speed_ref, 2, i), pair(speed_ref, 3, i)
+                out_y, in_y = both(split, pair(speed_ref, 2, i)), both(split, pair(speed_ref, 3, i))
                 new = []
                 for k, f in enumerate(fields):
                     jump, left, entering = streams[k]
                     jump, left, leaving = face_step(src, f, i, jump, left, plus_x, minus_x)
                     new.append((jump, left, leaving))
                     here = pair(src, f, i)
-                    sideways = across(here, next_column(here), plus_y, minus_y)
+                    sideways = across(here, next_column(here), out_y, in_y)
                     for t in range(1 if last_step else 2):
-                        net = growth_ref[f] * light_ref[i, t] - decay_ref[f]
+                        net = rates[k][0] * light_ref[i, t] - rates[k][1]
                         change = entering[t] - leaving[t] + sideways[t] + column_mix(here[t], mix_ref[i, t])
                         updated = (here[t] + change + net * here[t]) * wet_ref[i, t]
                         if last_step:
@@ -382,25 +446,25 @@
                             dst[f, i, t] = updated
                 return tuple(new)
 
-            lax.fori_loop(first, end, body, streams)
+            lax.fori_loop(first, end, body, streams, unroll=TRC_UNROLL)
             return carry
 
         lax.fori_loop(0, FIELDS // group, some, 0)
 
 
 def advance(
-    comp_ref, growth_ref, decay_ref, own_ref, near_ref, far_ref, out_ref,
+    comp_ref, rates_ref, own_ref, side_ref, in_ref, out_ref,
     q_ref, g_ref, heat_ref, c_ref, flow_ref, speed_ref, mix_ref, warm_ref, light_ref,
     wet_ref, facex_ref, facey_ref, facez_ref,
 ):
     @pl.when(comp_ref[0] == 0)
     def _():
-        dynamics(own_ref, near_ref, far_ref, out_ref, q_ref, g_ref, heat_ref, wet_ref, facex_ref, facey_ref, facez_ref)
+        dynamics(own_ref, side_ref, in_ref, out_ref, q_ref, g_ref, heat_ref, wet_ref, facex_ref, facey_ref, facez_ref)
 
     @pl.when(comp_ref[0] == 1)
     def _():
         tracers(
-            growth_ref, decay_ref, own_ref, near_ref, out_ref,
+            rates_ref, own_ref, side_ref, in_ref, out_ref,
             c_ref, flow_ref, speed_ref, mix_ref, warm_ref, light_ref, wet_ref, facex_ref, facey_ref, facez_ref,
         )
 
@@ -421,32 +485,7 @@
     return result
 
 
-def neighbours(gx, gy, by_x, by_y):
-    pairs = []
-    for c, way in ((0, 1), (1, -1)):
-        for i in range(gx):
-            for j in range(gy):
-                a, b = i + way * by_x, j + way * by_y
-                if 0 <= a < gx and 0 <= b < gy:
-                    pairs.append(((c * gx + i) * gy + j, (c * gx + a) * gy + b))
-    return pairs
-
-
-def local(ocean_state, land_sea, depth_levels, growth, decay):
-    axes = ("comp", "gx", "gy")
-    gx, gy = lax.axis_size("gx"), lax.axis_size("gy")
-    comp = lax.axis_index("comp").astype(jnp.int32).reshape(1)
-    fields = ocean_state.reshape(FIELDS, LEVELS * ROWS, LANES)
-    own = lax.all_gather(fields, "comp")
-    (columns,) = call(pack_columns, [comp], [own, land_sea, depth_levels], [(EDGE + 1,) + TILE])
-    columns = lax.ppermute(columns, axes, neighbours(gx, gy, 0, 1))
-    sides = lax.all_gather(columns, "comp")
-    near, far = call(
-        pack_rows, [comp], [own, land_sea, depth_levels, sides], [(NEAR,) + TILE, (FAR,) + TILE]
-    )
-    near_in = lax.ppermute(near, axes, neighbours(gx, gy, 1, 0))
-    far_in = lax.ppermute(far, axes, neighbours(gx, gy, 2, 0))
-    near_in, far_in = lax.all_gather((near_in, far_in), "comp")
+def all_steps(comp, rates, own, side, received):
     scratch = [
         (2, PROG, DYN_ROWS, 2),
         (PROG, DYN_ROWS, 2),
@@ -463,9 +502,46 @@
         (DYN_ROWS, 2),
     ]
     (out,) = call(
-        advance, [comp, growth, decay], [near, near_in, far_in],
+        advance, [comp], [rates, own, side, received],
         [(FIELDS, LEVELS * ROWS, LANES)], scratch, flops=20_000_000,
     )
+    return out
+
+
+def neighbours(gx, gy, by_x, by_y):
+    pairs = []
+    for c, way in ((0, 1), (1, -1)):
+        for i in range(gx):
+            for j in range(gy):
+                a, b = i + way * by_x, j + way * by_y
+                if 0 <= a < gx and 0 <= b < gy:
+                    pairs.append(((c * gx + i) * gy + j, (c * gx + a) * gy + b))
+    return pairs
+
+
+def local(ocean_state, land_sea, depth_levels, growth, decay):
+    axes = ("comp", "gx", "gy")
+    gx, gy = lax.axis_size("gx"), lax.axis_size("gy")
+    comp = lax.axis_index("comp").astype(jnp.int32).reshape(1)
+    fields = ocean_state.reshape(FIELDS, LEVELS * ROWS, LANES)
+    own = lax.all_gather(fields, "comp")
+    tall = (MAIN * LEVELS, LANES)
+    near_in = lax.ppermute(own.reshape(tall), axes, neighbours(gx, gy, 1, 0))
+    columns, rates = call(
+        pack_columns, [comp, growth, decay], [own, land_sea, depth_levels], [(SIDE,) + TILE, (2,) + TILE]
+    )
+    columns = lax.ppermute(columns, axes, neighbours(gx, gy, 0, 1))
+    columns = lax.all_gather(columns, "comp")
+    side, far = call(
+        pack_rows, [comp], [own, land_sea, depth_levels, columns], [(SIDE,) + TILE, (FAR,) + TILE]
+    )
+    side_in = lax.ppermute(side, axes, neighbours(gx, gy, 1, 0))
+    far_in = lax.ppermute(far, axes, neighbours(gx, gy, 2, 0))
+    (received,) = call(
+        join, [], [near_in, side_in.reshape(-1, LANES), far_in.reshape(-1, LANES)], [(IN * LEVELS, LANES)]
+    )
+    received = lax.all_gather(received, "comp")
+    out = all_steps(comp, rates, own, side, received)
     return out.reshape(ocean_state.shape)
 
 

time: 61.9 us -> 50 us (0.81)
  the two profiles are of different devices: /device:TPU:112 before, /device:TPU:376 now
where the time goes in v2:
time: 50 us; the launch traced here: 49.7 us
  waiting for transfers between devices  15.5 us (31%)
  starting transfers between devices  14 us (28%)
  blocking collectives  13.6 us (27%)
  Pallas kernels  5.8 us (12%)
  local copies, waits for them, and re-layouts  0.67 us (1%)
    ppermute x1, waiting for transfers between devices, local(): columns = lax.ppermute(columns, axes, neighbours(gx, gy, 0, 1))  11.2 us
    all_gather x1, blocking collectives, local(): received = lax.all_gather(received, 'comp')  9.58 us
    ppermute x1, starting transfers between devices, local(): near_in = lax.ppermute(own.reshape(tall), axes, neighbours(gx, gy, 1, 0))  6.81 us
    pallas_call x4, Pallas kernels, call(): pl.pallas_call(kernel, out_shape=out_shape, in_specs=[pl.BlockSpec(memory...  5.8 us
    ppermute x1, waiting for transfers between devices, local(): side_in = lax.ppermute(side, axes, neighbours(gx, gy, 1, 0))  4.34 us
    ppermute x1, starting transfers between devices, local(): columns = lax.ppermute(columns, axes, neighbours(gx, gy, 0, 1))  3.4 us
    all_gather x1, blocking collectives, local(): own = lax.all_gather(fields, 'comp')  2.19 us
    ppermute x1, starting transfers between devices, local(): far_in = lax.ppermute(far, axes, neighbours(gx, gy, 2, 0))  1.92 us
  transfers between devices with their start and end apart: 4, of which 2 were waited for; matrix products, arithmetic and copies ran while one was open for 0% of the time, Pallas kernels for 1%

profile of v2, /device:TPU:376, one launch (start us, length us, event | category | flops | bytes accessed | tf_op | source)
XLA Modules:
  0.0 49.7 jit_solution(1668485121396828534)
XLA Ops:
  0.0 2.2 %all_gather.15.own_ref = f32[2,8,32,128]{3,2,1,0:T(8,128)S(1)} all-gather(f32[1,8,32,128]{3,2,1,0:T(8,128)} %bitcast.13), channel_id=1, replica_groups=mesh['comp'=2,'gx'=24,'gy'=16] {'comp'}, dimensions={0}, use_global_device_ids=true | all-gather | bytes 393216 | tf_op jit(solution)/shard_map/all_gather | solution.py:527
  2.2 6.8 %collective-permute-start.1 = (f32[512,128]{1,0:T(8,128)S(1)}, f32[512,128]{1,0:T(8,128)S(1)}, u32[]{:S(2)}, u32[]{:S(2)}) collective-permute-start(f32[512,128]{1,0:T(8,128)S(1)} %bitcast.8), channel_id=1, source_target_pairs={{0,16},{1,17},{2,18},{3,19},{4,20},{5,21},{6,22},{7,23},{8,24},{9,... | collective-permute-start | bytes 786440 | tf_op jit(solution)/shard_map/ppermute | solution.py:529
  9.0 0.0 copy-start.1
  9.0 0.0 copy-start
  9.0 0.0 copy-start.2
  9.1 0.0 copy-start.3
  9.1 0.6 %copy-done.1 = s32[4,128]{1,0:T(4,128)S(1)} copy-done((s32[4,128]{1,0:T(4,128)S(1)}, s32[4,128]{1,0:T(4,128)}, u32[]{:S(2)}) %copy-start.1) | copy-done | bytes 2072
  9.7 0.0 copy-done
  9.7 0.0 copy-done.2
  9.7 0.0 copy-done.3
  9.7 0.7 %shard_map.55 = (f32[9,8,128]{2,1,0:T(8,128)S(1)}, f32[2,8,128]{2,1,0:T(8,128)S(1)}) custom-call(s32[1]{0:T(128)} %bitcast.comp_ref, f32[8]{0:T(128)S(1)} %copy-done.2, f32[8]{0:T(128)S(1)} %copy-done.3, f32[2,8,32,128]{3,2,1,0:T(8,128)S(1)} %all_gather.15.own_ref, s32[4,128]{1,0:T(4,128)S(1)} %copy-done, s32[4,128]{1,0:T(4,128)S(1)} %copy-done.1), custom_call_target="tpu_custom_call" | custom-call | bytes 311296 | tf_op jit(solution)/shard_map/pallas_call | solution.py:475
  10.4 3.4 %collective-permute-start = (f32[9,8,128]{2,1,0:T(8,128)S(1)}, f32[9,8,128]{2,1,0:T(8,128)S(1)}, u32[]{:S(2)}, u32[]{:S(2)}) collective-permute-start(f32[9,8,128]{2,1,0:T(8,128)S(1)} %get-tuple-element.10), channel_id=1, source_target_pairs={{0,1},{1,2},{2,3},{3,4},{4,5},{5,6},{6,7},{7,8},{8,9},{9,10},{10,1... | collective-permute-start | bytes 110600 | tf_op jit(solution)/shard_map/ppermute | solution.py:533
  13.8 11.2 %collective-permute-done = f32[9,8,128]{2,1,0:T(8,128)S(1)} collective-permute-done((f32[9,8,128]{2,1,0:T(8,128)S(1)}, f32[9,8,128]{2,1,0:T(8,128)S(1)}, u32[]{:S(2)}, u32[]{:S(2)}) %collective-permute-start) | collective-permute-done | bytes 36896 | tf_op jit(solution)/shard_map/ppermute | solution.py:533
  25.0 1.8 %all-gather = f32[18,8,128]{2,1,0:T(8,128)S(1)} all-gather(f32[9,8,128]{2,1,0:T(8,128)S(1)} %collective-permute-done), channel_id=2, replica_groups=mesh['comp'=2,'gx'=24,'gy'=16] {'comp'}, dimensions={0}, use_global_device_ids=true | all-gather | bytes 110592 | tf_op jit(solution)/shard_map/all_gather | solution.py:534
  26.8 1.9 %collective-permute-start.3 = (f32[33,8,128]{2,1,0:T(8,128)S(1)}, f32[33,8,128]{2,1,0:T(8,128)S(1)}, u32[]{:S(2)}, u32[]{:S(2)}) collective-permute-start(f32[33,8,128]{2,1,0:T(8,128)S(1)} %get-tuple-element.12), channel_id=1, source_target_pairs={{0,32},{1,33},{2,34},{3,35},{4,36},{5,37},{6,38},{7,39},{8,40},{9,... | collective-permute-start | bytes 405512 | tf_op jit(solution)/shard_map/ppermute | solution.py:539
  28.8 1.9 %collective-permute-start.2 = (f32[9,8,128]{2,1,0:T(8,128)S(1)}, f32[9,8,128]{2,1,0:T(8,128)S(1)}, u32[]{:S(2)}, u32[]{:S(2)}) collective-permute-start(f32[9,8,128]{2,1,0:T(8,128)S(1)} %get-tuple-element.11.side_ref), channel_id=1, source_target_pairs={{0,16},{1,17},{2,18},{3,19},{4,20},{5,21},{6,22},{7,23},{8,24},{9,... | collective-permute-start | bytes 110600 | tf_op jit(solution)/shard_map/ppermute | solution.py:538
  30.7 4.3 %collective-permute-done.2 = f32[9,8,128]{2,1,0:T(8,128)S(1)} collective-permute-done((f32[9,8,128]{2,1,0:T(8,128)S(1)}, f32[9,8,128]{2,1,0:T(8,128)S(1)}, u32[]{:S(2)}, u32[]{:S(2)}) %collective-permute-start.2) | collective-permute-done | bytes 36896 | tf_op jit(solution)/shard_map/ppermute | solution.py:538
  35.0 0.0 collective-permute-done.3
  35.0 0.0 collective-permute-done.1.main_ref
  35.1 9.6 %all-gather.1 = f32[1696,128]{1,0:T(8,128)S(1)} all-gather(f32[848,128]{1,0:T(8,128)S(1)} %shard_map.57), channel_id=3, replica_groups=mesh['comp'=2,'gx'=24,'gy'=16] {'comp'}, dimensions={0}, use_global_device_ids=true | all-gather | bytes 1302528 | tf_op jit(solution)/shard_map/all_gather | solution.py:543
  44.7 5.1 %shard_map.58 = f32[8,32,128]{2,1,0:T(8,128)} custom-call(s32[1]{0:T(128)} %bitcast.comp_ref, f32[2,8,128]{2,1,0:T(8,128)S(1)} %get-tuple-element.9.rates_ref, f32[2,8,32,128]{3,2,1,0:T(8,128)S(1)} %all_gather.15.own_ref, f32[9,8,128]{2,1,0:T(8,128)S(1)} %get-tuple-element.11.side_ref, f32[2,848,128]{2,1,0:T(8,128)S(1)} %bitcast.9), custom_call_target="tpu_custom_call" | custom-call | flops 20000000 | bytes 1306624 | tf_op jit(solution)/shard_map/pallas_call | solution.py:475
  (2 shorter events, 0.0 us)
Async XLA Ops:
  2.2 32.8 %collective-permute-start.1 = (f32[512,128]{1,0:T(8,128)S(1)}, f32[512,128]{1,0:T(8,128)S(1)}, u32[]{:S(2)}, u32[]{:S(2)}) collective-permute-start(f32[512,128]{1,0:T(8,128)S(1)} %bitcast.8), channel_id=1, source_target_pairs={{0,16},{1,17},{2,18},{3,19},{4,20},{5,21},{6,22},{7,23},{8,24},{9,... | collective-permute-start | bytes 786440 | tf_op jit(solution)/shard_map/ppermute | solution.py:529
  9.0 0.7 %copy-start.1 = (s32[4,128]{1,0:T(4,128)S(1)}, s32[4,128]{1,0:T(4,128)}, u32[]{:S(2)}) copy-start(s32[4,128]{1,0:T(4,128)} %depth_ref.3) | copy-start | bytes 6148
  9.0 0.7 %copy-start = (s32[4,128]{1,0:T(4,128)S(1)}, s32[4,128]{1,0:T(4,128)}, u32[]{:S(2)}) copy-start(s32[4,128]{1,0:T(4,128)} %land_ref.3) | copy-start | bytes 6148
  9.0 0.7 %copy-start.2 = (f32[8]{0:T(128)S(1)}, f32[8]{0:T(128)}, u32[]{:S(2)}) copy-start(f32[8]{0:T(128)} %growth_ref.1) | copy-start | bytes 100
  9.1 0.7 %copy-start.3 = (f32[8]{0:T(128)S(1)}, f32[8]{0:T(128)}, u32[]{:S(2)}) copy-start(f32[8]{0:T(128)} %decay_ref.1) | copy-start | bytes 100
  10.4 14.6 %collective-permute-start = (f32[9,8,128]{2,1,0:T(8,128)S(1)}, f32[9,8,128]{2,1,0:T(8,128)S(1)}, u32[]{:S(2)}, u32[]{:S(2)}) collective-permute-start(f32[9,8,128]{2,1,0:T(8,128)S(1)} %get-tuple-element.10), channel_id=1, source_target_pairs={{0,1},{1,2},{2,3},{3,4},{4,5},{5,6},{6,7},{7,8},{8,9},{9,10},{10,1... | collective-permute-start | bytes 110600 | tf_op jit(solution)/shard_map/ppermute | solution.py:533
  26.8 8.2 %collective-permute-start.3 = (f32[33,8,128]{2,1,0:T(8,128)S(1)}, f32[33,8,128]{2,1,0:T(8,128)S(1)}, u32[]{:S(2)}, u32[]{:S(2)}) collective-permute-start(f32[33,8,128]{2,1,0:T(8,128)S(1)} %get-tuple-element.12), channel_id=1, source_target_pairs={{0,32},{1,33},{2,34},{3,35},{4,36},{5,37},{6,38},{7,39},{8,40},{9,... | collective-permute-start | bytes 405512 | tf_op jit(solution)/shard_map/ppermute | solution.py:539
  28.8 6.3 %collective-permute-start.2 = (f32[9,8,128]{2,1,0:T(8,128)S(1)}, f32[9,8,128]{2,1,0:T(8,128)S(1)}, u32[]{:S(2)}, u32[]{:S(2)}) collective-permute-start(f32[9,8,128]{2,1,0:T(8,128)S(1)} %get-tuple-element.11.side_ref), channel_id=1, source_target_pairs={{0,16},{1,17},{2,18},{3,19},{4,20},{5,21},{6,22},{7,23},{8,24},{9,... | collective-permute-start | bytes 110600 | tf_op jit(solution)/shard_map/ppermute | solution.py:538

commit v3 on v2

--- a/solution.py
+++ b/solution.py
@@ -16,6 +16,7 @@
 LANES = 128
 FIELDS = 8
 PROG = 4
+HINT = 20_000_000_000
 ROWS = 4
 HALO = 8
 MAIN = 2 * FIELDS * ROWS
@@ -59,7 +60,7 @@
     return own_ref[comp, field, pl.ds(row, LEVELS, stride=ROWS), :]
 
 
-def pack_columns(comp_ref, growth_ref, decay_ref, own_ref, land_ref, depth_ref, out_ref, rates_ref):
+def pack_columns(comp_ref, own_ref, land_ref, depth_ref, out_ref, whole_ref):
     source = edge_source(comp_ref[0])
     for c in range(2):
         for r in range(ROWS):
@@ -72,9 +73,11 @@
     count = wet_count(land_ref, depth_ref)
     out_ref[EDGE] = jnp.zeros(TILE, jnp.float32)
     out_ref[EDGE, 0:ROWS, :] = jnp.where(source[0:ROWS], count, 0.0)
-    for f in range(FIELDS):
-        rates_ref[0, f : f + 1, :] = jnp.full((1, LANES), growth_ref[f])
-        rates_ref[1, f : f + 1, :] = jnp.full((1, LANES), decay_ref[f])
+    size = LEVELS * ROWS
+    for c in range(2):
+        for f in range(FIELDS):
+            at = (c * FIELDS + f) * size
+            whole_ref[at : at + size, :] = own_ref[c, f]
 
 
 def pack_rows(comp_ref, own_ref, land_ref, depth_ref, columns_ref, side_ref, far_ref):
@@ -525,15 +528,16 @@
     comp = lax.axis_index("comp").astype(jnp.int32).reshape(1)
     fields = ocean_state.reshape(FIELDS, LEVELS * ROWS, LANES)
     own = lax.all_gather(fields, "comp")
-    tall = (MAIN * LEVELS, LANES)
-    near_in = lax.ppermute(own.reshape(tall), axes, neighbours(gx, gy, 1, 0))
-    columns, rates = call(
-        pack_columns, [comp, growth, decay], [own, land_sea, depth_levels], [(SIDE,) + TILE, (2,) + TILE]
+    columns, whole = call(
+        pack_columns, [comp], [own, land_sea, depth_levels], [(SIDE,) + TILE, (MAIN * LEVELS, LANES)]
     )
     columns = lax.ppermute(columns, axes, neighbours(gx, gy, 0, 1))
+    near_in = lax.ppermute(whole, axes, neighbours(gx, gy, 1, 0))
+    rates = jnp.broadcast_to(jnp.stack([growth, decay])[:, :, None], (2, FIELDS, LANES))
     columns = lax.all_gather(columns, "comp")
     side, far = call(
-        pack_rows, [comp], [own, land_sea, depth_levels, columns], [(SIDE,) + TILE, (FAR,) + TILE]
+        pack_rows, [comp], [own, land_sea, depth_levels, columns], [(SIDE,) + TILE, (FAR,) + TILE],
+        flops=HINT,
     )
     side_in = lax.ppermute(side, axes, neighbours(gx, gy, 1, 0))
     far_in = lax.ppermute(far, axes, neighbours(gx, gy, 2, 0))

time: 50 us -> 45.3 us (0.906)
  the two profiles are of different devices: /device:TPU:376 before, /device:TPU:512 now
where the time goes in v3:
time: 45.3 us; the launch traced here: 45.1 us
  starting transfers between devices  16.1 us (36%)
  waiting for transfers between devices  15.7 us (35%)
  blocking collectives  6.48 us (14%)
  Pallas kernels  5.26 us (12%)
  local copies, waits for them, and re-layouts  1.42 us (3%)
    ppermute x1, waiting for transfers between devices, local(): side_in = lax.ppermute(side, axes, neighbours(gx, gy, 1, 0))  15.7 us
    pallas_call x4, Pallas kernels, call(): pl.pallas_call(kernel, out_shape=out_shape, in_specs=[pl.BlockSpec(memory...  5.26 us
    ppermute x1, starting transfers between devices, local(): side_in = lax.ppermute(side, axes, neighbours(gx, gy, 1, 0))  4.7 us
    ppermute x1, starting transfers between devices, local(): far_in = lax.ppermute(far, axes, neighbours(gx, gy, 2, 0))  4.5 us
    ppermute x1, starting transfers between devices, local(): near_in = lax.ppermute(whole, axes, neighbours(gx, gy, 1, 0))  3.48 us
    ppermute x1, starting transfers between devices, local(): columns = lax.ppermute(columns, axes, neighbours(gx, gy, 0, 1))  3.4 us
    all_gather x1, blocking collectives, local(): received = lax.all_gather(received, 'comp')  2.43 us
    all_gather x1, blocking collectives, local(): own = lax.all_gather(fields, 'comp')  2.19 us
  transfers between devices with their start and end apart: 4, of which 1 were waited for; matrix products, arithmetic and copies ran while one was open for 0% of the time, Pallas kernels for 0%

profile of v3, /device:TPU:512, one launch (start us, length us, event | category | flops | bytes accessed | tf_op | source)
XLA Modules:
  0.0 45.1 jit_solution(7445155875741797301)
XLA Ops:
  0.0 2.2 %all_gather.15.own_ref = f32[2,8,32,128]{3,2,1,0:T(8,128)S(1)} all-gather(f32[1,8,32,128]{3,2,1,0:T(8,128)} %bitcast.13), channel_id=1, replica_groups=mesh['comp'=2,'gx'=24,'gy'=16] {'comp'}, dimensions={0}, use_global_device_ids=true | all-gather | bytes 393216 | tf_op jit(solution)/shard_map/all_gather | solution.py:530
  2.2 0.0 copy-start.1
  2.2 0.0 copy-start
  2.2 0.7 %copy-done.1 = s32[4,128]{1,0:T(4,128)S(1)} copy-done((s32[4,128]{1,0:T(4,128)S(1)}, s32[4,128]{1,0:T(4,128)}, u32[]{:S(2)}) %copy-start.1) | copy-done | bytes 2072
  2.9 0.0 copy-done
  2.9 0.1 shard_map.55
  3.0 3.4 %collective-permute-start = (f32[9,8,128]{2,1,0:T(8,128)S(1)}, f32[9,8,128]{2,1,0:T(8,128)S(1)}, u32[]{:S(2)}, u32[]{:S(2)}) collective-permute-start(f32[9,8,128]{2,1,0:T(8,128)S(1)} %get-tuple-element.9), channel_id=1, source_target_pairs={{0,1},{1,2},{2,3},{3,4},{4,5},{5,6},{6,7},{7,8},{8,9},{9,10},{10,1... | collective-permute-start | bytes 110600 | tf_op jit(solution)/shard_map/ppermute | solution.py:534
  6.4 3.5 %collective-permute-start.1 = (f32[512,128]{1,0:T(8,128)S(1)}, f32[512,128]{1,0:T(8,128)S(1)}, u32[]{:S(2)}, u32[]{:S(2)}) collective-permute-start(f32[512,128]{1,0:T(8,128)S(1)} %get-tuple-element.11), channel_id=1, source_target_pairs={{0,16},{1,17},{2,18},{3,19},{4,20},{5,21},{6,22},{7,23},{8,24},{9,... | collective-permute-start | bytes 786440 | tf_op jit(solution)/shard_map/ppermute | solution.py:535
  9.9 0.0 collective-permute-done
  9.9 1.9 %all-gather = f32[18,8,128]{2,1,0:T(8,128)S(1)} all-gather(f32[9,8,128]{2,1,0:T(8,128)S(1)} %collective-permute-done), channel_id=2, replica_groups=mesh['comp'=2,'gx'=24,'gy'=16] {'comp'}, dimensions={0}, use_global_device_ids=true | all-gather | bytes 110592 | tf_op jit(solution)/shard_map/all_gather | solution.py:537
  11.8 4.5 %collective-permute-start.3 = (f32[33,8,128]{2,1,0:T(8,128)S(1)}, f32[33,8,128]{2,1,0:T(8,128)S(1)}, u32[]{:S(2)}, u32[]{:S(2)}) collective-permute-start(f32[33,8,128]{2,1,0:T(8,128)S(1)} %get-tuple-element.12), channel_id=1, source_target_pairs={{0,32},{1,33},{2,34},{3,35},{4,36},{5,37},{6,38},{7,39},{8,40},{9,... | collective-permute-start | bytes 405512 | tf_op jit(solution)/shard_map/ppermute | solution.py:543
  16.3 4.7 %collective-permute-start.2 = (f32[9,8,128]{2,1,0:T(8,128)S(1)}, f32[9,8,128]{2,1,0:T(8,128)S(1)}, u32[]{:S(2)}, u32[]{:S(2)}) collective-permute-start(f32[9,8,128]{2,1,0:T(8,128)S(1)} %get-tuple-element.10.side_ref), channel_id=1, source_target_pairs={{0,16},{1,17},{2,18},{3,19},{4,20},{5,21},{6,22},{7,23},{8,24},{9,... | collective-permute-start | bytes 110600 | tf_op jit(solution)/shard_map/ppermute | solution.py:542
  21.0 0.0 copy-start.2
  21.0 0.0 copy-start.3
  21.1 0.6 %copy-done.2 = f32[8]{0:T(128)S(1)} copy-done((f32[8]{0:T(128)S(1)}, f32[8]{0:T(128)}, u32[]{:S(2)}) %copy-start.2) | copy-done | bytes 56
  21.7 0.0 copy-done.3
  21.7 15.7 %collective-permute-done.2 = f32[9,8,128]{2,1,0:T(8,128)S(1)} collective-permute-done((f32[9,8,128]{2,1,0:T(8,128)S(1)}, f32[9,8,128]{2,1,0:T(8,128)S(1)}, u32[]{:S(2)}, u32[]{:S(2)}) %collective-permute-start.2) | collective-permute-done | bytes 36896 | tf_op jit(solution)/shard_map/ppermute | solution.py:542
  37.4 0.0 collective-permute-done.3
  37.5 0.0 collective-permute-done.1.main_ref
  37.5 2.4 %all-gather.1 = f32[1696,128]{1,0:T(8,128)S(1)} all-gather(f32[848,128]{1,0:T(8,128)S(1)} %shard_map.57), channel_id=3, replica_groups=mesh['comp'=2,'gx'=24,'gy'=16] {'comp'}, dimensions={0}, use_global_device_ids=true | all-gather | bytes 1302528 | tf_op jit(solution)/shard_map/all_gather | solution.py:547
  39.9 0.1 broadcast_in_dim.2.rates_ref
  40.0 5.1 %shard_map.58 = f32[8,32,128]{2,1,0:T(8,128)} custom-call(s32[1]{0:T(128)} %bitcast.comp_ref, f32[2,8,128]{2,1,0:T(8,128)S(1)} %broadcast_in_dim.2.rates_ref, f32[2,8,32,128]{3,2,1,0:T(8,128)S(1)} %all_gather.15.own_ref, f32[9,8,128]{2,1,0:T(8,128)S(1)} %get-tuple-element.10.side_ref, f32[2,848,128]{2,1,0:T(8,128)S(1)} %bitcast.9), custom_call_target="tpu_custom_call" | custom-call | flops 20000000 | bytes 1306624 | tf_op jit(solution)/shard_map/pallas_call | solution.py:478
  (3 shorter events, 0.1 us)
Async XLA Ops:
  2.2 0.7 %copy-start.1 = (s32[4,128]{1,0:T(4,128)S(1)}, s32[4,128]{1,0:T(4,128)}, u32[]{:S(2)}) copy-start(s32[4,128]{1,0:T(4,128)} %depth_ref.3) | copy-start | bytes 6148
  2.2 0.7 %copy-start = (s32[4,128]{1,0:T(4,128)S(1)}, s32[4,128]{1,0:T(4,128)}, u32[]{:S(2)}) copy-start(s32[4,128]{1,0:T(4,128)} %land_ref.3) | copy-start | bytes 6148
  3.0 6.9 %collective-permute-start = (f32[9,8,128]{2,1,0:T(8,128)S(1)}, f32[9,8,128]{2,1,0:T(8,128)S(1)}, u32[]{:S(2)}, u32[]{:S(2)}) collective-permute-start(f32[9,8,128]{2,1,0:T(8,128)S(1)} %get-tuple-element.9), channel_id=1, source_target_pairs={{0,1},{1,2},{2,3},{3,4},{4,5},{5,6},{6,7},{7,8},{8,9},{9,10},{10,1... | collective-permute-start | bytes 110600 | tf_op jit(solution)/shard_map/ppermute | solution.py:534
  6.4 31.0 %collective-permute-start.1 = (f32[512,128]{1,0:T(8,128)S(1)}, f32[512,128]{1,0:T(8,128)S(1)}, u32[]{:S(2)}, u32[]{:S(2)}) collective-permute-start(f32[512,128]{1,0:T(8,128)S(1)} %get-tuple-element.11), channel_id=1, source_target_pairs={{0,16},{1,17},{2,18},{3,19},{4,20},{5,21},{6,22},{7,23},{8,24},{9,... | collective-permute-start | bytes 786440 | tf_op jit(solution)/shard_map/ppermute | solution.py:535
  11.8 25.6 %collective-permute-start.3 = (f32[33,8,128]{2,1,0:T(8,128)S(1)}, f32[33,8,128]{2,1,0:T(8,128)S(1)}, u32[]{:S(2)}, u32[]{:S(2)}) collective-permute-start(f32[33,8,128]{2,1,0:T(8,128)S(1)} %get-tuple-element.12), channel_id=1, source_target_pairs={{0,32},{1,33},{2,34},{3,35},{4,36},{5,37},{6,38},{7,39},{8,40},{9,... | collective-permute-start | bytes 405512 | tf_op jit(solution)/shard_map/ppermute | solution.py:543
  16.3 21.1 %collective-permute-start.2 = (f32[9,8,128]{2,1,0:T(8,128)S(1)}, f32[9,8,128]{2,1,0:T(8,128)S(1)}, u32[]{:S(2)}, u32[]{:S(2)}) collective-permute-start(f32[9,8,128]{2,1,0:T(8,128)S(1)} %get-tuple-element.10.side_ref), channel_id=1, source_target_pairs={{0,16},{1,17},{2,18},{3,19},{4,20},{5,21},{6,22},{7,23},{8,24},{9,... | collective-permute-start | bytes 110600 | tf_op jit(solution)/shard_map/ppermute | solution.py:542
  21.0 0.7 %copy-start.2 = (f32[8]{0:T(128)S(1)}, f32[8]{0:T(128)}, u32[]{:S(2)}) copy-start(f32[8]{0:T(128)} %param.9) | copy-start | bytes 100
  21.0 0.7 %copy-start.3 = (f32[8]{0:T(128)S(1)}, f32[8]{0:T(128)}, u32[]{:S(2)}) copy-start(f32[8]{0:T(128)} %param.8) | copy-start | bytes 100

commit v4 on v3

--- a/solution.py
+++ b/solution.py
@@ -16,7 +16,6 @@
 LANES = 128
 FIELDS = 8
 PROG = 4
-HINT = 20_000_000_000
 ROWS = 4
 HALO = 8
 MAIN = 2 * FIELDS * ROWS
@@ -47,7 +46,7 @@
 
 
 def edge_source(comp):
-    first = jnp.where(comp == 0, LANES - HALO, 0)
+    first = jnp.where(comp == 0, 0, LANES - HALO)
     lane = lanes()
     return (lane >= first) & (lane < first + HALO)
 
@@ -60,7 +59,7 @@
     return own_ref[comp, field, pl.ds(row, LEVELS, stride=ROWS), :]
 
 
-def pack_columns(comp_ref, own_ref, land_ref, depth_ref, out_ref, whole_ref):
+def pack_columns(comp_ref, own_ref, land_ref, depth_ref, out_ref):
     source = edge_source(comp_ref[0])
     for c in range(2):
         for r in range(ROWS):
@@ -73,11 +72,6 @@
     count = wet_count(land_ref, depth_ref)
     out_ref[EDGE] = jnp.zeros(TILE, jnp.float32)
     out_ref[EDGE, 0:ROWS, :] = jnp.where(source[0:ROWS], count, 0.0)
-    size = LEVELS * ROWS
-    for c in range(2):
-        for f in range(FIELDS):
-            at = (c * FIELDS + f) * size
-            whole_ref[at : at + size, :] = own_ref[c, f]
 
 
 def pack_rows(comp_ref, own_ref, land_ref, depth_ref, columns_ref, side_ref, far_ref):
@@ -528,16 +522,13 @@
     comp = lax.axis_index("comp").astype(jnp.int32).reshape(1)
     fields = ocean_state.reshape(FIELDS, LEVELS * ROWS, LANES)
     own = lax.all_gather(fields, "comp")
-    columns, whole = call(
-        pack_columns, [comp], [own, land_sea, depth_levels], [(SIDE,) + TILE, (MAIN * LEVELS, LANES)]
-    )
-    columns = lax.ppermute(columns, axes, neighbours(gx, gy, 0, 1))
-    near_in = lax.ppermute(whole, axes, neighbours(gx, gy, 1, 0))
+    near_in = lax.ppermute(own.reshape(MAIN * LEVELS, LANES), axes, neighbours(gx, gy, 1, 0))
+    (columns,) = call(pack_columns, [comp], [own, land_sea, depth_levels], [(SIDE,) + TILE])
+    columns = lax.ppermute(columns, axes, neighbours(gx, gy, 0, -1))
     rates = jnp.broadcast_to(jnp.stack([growth, decay])[:, :, None], (2, FIELDS, LANES))
     columns = lax.all_gather(columns, "comp")
     side, far = call(
         pack_rows, [comp], [own, land_sea, depth_levels, columns], [(SIDE,) + TILE, (FAR,) + TILE],
-        flops=HINT,
     )
     side_in = lax.ppermute(side, axes, neighbours(gx, gy, 1, 0))
     far_in = lax.ppermute(far, axes, neighbours(gx, gy, 2, 0))

time: 45.3 us -> 46 us (1.015)
  the two profiles are of different devices: /device:TPU:512 before, /device:TPU:126 now
where the time goes in v4:
time: 46 us; the launch traced here: 45.7 us
  starting transfers between devices  20.8 us (45%)
  blocking collectives  10.8 us (23%)
  waiting for transfers between devices  7.27 us (16%)
  Pallas kernels  5.26 us (11%)
  local copies, waits for them, and re-layouts  1.41 us (3%)
    ppermute x1, starting transfers between devices, local(): lax.ppermute(own.reshape(MAIN * LEVELS, LANES), axes, neighbours(gx, gy,...  10.1 us
    all_gather x1, blocking collectives, local(): received = lax.all_gather(received, 'comp')  6.77 us
    pallas_call x4, Pallas kernels, call(): pl.pallas_call(kernel, out_shape=out_shape, in_specs=[pl.BlockSpec(memory...  5.26 us
    ppermute x1, waiting for transfers between devices, local(): columns = lax.ppermute(columns, axes, neighbours(gx, gy, 0, -1))  5.22 us
    ppermute x1, starting transfers between devices, local(): far_in = lax.ppermute(far, axes, neighbours(gx, gy, 2, 0))  4.5 us
    ppermute x1, starting transfers between devices, local(): side_in = lax.ppermute(side, axes, neighbours(gx, gy, 1, 0))  3.48 us
    ppermute x1, starting transfers between devices, local(): columns = lax.ppermute(columns, axes, neighbours(gx, gy, 0, -1))  2.74 us
    all_gather x1, blocking collectives, local(): own = lax.all_gather(fields, 'comp')  2.19 us
  transfers between devices with their start and end apart: 4, of which 2 were waited for; matrix products, arithmetic and copies ran while one was open for 0% of the time, Pallas kernels for 0%

profile of v4, /device:TPU:126, one launch (start us, length us, event | category | flops | bytes accessed | tf_op | source)
XLA Modules:
  0.0 45.7 jit_solution(16698039093360220084)
XLA Ops:
  0.0 2.2 %all_gather.15.own_ref = f32[2,8,32,128]{3,2,1,0:T(8,128)S(1)} all-gather(f32[1,8,32,128]{3,2,1,0:T(8,128)} %bitcast.15), channel_id=1, replica_groups=mesh['comp'=2,'gx'=24,'gy'=16] {'comp'}, dimensions={0}, use_global_device_ids=true | all-gather | bytes 393216 | tf_op jit(solution)/shard_map/all_gather | solution.py:524
  2.2 10.1 %collective-permute-start.1 = (f32[512,128]{1,0:T(8,128)S(1)}, f32[512,128]{1,0:T(8,128)S(1)}, u32[]{:S(2)}, u32[]{:S(2)}) collective-permute-start(f32[512,128]{1,0:T(8,128)S(1)} %bitcast.10), channel_id=1, source_target_pairs={{0,16},{1,17},{2,18},{3,19},{4,20},{5,21},{6,22},{7,23},{8,24},{9,... | collective-permute-start | bytes 786440 | tf_op jit(solution)/shard_map/ppermute | solution.py:525
  12.3 0.0 copy-start.1
  12.3 0.0 copy-start
  12.3 0.7 %copy-done.1 = s32[4,128]{1,0:T(4,128)S(1)} copy-done((s32[4,128]{1,0:T(4,128)S(1)}, s32[4,128]{1,0:T(4,128)}, u32[]{:S(2)}) %copy-start.1) | copy-done | bytes 2072
  13.0 0.0 copy-done
  13.0 0.1 shard_map.55
  13.2 2.7 %collective-permute-start = (f32[9,8,128]{2,1,0:T(8,128)S(1)}, f32[9,8,128]{2,1,0:T(8,128)S(1)}, u32[]{:S(2)}, u32[]{:S(2)}) collective-permute-start(f32[9,8,128]{2,1,0:T(8,128)S(1)} %shard_map.55), channel_id=1, source_target_pairs={{1,0},{2,1},{3,2},{4,3},{5,4},{6,5},{7,6},{8,7},{9,8},{10,9},{11,1... | collective-permute-start | bytes 110600 | tf_op jit(solution)/shard_map/ppermute | solution.py:527
  15.9 5.2 %collective-permute-done = f32[9,8,128]{2,1,0:T(8,128)S(1)} collective-permute-done((f32[9,8,128]{2,1,0:T(8,128)S(1)}, f32[9,8,128]{2,1,0:T(8,128)S(1)}, u32[]{:S(2)}, u32[]{:S(2)}) %collective-permute-start) | collective-permute-done | bytes 36896 | tf_op jit(solution)/shard_map/ppermute | solution.py:527
  21.1 1.8 %all-gather = f32[18,8,128]{2,1,0:T(8,128)S(1)} all-gather(f32[9,8,128]{2,1,0:T(8,128)S(1)} %collective-permute-done), channel_id=2, replica_groups=mesh['comp'=2,'gx'=24,'gy'=16] {'comp'}, dimensions={0}, use_global_device_ids=true | all-gather | bytes 110592 | tf_op jit(solution)/shard_map/all_gather | solution.py:529
  23.0 4.5 %collective-permute-start.3 = (f32[33,8,128]{2,1,0:T(8,128)S(1)}, f32[33,8,128]{2,1,0:T(8,128)S(1)}, u32[]{:S(2)}, u32[]{:S(2)}) collective-permute-start(f32[33,8,128]{2,1,0:T(8,128)S(1)} %get-tuple-element.8), channel_id=1, source_target_pairs={{0,32},{1,33},{2,34},{3,35},{4,36},{5,37},{6,38},{7,39},{8,40},{9,... | collective-permute-start | bytes 405512 | tf_op jit(solution)/shard_map/ppermute | solution.py:534
  27.5 3.5 %collective-permute-start.2 = (f32[9,8,128]{2,1,0:T(8,128)S(1)}, f32[9,8,128]{2,1,0:T(8,128)S(1)}, u32[]{:S(2)}, u32[]{:S(2)}) collective-permute-start(f32[9,8,128]{2,1,0:T(8,128)S(1)} %get-tuple-element.7.side_ref), channel_id=1, source_target_pairs={{0,16},{1,17},{2,18},{3,19},{4,20},{5,21},{6,22},{7,23},{8,24},{9,... | collective-permute-start | bytes 110600 | tf_op jit(solution)/shard_map/ppermute | solution.py:533
  31.0 0.0 copy-start.2
  31.0 0.0 copy-start.3
  31.0 0.6 %copy-done.2 = f32[8]{0:T(128)S(1)} copy-done((f32[8]{0:T(128)S(1)}, f32[8]{0:T(128)}, u32[]{:S(2)}) %copy-start.2) | copy-done | bytes 56
  31.6 0.0 copy-done.3
  31.7 2.1 %collective-permute-done.2 = f32[9,8,128]{2,1,0:T(8,128)S(1)} collective-permute-done((f32[9,8,128]{2,1,0:T(8,128)S(1)}, f32[9,8,128]{2,1,0:T(8,128)S(1)}, u32[]{:S(2)}, u32[]{:S(2)}) %collective-permute-start.2) | collective-permute-done | bytes 36896 | tf_op jit(solution)/shard_map/ppermute | solution.py:533
  33.7 0.0 collective-permute-done.3
  33.7 0.0 collective-permute-done.1.main_ref
  33.8 6.8 %all-gather.1 = f32[1696,128]{1,0:T(8,128)S(1)} all-gather(f32[848,128]{1,0:T(8,128)S(1)} %shard_map.57), channel_id=3, replica_groups=mesh['comp'=2,'gx'=24,'gy'=16] {'comp'}, dimensions={0}, use_global_device_ids=true | all-gather | bytes 1302528 | tf_op jit(solution)/shard_map/all_gather | solution.py:538
  40.5 0.1 broadcast_in_dim.2.rates_ref
  40.6 5.1 %shard_map.58 = f32[8,32,128]{2,1,0:T(8,128)} custom-call(s32[1]{0:T(128)} %bitcast.comp_ref, f32[2,8,128]{2,1,0:T(8,128)S(1)} %broadcast_in_dim.2.rates_ref, f32[2,8,32,128]{3,2,1,0:T(8,128)S(1)} %all_gather.15.own_ref, f32[9,8,128]{2,1,0:T(8,128)S(1)} %get-tuple-element.7.side_ref, f32[2,848,128]{2,1,0:T(8,128)S(1)} %bitcast.11), custom_call_target="tpu_custom_call" | custom-call | flops 20000000 | bytes 1306624 | tf_op jit(solution)/shard_map/pallas_call | solution.py:472
  (3 shorter events, 0.1 us)
Async XLA Ops:
  2.2 31.5 %collective-permute-start.1 = (f32[512,128]{1,0:T(8,128)S(1)}, f32[512,128]{1,0:T(8,128)S(1)}, u32[]{:S(2)}, u32[]{:S(2)}) collective-permute-start(f32[512,128]{1,0:T(8,128)S(1)} %bitcast.10), channel_id=1, source_target_pairs={{0,16},{1,17},{2,18},{3,19},{4,20},{5,21},{6,22},{7,23},{8,24},{9,... | collective-permute-start | bytes 786440 | tf_op jit(solution)/shard_map/ppermute | solution.py:525
  12.3 0.7 %copy-start.1 = (s32[4,128]{1,0:T(4,128)S(1)}, s32[4,128]{1,0:T(4,128)}, u32[]{:S(2)}) copy-start(s32[4,128]{1,0:T(4,128)} %depth_ref.3) | copy-start | bytes 6148
  12.3 0.7 %copy-start = (s32[4,128]{1,0:T(4,128)S(1)}, s32[4,128]{1,0:T(4,128)}, u32[]{:S(2)}) copy-start(s32[4,128]{1,0:T(4,128)} %land_ref.3) | copy-start | bytes 6148
  13.2 8.0 %collective-permute-start = (f32[9,8,128]{2,1,0:T(8,128)S(1)}, f32[9,8,128]{2,1,0:T(8,128)S(1)}, u32[]{:S(2)}, u32[]{:S(2)}) collective-permute-start(f32[9,8,128]{2,1,0:T(8,128)S(1)} %shard_map.55), channel_id=1, source_target_pairs={{1,0},{2,1},{3,2},{4,3},{5,4},{6,5},{7,6},{8,7},{9,8},{10,9},{11,1... | collective-permute-start | bytes 110600 | tf_op jit(solution)/shard_map/ppermute | solution.py:527
  23.0 10.7 %collective-permute-start.3 = (f32[33,8,128]{2,1,0:T(8,128)S(1)}, f32[33,8,128]{2,1,0:T(8,128)S(1)}, u32[]{:S(2)}, u32[]{:S(2)}) collective-permute-start(f32[33,8,128]{2,1,0:T(8,128)S(1)} %get-tuple-element.8), channel_id=1, source_target_pairs={{0,32},{1,33},{2,34},{3,35},{4,36},{5,37},{6,38},{7,39},{8,40},{9,... | collective-permute-start | bytes 405512 | tf_op jit(solution)/shard_map/ppermute | solution.py:534
  27.5 6.2 %collective-permute-start.2 = (f32[9,8,128]{2,1,0:T(8,128)S(1)}, f32[9,8,128]{2,1,0:T(8,128)S(1)}, u32[]{:S(2)}, u32[]{:S(2)}) collective-permute-start(f32[9,8,128]{2,1,0:T(8,128)S(1)} %get-tuple-element.7.side_ref), channel_id=1, source_target_pairs={{0,16},{1,17},{2,18},{3,19},{4,20},{5,21},{6,22},{7,23},{8,24},{9,... | collective-permute-start | bytes 110600 | tf_op jit(solution)/shard_map/ppermute | solution.py:533
  31.0 0.7 %copy-start.2 = (f32[8]{0:T(128)S(1)}, f32[8]{0:T(128)}, u32[]{:S(2)}) copy-start(f32[8]{0:T(128)} %param.9) | copy-start | bytes 100
  31.0 0.7 %copy-start.3 = (f32[8]{0:T(128)S(1)}, f32[8]{0:T(128)}, u32[]{:S(2)}) copy-start(f32[8]{0:T(128)} %param.8) | copy-start | bytes 100

commit v5 on v4

--- a/solution.py
+++ b/solution.py
@@ -23,13 +23,11 @@
 SIDE = EDGE + 1
 FAR_G = PROG * ROWS
 FAR_CHL = FAR_G + PROG * 2
-FAR_EDGE = FAR_CHL + 2
-FAR_CHL_EDGE = FAR_EDGE + ROWS
-FAR_WET = FAR_CHL_EDGE + 2
-FAR = FAR_WET + 1
+FAR = FAR_CHL + 2
 IN_SIDE = MAIN
-IN_FAR = MAIN + SIDE
-IN = IN_FAR + FAR
+IN_FAR = IN_SIDE + SIDE
+IN_FAR_SIDE = IN_FAR + FAR
+IN = IN_FAR_SIDE + SIDE
 DYN_ROWS = 5 * ROWS
 TRC_ROWS = 3 * ROWS
 TILE = (LEVELS, LANES)
@@ -59,8 +57,9 @@
     return own_ref[comp, field, pl.ds(row, LEVELS, stride=ROWS), :]
 
 
-def pack_columns(comp_ref, own_ref, land_ref, depth_ref, out_ref):
-    source = edge_source(comp_ref[0])
+def pack_columns(comp_ref, own_ref, land_ref, depth_ref, out_ref, far_ref):
+    comp = comp_ref[0]
+    source = edge_source(comp)
     for c in range(2):
         for r in range(ROWS):
             total = None
@@ -72,36 +71,28 @@
     count = wet_count(land_ref, depth_ref)
     out_ref[EDGE] = jnp.zeros(TILE, jnp.float32)
     out_ref[EDGE, 0:ROWS, :] = jnp.where(source[0:ROWS], count, 0.0)
-
-
-def pack_rows(comp_ref, own_ref, land_ref, depth_ref, columns_ref, side_ref, far_ref):
-    first = jnp.where(comp_ref[0] == 0, 2, 0)
     for f in range(PROG):
         for r in range(ROWS):
             far_ref[f * ROWS + r] = row_of(own_ref, 0, f, r)
+    first = jnp.where(comp == 0, 2, 0)
     for k in range(2):
         for f in range(PROG):
             far_ref[FAR_G + f * 2 + k] = row_of(own_ref, 0, PROG + f, first + k)
         far_ref[FAR_CHL + k] = row_of(own_ref, 1, 0, first + k)
-        at = ROWS + first + k
-        far_ref[FAR_CHL_EDGE + k] = columns_ref[0, at] + columns_ref[1, at]
+
+
+def pack_corners(land_ref, depth_ref, columns_ref, side_ref):
     for t in range(EDGE):
-        joined = columns_ref[0, t] + columns_ref[1, t]
-        side_ref[t] = joined
-        if t < ROWS:
-            far_ref[FAR_EDGE + t] = joined
-    count = wet_count(land_ref, depth_ref)
-    outer = columns_ref[0, EDGE, 0:ROWS, :] + columns_ref[1, EDGE, 0:ROWS, :]
-    for ref, at in ((side_ref, EDGE), (far_ref, FAR_WET)):
-        ref[at, 0:ROWS, :] = count
-        ref[at, ROWS : 2 * ROWS, :] = outer
-
-
-def join(main_ref, side_ref, far_ref, out_ref):
+        side_ref[t] = columns_ref[0, t] + columns_ref[1, t]
+    side_ref[EDGE, 0:ROWS, :] = wet_count(land_ref, depth_ref)
+    side_ref[EDGE, ROWS : 2 * ROWS, :] = columns_ref[0, EDGE, 0:ROWS, :] + columns_ref[1, EDGE, 0:ROWS, :]
+
+
+def join(*refs):
     at = 0
-    for ref in (main_ref, side_ref, far_ref):
+    for ref in refs[:-1]:
         size = ref.shape[0]
-        out_ref[at : at + size, :] = ref[...]
+        refs[-1][at : at + size, :] = ref[...]
         at += size
 
 
@@ -141,10 +132,10 @@
             return tile(FAR_CHL + r - first)
         return tile(f * ROWS + r if f < PROG else FAR_G + (f - PROG) * 2 + r - first)
 
-    at = (IN_FAR + FAR_WET) * LEVELS
+    at = (IN_FAR_SIDE + EDGE) * LEVELS
     return Block(
         main,
-        lambda c, r: tile(FAR_EDGE + r if c == 0 else FAR_CHL_EDGE + r - first),
+        lambda c, r: tile(FAR + c * ROWS + r),
         lambda row: in_ref[way, at + row : at + row + 1, :],
         range(first, first + 2),
     )
@@ -523,18 +514,18 @@
     fields = ocean_state.reshape(FIELDS, LEVELS * ROWS, LANES)
     own = lax.all_gather(fields, "comp")
     near_in = lax.ppermute(own.reshape(MAIN * LEVELS, LANES), axes, neighbours(gx, gy, 1, 0))
-    (columns,) = call(pack_columns, [comp], [own, land_sea, depth_levels], [(SIDE,) + TILE])
+    columns, far = call(
+        pack_columns, [comp], [own, land_sea, depth_levels], [(SIDE,) + TILE, (FAR,) + TILE]
+    )
     columns = lax.ppermute(columns, axes, neighbours(gx, gy, 0, -1))
+    far_in = lax.ppermute(far, axes, neighbours(gx, gy, 2, 0))
     rates = jnp.broadcast_to(jnp.stack([growth, decay])[:, :, None], (2, FIELDS, LANES))
     columns = lax.all_gather(columns, "comp")
-    side, far = call(
-        pack_rows, [comp], [own, land_sea, depth_levels, columns], [(SIDE,) + TILE, (FAR,) + TILE],
-    )
+    (side,) = call(pack_corners, [], [land_sea, depth_levels, columns], [(SIDE,) + TILE])
     side_in = lax.ppermute(side, axes, neighbours(gx, gy, 1, 0))
-    far_in = lax.ppermute(far, axes, neighbours(gx, gy, 2, 0))
-    (received,) = call(
-        join, [], [near_in, side_in.reshape(-1, LANES), far_in.reshape(-1, LANES)], [(IN * LEVELS, LANES)]
-    )
+    far_side_in = lax.ppermute(side, axes, neighbours(gx, gy, 2, 0))
+    parts = [a.reshape(-1, LANES) for a in (near_in, side_in, far_in, far_side_in)]
+    (received,) = call(join, [], parts, [(IN * LEVELS, LANES)])
     received = lax.all_gather(received, "comp")
     out = all_steps(comp, rates, own, side, received)
     return out.reshape(ocean_state.shape)

time: 46 us -> 45.1 us (0.980)
  the two profiles are of different devices: /device:TPU:126 before, /device:TPU:184 now
where the time goes in v5:
time: 45.1 us; the launch traced here: 44.8 us
  starting transfers between devices  26.7 us (59%)
  blocking collectives  9.81 us (22%)
  Pallas kernels  5.25 us (12%)
  waiting for transfers between devices  1.54 us (3%)
  local copies, waits for them, and re-layouts  1.41 us (3%)
    ppermute x1, starting transfers between devices, local(): lax.ppermute(own.reshape(MAIN * LEVELS, LANES), axes, neighbours(gx, gy,...  10.1 us
    all_gather x1, blocking collectives, local(): received = lax.all_gather(received, 'comp')  5.75 us
    pallas_call x4, Pallas kernels, call(): pl.pallas_call(kernel, out_shape=out_shape, in_specs=[pl.BlockSpec(memory...  5.25 us
    ppermute x1, starting transfers between devices, local(): far_side_in = lax.ppermute(side, axes, neighbours(gx, gy, 2, 0))  4.81 us
    ppermute x1, starting transfers between devices, local(): far_in = lax.ppermute(far, axes, neighbours(gx, gy, 2, 0))  4.5 us
    ppermute x1, starting transfers between devices, local(): columns = lax.ppermute(columns, axes, neighbours(gx, gy, 0, -1))  3.76 us
    ppermute x1, starting transfers between devices, local(): side_in = lax.ppermute(side, axes, neighbours(gx, gy, 1, 0))  3.48 us
    all_gather x1, blocking collectives, local(): own = lax.all_gather(fields, 'comp')  2.19 us
  transfers between devices with their start and end apart: 5, of which 1 were waited for; matrix products, arithmetic and copies ran while one was open for 0% of the time, Pallas kernels for 0%

profile of v5, /device:TPU:184, one launch (start us, length us, event | category | flops | bytes accessed | tf_op | source)
XLA Modules:
  0.0 44.8 jit_solution(3699101643763242394)
XLA Ops:
  0.0 2.2 %all_gather.15.own_ref = f32[2,8,32,128]{3,2,1,0:T(8,128)S(1)} all-gather(f32[1,8,32,128]{3,2,1,0:T(8,128)} %bitcast.17), channel_id=1, replica_groups=mesh['comp'=2,'gx'=24,'gy'=16] {'comp'}, dimensions={0}, use_global_device_ids=true | all-gather | bytes 393216 | tf_op jit(solution)/shard_map/all_gather | solution.py:515
  2.2 10.1 %collective-permute-start.1 = (f32[512,128]{1,0:T(8,128)S(1)}, f32[512,128]{1,0:T(8,128)S(1)}, u32[]{:S(2)}, u32[]{:S(2)}) collective-permute-start(f32[512,128]{1,0:T(8,128)S(1)} %bitcast.12), channel_id=1, source_target_pairs={{0,16},{1,17},{2,18},{3,19},{4,20},{5,21},{6,22},{7,23},{8,24},{9,... | collective-permute-start | bytes 786440 | tf_op jit(solution)/shard_map/ppermute | solution.py:516
  12.3 0.0 copy-start.1
  12.3 0.0 copy-start
  12.3 0.7 %copy-done.1 = s32[4,128]{1,0:T(4,128)S(1)} copy-done((s32[4,128]{1,0:T(4,128)S(1)}, s32[4,128]{1,0:T(4,128)}, u32[]{:S(2)}) %copy-start.1) | copy-done | bytes 2072
  13.0 0.0 copy-done
  13.0 0.1 shard_map.55
  13.2 3.8 %collective-permute-start = (f32[9,8,128]{2,1,0:T(8,128)S(1)}, f32[9,8,128]{2,1,0:T(8,128)S(1)}, u32[]{:S(2)}, u32[]{:S(2)}) collective-permute-start(f32[9,8,128]{2,1,0:T(8,128)S(1)} %get-tuple-element.7), channel_id=1, source_target_pairs={{1,0},{2,1},{3,2},{4,3},{5,4},{6,5},{7,6},{8,7},{9,8},{10,9},{11,1... | collective-permute-start | bytes 110600 | tf_op jit(solution)/shard_map/ppermute | solution.py:520
  16.9 4.5 %collective-permute-start.3 = (f32[26,8,128]{2,1,0:T(8,128)S(1)}, f32[26,8,128]{2,1,0:T(8,128)S(1)}, u32[]{:S(2)}, u32[]{:S(2)}) collective-permute-start(f32[26,8,128]{2,1,0:T(8,128)S(1)} %get-tuple-element.8), channel_id=1, source_target_pairs={{0,32},{1,33},{2,34},{3,35},{4,36},{5,37},{6,38},{7,39},{8,40},{9,... | collective-permute-start | bytes 319496 | tf_op jit(solution)/shard_map/ppermute | solution.py:521
  21.4 0.0 collective-permute-done
  21.4 1.9 %all-gather = f32[18,8,128]{2,1,0:T(8,128)S(1)} all-gather(f32[9,8,128]{2,1,0:T(8,128)S(1)} %collective-permute-done), channel_id=2, replica_groups=mesh['comp'=2,'gx'=24,'gy'=16] {'comp'}, dimensions={0}, use_global_device_ids=true | all-gather | bytes 110592 | tf_op jit(solution)/shard_map/all_gather | solution.py:523
  23.3 3.5 %collective-permute-start.2 = (f32[9,8,128]{2,1,0:T(8,128)S(1)}, f32[9,8,128]{2,1,0:T(8,128)S(1)}, u32[]{:S(2)}, u32[]{:S(2)}) collective-permute-start(f32[9,8,128]{2,1,0:T(8,128)S(1)} %shard_map.56.side_ref), channel_id=1, source_target_pairs={{0,16},{1,17},{2,18},{3,19},{4,20},{5,21},{6,22},{7,23},{8,24},{9,... | collective-permute-start | bytes 110600 | tf_op jit(solution)/shard_map/ppermute | solution.py:525
  26.8 4.8 %collective-permute-start.4 = (f32[9,8,128]{2,1,0:T(8,128)S(1)}, f32[9,8,128]{2,1,0:T(8,128)S(1)}, u32[]{:S(2)}, u32[]{:S(2)}) collective-permute-start(f32[9,8,128]{2,1,0:T(8,128)S(1)} %shard_map.56.side_ref), channel_id=1, source_target_pairs={{0,32},{1,33},{2,34},{3,35},{4,36},{5,37},{6,38},{7,39},{8,40},{9,... | collective-permute-start | bytes 110600 | tf_op jit(solution)/shard_map/ppermute | solution.py:526
  31.6 0.0 copy-start.2
  31.6 0.0 copy-start.3
  31.6 0.6 %copy-done.2 = f32[8]{0:T(128)S(1)} copy-done((f32[8]{0:T(128)S(1)}, f32[8]{0:T(128)}, u32[]{:S(2)}) %copy-start.2) | copy-done | bytes 56
  32.3 0.0 copy-done.3
  32.3 0.0 collective-permute-done.2
  32.3 1.5 %collective-permute-done.4 = f32[9,8,128]{2,1,0:T(8,128)S(1)} collective-permute-done((f32[9,8,128]{2,1,0:T(8,128)S(1)}, f32[9,8,128]{2,1,0:T(8,128)S(1)}, u32[]{:S(2)}, u32[]{:S(2)}) %collective-permute-start.4) | collective-permute-done | bytes 36896 | tf_op jit(solution)/shard_map/ppermute | solution.py:526
  33.8 0.0 collective-permute-done.3
  33.8 0.0 collective-permute-done.1.refs_0_
  33.9 5.8 %all-gather.1 = f32[1728,128]{1,0:T(8,128)S(1)} all-gather(f32[864,128]{1,0:T(8,128)S(1)} %shard_map.57), channel_id=3, replica_groups=mesh['comp'=2,'gx'=24,'gy'=16] {'comp'}, dimensions={0}, use_global_device_ids=true | all-gather | bytes 1327104 | tf_op jit(solution)/shard_map/all_gather | solution.py:529
  39.6 0.1 broadcast_in_dim.2.rates_ref
  39.7 5.1 %shard_map.58 = f32[8,32,128]{2,1,0:T(8,128)} custom-call(s32[1]{0:T(128)} %bitcast.comp_ref, f32[2,8,128]{2,1,0:T(8,128)S(1)} %broadcast_in_dim.2.rates_ref, f32[2,8,32,128]{3,2,1,0:T(8,128)S(1)} %all_gather.15.own_ref, f32[9,8,128]{2,1,0:T(8,128)S(1)} %shard_map.56.side_ref, f32[2,864,128]{2,1,0:T(8,128)S(1)} %bitcast.11), custom_call_target="tpu_custom_call" | custom-call | flops 20000000 | bytes 1323008 | tf_op jit(solution)/shard_map/pallas_call | solution.py:463
  (3 shorter events, 0.0 us)
Async XLA Ops:
  2.2 31.6 %collective-permute-start.1 = (f32[512,128]{1,0:T(8,128)S(1)}, f32[512,128]{1,0:T(8,128)S(1)}, u32[]{:S(2)}, u32[]{:S(2)}) collective-permute-start(f32[512,128]{1,0:T(8,128)S(1)} %bitcast.12), channel_id=1, source_target_pairs={{0,16},{1,17},{2,18},{3,19},{4,20},{5,21},{6,22},{7,23},{8,24},{9,... | collective-permute-start | bytes 786440 | tf_op jit(solution)/shard_map/ppermute | solution.py:516
  12.3 0.7 %copy-start.1 = (s32[4,128]{1,0:T(4,128)S(1)}, s32[4,128]{1,0:T(4,128)}, u32[]{:S(2)}) copy-start(s32[4,128]{1,0:T(4,128)} %depth_ref.3) | copy-start | bytes 6148
  12.3 0.7 %copy-start = (s32[4,128]{1,0:T(4,128)S(1)}, s32[4,128]{1,0:T(4,128)}, u32[]{:S(2)}) copy-start(s32[4,128]{1,0:T(4,128)} %land_ref.3) | copy-start | bytes 6148
  13.2 8.3 %collective-permute-start = (f32[9,8,128]{2,1,0:T(8,128)S(1)}, f32[9,8,128]{2,1,0:T(8,128)S(1)}, u32[]{:S(2)}, u32[]{:S(2)}) collective-permute-start(f32[9,8,128]{2,1,0:T(8,128)S(1)} %get-tuple-element.7), channel_id=1, source_target_pairs={{1,0},{2,1},{3,2},{4,3},{5,4},{6,5},{7,6},{8,7},{9,8},{10,9},{11,1... | collective-permute-start | bytes 110600 | tf_op jit(solution)/shard_map/ppermute | solution.py:520
  16.9 16.9 %collective-permute-start.3 = (f32[26,8,128]{2,1,0:T(8,128)S(1)}, f32[26,8,128]{2,1,0:T(8,128)S(1)}, u32[]{:S(2)}, u32[]{:S(2)}) collective-permute-start(f32[26,8,128]{2,1,0:T(8,128)S(1)} %get-tuple-element.8), channel_id=1, source_target_pairs={{0,32},{1,33},{2,34},{3,35},{4,36},{5,37},{6,38},{7,39},{8,40},{9,... | collective-permute-start | bytes 319496 | tf_op jit(solution)/shard_map/ppermute | solution.py:521
  23.3 9.0 %collective-permute-start.2 = (f32[9,8,128]{2,1,0:T(8,128)S(1)}, f32[9,8,128]{2,1,0:T(8,128)S(1)}, u32[]{:S(2)}, u32[]{:S(2)}) collective-permute-start(f32[9,8,128]{2,1,0:T(8,128)S(1)} %shard_map.56.side_ref), channel_id=1, source_target_pairs={{0,16},{1,17},{2,18},{3,19},{4,20},{5,21},{6,22},{7,23},{8,24},{9,... | collective-permute-start | bytes 110600 | tf_op jit(solution)/shard_map/ppermute | solution.py:525
  26.8 7.0 %collective-permute-start.4 = (f32[9,8,128]{2,1,0:T(8,128)S(1)}, f32[9,8,128]{2,1,0:T(8,128)S(1)}, u32[]{:S(2)}, u32[]{:S(2)}) collective-permute-start(f32[9,8,128]{2,1,0:T(8,128)S(1)} %shard_map.56.side_ref), channel_id=1, source_target_pairs={{0,32},{1,33},{2,34},{3,35},{4,36},{5,37},{6,38},{7,39},{8,40},{9,... | collective-permute-start | bytes 110600 | tf_op jit(solution)/shard_map/ppermute | solution.py:526
  31.6 0.7 %copy-start.2 = (f32[8]{0:T(128)S(1)}, f32[8]{0:T(128)}, u32[]{:S(2)}) copy-start(f32[8]{0:T(128)} %param.9) | copy-start | bytes 100
  31.6 0.7 %copy-start.3 = (f32[8]{0:T(128)S(1)}, f32[8]{0:T(128)}, u32[]{:S(2)}) copy-start(f32[8]{0:T(128)} %param.8) | copy-start | bytes 100

commit v6 on v5

--- a/solution.py
+++ b/solution.py
@@ -74,7 +74,7 @@
     for f in range(PROG):
         for r in range(ROWS):
             far_ref[f * ROWS + r] = row_of(own_ref, 0, f, r)
-    first = jnp.where(comp == 0, 2, 0)
+    first = jnp.where(comp == 0, 0, 2)
     for k in range(2):
         for f in range(PROG):
             far_ref[FAR_G + f * 2 + k] = row_of(own_ref, 0, PROG + f, first + k)
@@ -123,9 +123,10 @@
 
 def far_block(in_ref, way):
     first = 2 if way == 0 else 0
+    core = 1 - way
 
     def tile(index):
-        return in_ref[way, (IN_FAR + index) * LEVELS : (IN_FAR + index + 1) * LEVELS, :]
+        return in_ref[core, (IN_FAR + index) * LEVELS : (IN_FAR + index + 1) * LEVELS, :]
 
     def main(c, f, r):
         if c == 1:
@@ -136,7 +137,7 @@
     return Block(
         main,
         lambda c, r: tile(FAR + c * ROWS + r),
-        lambda row: in_ref[way, at + row : at + row + 1, :],
+        lambda row: in_ref[core, at + row : at + row + 1, :],
         range(first, first + 2),
     )
 
@@ -518,12 +519,12 @@
         pack_columns, [comp], [own, land_sea, depth_levels], [(SIDE,) + TILE, (FAR,) + TILE]
     )
     columns = lax.ppermute(columns, axes, neighbours(gx, gy, 0, -1))
-    far_in = lax.ppermute(far, axes, neighbours(gx, gy, 2, 0))
+    far_in = lax.ppermute(far, axes, neighbours(gx, gy, -2, 0))
     rates = jnp.broadcast_to(jnp.stack([growth, decay])[:, :, None], (2, FIELDS, LANES))
     columns = lax.all_gather(columns, "comp")
     (side,) = call(pack_corners, [], [land_sea, depth_levels, columns], [(SIDE,) + TILE])
     side_in = lax.ppermute(side, axes, neighbours(gx, gy, 1, 0))
-    far_side_in = lax.ppermute(side, axes, neighbours(gx, gy, 2, 0))
+    far_side_in = lax.ppermute(side, axes, neighbours(gx, gy, -2, 0))
     parts = [a.reshape(-1, LANES) for a in (near_in, side_in, far_in, far_side_in)]
     (received,) = call(join, [], parts, [(IN * LEVELS, LANES)])
     received = lax.all_gather(received, "comp")

time: 45.1 us -> 49.4 us (1.095)
  the two profiles are of different devices: /device:TPU:184 before, /device:TPU:62 now
where the time goes in v6:
time: 49.4 us; the launch traced here: 49.1 us
  starting transfers between devices  22.1 us (45%)
  waiting for transfers between devices  13.8 us (28%)
  blocking collectives  6.48 us (13%)
  Pallas kernels  5.25 us (11%)
  local copies, waits for them, and re-layouts  1.41 us (3%)
    ppermute x1, waiting for transfers between devices, local(): far_side_in = lax.ppermute(side, axes, neighbours(gx, gy, -2, 0))  10.5 us
    ppermute x1, starting transfers between devices, local(): lax.ppermute(own.reshape(MAIN * LEVELS, LANES), axes, neighbours(gx, gy,...  10.1 us
    ppermute x1, starting transfers between devices, local(): side_in = lax.ppermute(side, axes, neighbours(gx, gy, 1, 0))  5.41 us
    pallas_call x4, Pallas kernels, call(): pl.pallas_call(kernel, out_shape=out_shape, in_specs=[pl.BlockSpec(memory...  5.25 us
    ppermute x1, waiting for transfers between devices, local(): columns = lax.ppermute(columns, axes, neighbours(gx, gy, 0, -1))  3.29 us
    ppermute x1, starting transfers between devices, local(): columns = lax.ppermute(columns, axes, neighbours(gx, gy, 0, -1))  2.74 us
    all_gather x1, blocking collectives, local(): received = lax.all_gather(received, 'comp')  2.44 us
    all_gather x1, blocking collectives, local(): own = lax.all_gather(fields, 'comp')  2.19 us
  transfers between devices with their start and end apart: 5, of which 2 were waited for; matrix products, arithmetic and copies ran while one was open for 0% of the time, Pallas kernels for 0%

profile of v6, /device:TPU:62, one launch (start us, length us, event | category | flops | bytes accessed | tf_op | source)
XLA Modules:
  0.0 49.1 jit_solution(4237862422586949968)
XLA Ops:
  0.0 2.2 %all_gather.15.own_ref = f32[2,8,32,128]{3,2,1,0:T(8,128)S(1)} all-gather(f32[1,8,32,128]{3,2,1,0:T(8,128)} %bitcast.17), channel_id=1, replica_groups=mesh['comp'=2,'gx'=24,'gy'=16] {'comp'}, dimensions={0}, use_global_device_ids=true | all-gather | bytes 393216 | tf_op jit(solution)/shard_map/all_gather | solution.py:516
  2.2 10.1 %collective-permute-start.1 = (f32[512,128]{1,0:T(8,128)S(1)}, f32[512,128]{1,0:T(8,128)S(1)}, u32[]{:S(2)}, u32[]{:S(2)}) collective-permute-start(f32[512,128]{1,0:T(8,128)S(1)} %bitcast.12), channel_id=1, source_target_pairs={{0,16},{1,17},{2,18},{3,19},{4,20},{5,21},{6,22},{7,23},{8,24},{9,... | collective-permute-start | bytes 786440 | tf_op jit(solution)/shard_map/ppermute | solution.py:517
  12.3 0.0 copy-start.1
  12.3 0.0 copy-start
  12.3 0.7 %copy-done.1 = s32[4,128]{1,0:T(4,128)S(1)} copy-done((s32[4,128]{1,0:T(4,128)S(1)}, s32[4,128]{1,0:T(4,128)}, u32[]{:S(2)}) %copy-start.1) | copy-done | bytes 2072
  13.0 0.0 copy-done
  13.0 0.1 shard_map.55
  13.2 2.7 %collective-permute-start = (f32[9,8,128]{2,1,0:T(8,128)S(1)}, f32[9,8,128]{2,1,0:T(8,128)S(1)}, u32[]{:S(2)}, u32[]{:S(2)}) collective-permute-start(f32[9,8,128]{2,1,0:T(8,128)S(1)} %get-tuple-element.7), channel_id=1, source_target_pairs={{1,0},{2,1},{3,2},{4,3},{5,4},{6,5},{7,6},{8,7},{9,8},{10,9},{11,1... | collective-permute-start | bytes 110600 | tf_op jit(solution)/shard_map/ppermute | solution.py:521
  15.9 1.9 %collective-permute-start.3 = (f32[26,8,128]{2,1,0:T(8,128)S(1)}, f32[26,8,128]{2,1,0:T(8,128)S(1)}, u32[]{:S(2)}, u32[]{:S(2)}) collective-permute-start(f32[26,8,128]{2,1,0:T(8,128)S(1)} %get-tuple-element.8), channel_id=1, source_target_pairs={{32,0},{33,1},{34,2},{35,3},{36,4},{37,5},{38,6},{39,7},{40,8},{41... | collective-permute-start | bytes 319496 | tf_op jit(solution)/shard_map/ppermute | solution.py:522
  17.8 3.3 %collective-permute-done = f32[9,8,128]{2,1,0:T(8,128)S(1)} collective-permute-done((f32[9,8,128]{2,1,0:T(8,128)S(1)}, f32[9,8,128]{2,1,0:T(8,128)S(1)}, u32[]{:S(2)}, u32[]{:S(2)}) %collective-permute-start) | collective-permute-done | bytes 36896 | tf_op jit(solution)/shard_map/ppermute | solution.py:521
  21.1 1.8 %all-gather = f32[18,8,128]{2,1,0:T(8,128)S(1)} all-gather(f32[9,8,128]{2,1,0:T(8,128)S(1)} %collective-permute-done), channel_id=2, replica_groups=mesh['comp'=2,'gx'=24,'gy'=16] {'comp'}, dimensions={0}, use_global_device_ids=true | all-gather | bytes 110592 | tf_op jit(solution)/shard_map/all_gather | solution.py:524
  23.0 5.4 %collective-permute-start.2 = (f32[9,8,128]{2,1,0:T(8,128)S(1)}, f32[9,8,128]{2,1,0:T(8,128)S(1)}, u32[]{:S(2)}, u32[]{:S(2)}) collective-permute-start(f32[9,8,128]{2,1,0:T(8,128)S(1)} %shard_map.56.side_ref), channel_id=1, source_target_pairs={{0,16},{1,17},{2,18},{3,19},{4,20},{5,21},{6,22},{7,23},{8,24},{9,... | collective-permute-start | bytes 110600 | tf_op jit(solution)/shard_map/ppermute | solution.py:526
  28.4 1.9 %collective-permute-start.4 = (f32[9,8,128]{2,1,0:T(8,128)S(1)}, f32[9,8,128]{2,1,0:T(8,128)S(1)}, u32[]{:S(2)}, u32[]{:S(2)}) collective-permute-start(f32[9,8,128]{2,1,0:T(8,128)S(1)} %shard_map.56.side_ref), channel_id=1, source_target_pairs={{32,0},{33,1},{34,2},{35,3},{36,4},{37,5},{38,6},{39,7},{40,8},{41... | collective-permute-start | bytes 110600 | tf_op jit(solution)/shard_map/ppermute | solution.py:527
  30.3 0.0 copy-start.2
  30.3 0.0 copy-start.3
  30.4 0.6 %copy-done.2 = f32[8]{0:T(128)S(1)} copy-done((f32[8]{0:T(128)S(1)}, f32[8]{0:T(128)}, u32[]{:S(2)}) %copy-start.2) | copy-done | bytes 56
  31.0 0.0 copy-done.3
  31.0 0.0 collective-permute-done.2
  31.0 10.5 %collective-permute-done.4 = f32[9,8,128]{2,1,0:T(8,128)S(1)} collective-permute-done((f32[9,8,128]{2,1,0:T(8,128)S(1)}, f32[9,8,128]{2,1,0:T(8,128)S(1)}, u32[]{:S(2)}, u32[]{:S(2)}) %collective-permute-start.4) | collective-permute-done | bytes 36896 | tf_op jit(solution)/shard_map/ppermute | solution.py:527
  41.5 0.0 collective-permute-done.3
  41.5 0.0 collective-permute-done.1.refs_0_
  41.5 2.4 %all-gather.1 = f32[1728,128]{1,0:T(8,128)S(1)} all-gather(f32[864,128]{1,0:T(8,128)S(1)} %shard_map.57), channel_id=3, replica_groups=mesh['comp'=2,'gx'=24,'gy'=16] {'comp'}, dimensions={0}, use_global_device_ids=true | all-gather | bytes 1327104 | tf_op jit(solution)/shard_map/all_gather | solution.py:530
  44.0 0.1 broadcast_in_dim.2.rates_ref
  44.0 5.1 %shard_map.58 = f32[8,32,128]{2,1,0:T(8,128)} custom-call(s32[1]{0:T(128)} %bitcast.comp_ref, f32[2,8,128]{2,1,0:T(8,128)S(1)} %broadcast_in_dim.2.rates_ref, f32[2,8,32,128]{3,2,1,0:T(8,128)S(1)} %all_gather.15.own_ref, f32[9,8,128]{2,1,0:T(8,128)S(1)} %shard_map.56.side_ref, f32[2,864,128]{2,1,0:T(8,128)S(1)} %bitcast.11), custom_call_target="tpu_custom_call" | custom-call | flops 20000000 | bytes 1323008 | tf_op jit(solution)/shard_map/pallas_call | solution.py:464
  (3 shorter events, 0.0 us)
Async XLA Ops:
  2.2 39.3 %collective-permute-start.1 = (f32[512,128]{1,0:T(8,128)S(1)}, f32[512,128]{1,0:T(8,128)S(1)}, u32[]{:S(2)}, u32[]{:S(2)}) collective-permute-start(f32[512,128]{1,0:T(8,128)S(1)} %bitcast.12), channel_id=1, source_target_pairs={{0,16},{1,17},{2,18},{3,19},{4,20},{5,21},{6,22},{7,23},{8,24},{9,... | collective-permute-start | bytes 786440 | tf_op jit(solution)/shard_map/ppermute | solution.py:517
  12.3 0.7 %copy-start.1 = (s32[4,128]{1,0:T(4,128)S(1)}, s32[4,128]{1,0:T(4,128)}, u32[]{:S(2)}) copy-start(s32[4,128]{1,0:T(4,128)} %depth_ref.3) | copy-start | bytes 6148
  12.3 0.7 %copy-start = (s32[4,128]{1,0:T(4,128)S(1)}, s32[4,128]{1,0:T(4,128)}, u32[]{:S(2)}) copy-start(s32[4,128]{1,0:T(4,128)} %land_ref.3) | copy-start | bytes 6148
  13.2 8.0 %collective-permute-start = (f32[9,8,128]{2,1,0:T(8,128)S(1)}, f32[9,8,128]{2,1,0:T(8,128)S(1)}, u32[]{:S(2)}, u32[]{:S(2)}) collective-permute-start(f32[9,8,128]{2,1,0:T(8,128)S(1)} %get-tuple-element.7), channel_id=1, source_target_pairs={{1,0},{2,1},{3,2},{4,3},{5,4},{6,5},{7,6},{8,7},{9,8},{10,9},{11,1... | collective-permute-start | bytes 110600 | tf_op jit(solution)/shard_map/ppermute | solution.py:521
  15.9 25.6 %collective-permute-start.3 = (f32[26,8,128]{2,1,0:T(8,128)S(1)}, f32[26,8,128]{2,1,0:T(8,128)S(1)}, u32[]{:S(2)}, u32[]{:S(2)}) collective-permute-start(f32[26,8,128]{2,1,0:T(8,128)S(1)} %get-tuple-element.8), channel_id=1, source_target_pairs={{32,0},{33,1},{34,2},{35,3},{36,4},{37,5},{38,6},{39,7},{40,8},{41... | collective-permute-start | bytes 319496 | tf_op jit(solution)/shard_map/ppermute | solution.py:522
  23.0 8.0 %collective-permute-start.2 = (f32[9,8,128]{2,1,0:T(8,128)S(1)}, f32[9,8,128]{2,1,0:T(8,128)S(1)}, u32[]{:S(2)}, u32[]{:S(2)}) collective-permute-start(f32[9,8,128]{2,1,0:T(8,128)S(1)} %shard_map.56.side_ref), channel_id=1, source_target_pairs={{0,16},{1,17},{2,18},{3,19},{4,20},{5,21},{6,22},{7,23},{8,24},{9,... | collective-permute-start | bytes 110600 | tf_op jit(solution)/shard_map/ppermute | solution.py:526
  28.4 13.1 %collective-permute-start.4 = (f32[9,8,128]{2,1,0:T(8,128)S(1)}, f32[9,8,128]{2,1,0:T(8,128)S(1)}, u32[]{:S(2)}, u32[]{:S(2)}) collective-permute-start(f32[9,8,128]{2,1,0:T(8,128)S(1)} %shard_map.56.side_ref), channel_id=1, source_target_pairs={{32,0},{33,1},{34,2},{35,3},{36,4},{37,5},{38,6},{39,7},{40,8},{41... | collective-permute-start | bytes 110600 | tf_op jit(solution)/shard_map/ppermute | solution.py:527
  30.3 0.7 %copy-start.2 = (f32[8]{0:T(128)S(1)}, f32[8]{0:T(128)}, u32[]{:S(2)}) copy-start(f32[8]{0:T(128)} %param.9) | copy-start | bytes 100
  30.3 0.7 %copy-start.3 = (f32[8]{0:T(128)S(1)}, f32[8]{0:T(128)}, u32[]{:S(2)}) copy-start(f32[8]{0:T(128)} %param.8) | copy-start | bytes 100

commit v7 on v5

--- a/solution.py
+++ b/solution.py
@@ -27,7 +27,8 @@
 IN_SIDE = MAIN
 IN_FAR = IN_SIDE + SIDE
 IN_FAR_SIDE = IN_FAR + FAR
-IN = IN_FAR_SIDE + SIDE
+FAR_SIDE = 2
+IN = IN_FAR_SIDE + FAR_SIDE
 DYN_ROWS = 5 * ROWS
 TRC_ROWS = 3 * ROWS
 TILE = (LEVELS, LANES)
@@ -81,11 +82,17 @@
         far_ref[FAR_CHL + k] = row_of(own_ref, 1, 0, first + k)
 
 
-def pack_corners(land_ref, depth_ref, columns_ref, side_ref):
+def pack_corners(comp_ref, land_ref, depth_ref, columns_ref, side_ref, far_ref):
     for t in range(EDGE):
         side_ref[t] = columns_ref[0, t] + columns_ref[1, t]
-    side_ref[EDGE, 0:ROWS, :] = wet_count(land_ref, depth_ref)
-    side_ref[EDGE, ROWS : 2 * ROWS, :] = columns_ref[0, EDGE, 0:ROWS, :] + columns_ref[1, EDGE, 0:ROWS, :]
+    first = jnp.where(comp_ref[0] == 0, 2, 0)
+    near, far = [columns_ref[0, first + k] + columns_ref[1, first + k] for k in range(2)]
+    far_ref[0] = jnp.where(lanes() < LANES // 2, near, pltpu.roll(far, LANES // 2, 1))
+    count = wet_count(land_ref, depth_ref)
+    outer = columns_ref[0, EDGE, 0:ROWS, :] + columns_ref[1, EDGE, 0:ROWS, :]
+    for ref, at in ((side_ref, EDGE), (far_ref, 1)):
+        ref[at, 0:ROWS, :] = count
+        ref[at, ROWS : 2 * ROWS, :] = outer
 
 
 def join(*refs):
@@ -132,10 +139,15 @@
             return tile(FAR_CHL + r - first)
         return tile(f * ROWS + r if f < PROG else FAR_G + (f - PROG) * 2 + r - first)
 
-    at = (IN_FAR_SIDE + EDGE) * LEVELS
+    def edge(c, r):
+        if c == 1 or r - first not in (0, 1):
+            return jnp.zeros(TILE, jnp.float32)
+        return tile(FAR) if r == first else pltpu.roll(tile(FAR), LANES // 2, 1)
+
+    at = (IN_FAR_SIDE + 1) * LEVELS
     return Block(
         main,
-        lambda c, r: tile(FAR + c * ROWS + r),
+        edge,
         lambda row: in_ref[way, at + row : at + row + 1, :],
         range(first, first + 2),
     )
@@ -521,9 +533,11 @@
     far_in = lax.ppermute(far, axes, neighbours(gx, gy, 2, 0))
     rates = jnp.broadcast_to(jnp.stack([growth, decay])[:, :, None], (2, FIELDS, LANES))
     columns = lax.all_gather(columns, "comp")
-    (side,) = call(pack_corners, [], [land_sea, depth_levels, columns], [(SIDE,) + TILE])
+    side, far_side = call(
+        pack_corners, [comp], [land_sea, depth_levels, columns], [(SIDE,) + TILE, (FAR_SIDE,) + TILE]
+    )
     side_in = lax.ppermute(side, axes, neighbours(gx, gy, 1, 0))
-    far_side_in = lax.ppermute(side, axes, neighbours(gx, gy, 2, 0))
+    far_side_in = lax.ppermute(far_side, axes, neighbours(gx, gy, 2, 0))
     parts = [a.reshape(-1, LANES) for a in (near_in, side_in, far_in, far_side_in)]
     (received,) = call(join, [], parts, [(IN * LEVELS, LANES)])
     received = lax.all_gather(received, "comp")

time: 45.1 us -> 44.5 us (0.987)
  waiting for transfers between devices: 1.54 us -> 0.95 us
    ppermute x1, waiting for transfers between devices: 1.53 us -> 0.94 us  [local(): far_side_in = lax.ppermute(far_side, axes, neighbours(gx, gy, 2, 0))]
where the time goes in v7:
time: 44.5 us; the launch traced here: 44.2 us
  starting transfers between devices  26.6 us (60%)
  blocking collectives  9.75 us (22%)
  Pallas kernels  5.32 us (12%)
  local copies, waits for them, and re-layouts  1.41 us (3%)
  waiting for transfers between devices  0.95 us (2%)
    ppermute x1, starting transfers between devices, local(): lax.ppermute(own.reshape(MAIN * LEVELS, LANES), axes, neighbours(gx, gy,...  10.1 us
    all_gather x1, blocking collectives, local(): received = lax.all_gather(received, 'comp')  5.7 us
    pallas_call x4, Pallas kernels, call(): pl.pallas_call(kernel, out_shape=out_shape, in_specs=[pl.BlockSpec(memory...  5.32 us
    ppermute x1, starting transfers between devices, local(): far_side_in = lax.ppermute(far_side, axes, neighbours(gx, gy, 2, 0))  4.81 us
    ppermute x1, starting transfers between devices, local(): far_in = lax.ppermute(far, axes, neighbours(gx, gy, 2, 0))  4.5 us
    ppermute x1, starting transfers between devices, local(): columns = lax.ppermute(columns, axes, neighbours(gx, gy, 0, -1))  3.76 us
    ppermute x1, starting transfers between devices, local(): side_in = lax.ppermute(side, axes, neighbours(gx, gy, 1, 0))  3.47 us
    all_gather x1, blocking collectives, local(): own = lax.all_gather(fields, 'comp')  2.19 us
  transfers between devices with their start and end apart: 5, of which 1 were waited for; matrix products, arithmetic and copies ran while one was open for 0% of the time, Pallas kernels for 0%

profile of v7, /device:TPU:184, one launch (start us, length us, event | category | flops | bytes accessed | tf_op | source)
XLA Modules:
  0.0 44.2 jit_solution(2063385084358234953)
XLA Ops:
  0.0 2.2 %all_gather.15.own_ref = f32[2,8,32,128]{3,2,1,0:T(8,128)S(1)} all-gather(f32[1,8,32,128]{3,2,1,0:T(8,128)} %bitcast.17), channel_id=1, replica_groups=mesh['comp'=2,'gx'=24,'gy'=16] {'comp'}, dimensions={0}, use_global_device_ids=true | all-gather | bytes 393216 | tf_op jit(solution)/shard_map/all_gather | solution.py:527
  2.2 10.1 %collective-permute-start.1 = (f32[512,128]{1,0:T(8,128)S(1)}, f32[512,128]{1,0:T(8,128)S(1)}, u32[]{:S(2)}, u32[]{:S(2)}) collective-permute-start(f32[512,128]{1,0:T(8,128)S(1)} %bitcast.12), channel_id=1, source_target_pairs={{0,16},{1,17},{2,18},{3,19},{4,20},{5,21},{6,22},{7,23},{8,24},{9,... | collective-permute-start | bytes 786440 | tf_op jit(solution)/shard_map/ppermute | solution.py:528
  12.3 0.0 copy-start.1
  12.3 0.0 copy-start
  12.3 0.7 %copy-done.1 = s32[4,128]{1,0:T(4,128)S(1)} copy-done((s32[4,128]{1,0:T(4,128)S(1)}, s32[4,128]{1,0:T(4,128)}, u32[]{:S(2)}) %copy-start.1) | copy-done | bytes 2072
  13.0 0.0 copy-done
  13.0 0.1 shard_map.55
  13.2 3.8 %collective-permute-start = (f32[9,8,128]{2,1,0:T(8,128)S(1)}, f32[9,8,128]{2,1,0:T(8,128)S(1)}, u32[]{:S(2)}, u32[]{:S(2)}) collective-permute-start(f32[9,8,128]{2,1,0:T(8,128)S(1)} %get-tuple-element.9), channel_id=1, source_target_pairs={{1,0},{2,1},{3,2},{4,3},{5,4},{6,5},{7,6},{8,7},{9,8},{10,9},{11,1... | collective-permute-start | bytes 110600 | tf_op jit(solution)/shard_map/ppermute | solution.py:532
  16.9 4.5 %collective-permute-start.3 = (f32[26,8,128]{2,1,0:T(8,128)S(1)}, f32[26,8,128]{2,1,0:T(8,128)S(1)}, u32[]{:S(2)}, u32[]{:S(2)}) collective-permute-start(f32[26,8,128]{2,1,0:T(8,128)S(1)} %get-tuple-element.11), channel_id=1, source_target_pairs={{0,32},{1,33},{2,34},{3,35},{4,36},{5,37},{6,38},{7,39},{8,40},{9,... | collective-permute-start | bytes 319496 | tf_op jit(solution)/shard_map/ppermute | solution.py:533
  21.4 0.0 collective-permute-done
  21.4 1.9 %all-gather = f32[18,8,128]{2,1,0:T(8,128)S(1)} all-gather(f32[9,8,128]{2,1,0:T(8,128)S(1)} %collective-permute-done), channel_id=2, replica_groups=mesh['comp'=2,'gx'=24,'gy'=16] {'comp'}, dimensions={0}, use_global_device_ids=true | all-gather | bytes 110592 | tf_op jit(solution)/shard_map/all_gather | solution.py:535
  23.3 0.1 shard_map.56
  23.4 3.5 %collective-permute-start.2 = (f32[9,8,128]{2,1,0:T(8,128)S(1)}, f32[9,8,128]{2,1,0:T(8,128)S(1)}, u32[]{:S(2)}, u32[]{:S(2)}) collective-permute-start(f32[9,8,128]{2,1,0:T(8,128)S(1)} %get-tuple-element.10.side_ref), channel_id=1, source_target_pairs={{0,16},{1,17},{2,18},{3,19},{4,20},{5,21},{6,22},{7,23},{8,24},{9,... | collective-permute-start | bytes 110600 | tf_op jit(solution)/shard_map/ppermute | solution.py:539
  26.9 4.8 %collective-permute-start.4 = (f32[2,8,128]{2,1,0:T(8,128)S(1)}, f32[2,8,128]{2,1,0:T(8,128)S(1)}, u32[]{:S(2)}, u32[]{:S(2)}) collective-permute-start(f32[2,8,128]{2,1,0:T(8,128)S(1)} %get-tuple-element.12), channel_id=1, source_target_pairs={{0,32},{1,33},{2,34},{3,35},{4,36},{5,37},{6,38},{7,39},{8,40},{9,... | collective-permute-start | bytes 24584 | tf_op jit(solution)/shard_map/ppermute | solution.py:540
  31.7 0.0 copy-start.2
  31.7 0.0 copy-start.3
  31.7 0.6 %copy-done.2 = f32[8]{0:T(128)S(1)} copy-done((f32[8]{0:T(128)S(1)}, f32[8]{0:T(128)}, u32[]{:S(2)}) %copy-start.2) | copy-done | bytes 56
  32.3 0.0 copy-done.3
  32.4 0.9 %collective-permute-done.4 = f32[2,8,128]{2,1,0:T(8,128)S(1)} collective-permute-done((f32[2,8,128]{2,1,0:T(8,128)S(1)}, f32[2,8,128]{2,1,0:T(8,128)S(1)}, u32[]{:S(2)}, u32[]{:S(2)}) %collective-permute-start.4) | collective-permute-done | bytes 8224 | tf_op jit(solution)/shard_map/ppermute | solution.py:540
  33.3 0.0 collective-permute-done.2
  33.3 0.0 collective-permute-done.3
  33.3 0.0 collective-permute-done.1.refs_0_
  33.4 5.7 %all-gather.1 = f32[1616,128]{1,0:T(8,128)S(1)} all-gather(f32[808,128]{1,0:T(8,128)S(1)} %shard_map.57), channel_id=3, replica_groups=mesh['comp'=2,'gx'=24,'gy'=16] {'comp'}, dimensions={0}, use_global_device_ids=true | all-gather | bytes 1241088 | tf_op jit(solution)/shard_map/all_gather | solution.py:543
  39.0 0.1 broadcast_in_dim.2.rates_ref
  39.1 5.1 %shard_map.58 = f32[8,32,128]{2,1,0:T(8,128)} custom-call(s32[1]{0:T(128)} %bitcast.comp_ref, f32[2,8,128]{2,1,0:T(8,128)S(1)} %broadcast_in_dim.2.rates_ref, f32[2,8,32,128]{3,2,1,0:T(8,128)S(1)} %all_gather.15.own_ref, f32[9,8,128]{2,1,0:T(8,128)S(1)} %get-tuple-element.10.side_ref, f32[2,808,128]{2,1,0:T(8,128)S(1)} %bitcast.11), custom_call_target="tpu_custom_call" | custom-call | flops 20000000 | bytes 1265664 | tf_op jit(solution)/shard_map/pallas_call | solution.py:475
  (2 shorter events, 0.0 us)
Async XLA Ops:
  2.2 31.1 %collective-permute-start.1 = (f32[512,128]{1,0:T(8,128)S(1)}, f32[512,128]{1,0:T(8,128)S(1)}, u32[]{:S(2)}, u32[]{:S(2)}) collective-permute-start(f32[512,128]{1,0:T(8,128)S(1)} %bitcast.12), channel_id=1, source_target_pairs={{0,16},{1,17},{2,18},{3,19},{4,20},{5,21},{6,22},{7,23},{8,24},{9,... | collective-permute-start | bytes 786440 | tf_op jit(solution)/shard_map/ppermute | solution.py:528
  12.3 0.7 %copy-start.1 = (s32[4,128]{1,0:T(4,128)S(1)}, s32[4,128]{1,0:T(4,128)}, u32[]{:S(2)}) copy-start(s32[4,128]{1,0:T(4,128)} %depth_ref.3) | copy-start | bytes 6148
  12.3 0.7 %copy-start = (s32[4,128]{1,0:T(4,128)S(1)}, s32[4,128]{1,0:T(4,128)}, u32[]{:S(2)}) copy-start(s32[4,128]{1,0:T(4,128)} %land_ref.3) | copy-start | bytes 6148
  13.2 8.3 %collective-permute-start = (f32[9,8,128]{2,1,0:T(8,128)S(1)}, f32[9,8,128]{2,1,0:T(8,128)S(1)}, u32[]{:S(2)}, u32[]{:S(2)}) collective-permute-start(f32[9,8,128]{2,1,0:T(8,128)S(1)} %get-tuple-element.9), channel_id=1, source_target_pairs={{1,0},{2,1},{3,2},{4,3},{5,4},{6,5},{7,6},{8,7},{9,8},{10,9},{11,1... | collective-permute-start | bytes 110600 | tf_op jit(solution)/shard_map/ppermute | solution.py:532
  16.9 16.4 %collective-permute-start.3 = (f32[26,8,128]{2,1,0:T(8,128)S(1)}, f32[26,8,128]{2,1,0:T(8,128)S(1)}, u32[]{:S(2)}, u32[]{:S(2)}) collective-permute-start(f32[26,8,128]{2,1,0:T(8,128)S(1)} %get-tuple-element.11), channel_id=1, source_target_pairs={{0,32},{1,33},{2,34},{3,35},{4,36},{5,37},{6,38},{7,39},{8,40},{9,... | collective-permute-start | bytes 319496 | tf_op jit(solution)/shard_map/ppermute | solution.py:533
  23.4 9.9 %collective-permute-start.2 = (f32[9,8,128]{2,1,0:T(8,128)S(1)}, f32[9,8,128]{2,1,0:T(8,128)S(1)}, u32[]{:S(2)}, u32[]{:S(2)}) collective-permute-start(f32[9,8,128]{2,1,0:T(8,128)S(1)} %get-tuple-element.10.side_ref), channel_id=1, source_target_pairs={{0,16},{1,17},{2,18},{3,19},{4,20},{5,21},{6,22},{7,23},{8,24},{9,... | collective-permute-start | bytes 110600 | tf_op jit(solution)/shard_map/ppermute | solution.py:539
  26.9 6.4 %collective-permute-start.4 = (f32[2,8,128]{2,1,0:T(8,128)S(1)}, f32[2,8,128]{2,1,0:T(8,128)S(1)}, u32[]{:S(2)}, u32[]{:S(2)}) collective-permute-start(f32[2,8,128]{2,1,0:T(8,128)S(1)} %get-tuple-element.12), channel_id=1, source_target_pairs={{0,32},{1,33},{2,34},{3,35},{4,36},{5,37},{6,38},{7,39},{8,40},{9,... | collective-permute-start | bytes 24584 | tf_op jit(solution)/shard_map/ppermute | solution.py:540
  31.7 0.7 %copy-start.2 = (f32[8]{0:T(128)S(1)}, f32[8]{0:T(128)}, u32[]{:S(2)}) copy-start(f32[8]{0:T(128)} %param.9) | copy-start | bytes 100
  31.7 0.7 %copy-start.3 = (f32[8]{0:T(128)S(1)}, f32[8]{0:T(128)}, u32[]{:S(2)}) copy-start(f32[8]{0:T(128)} %param.8) | copy-start | bytes 100

commit v8 on v7

--- a/solution.py
+++ b/solution.py
@@ -32,6 +32,7 @@
 DYN_ROWS = 5 * ROWS
 TRC_ROWS = 3 * ROWS
 TILE = (LEVELS, LANES)
+HINT = 3_000_000_000
 DYN_UNROLL = 4
 TRC_UNROLL = 4
 
@@ -534,7 +535,8 @@
     rates = jnp.broadcast_to(jnp.stack([growth, decay])[:, :, None], (2, FIELDS, LANES))
     columns = lax.all_gather(columns, "comp")
     side, far_side = call(
-        pack_corners, [comp], [land_sea, depth_levels, columns], [(SIDE,) + TILE, (FAR_SIDE,) + TILE]
+        pack_corners, [comp], [land_sea, depth_levels, columns], [(SIDE,) + TILE, (FAR_SIDE,) + TILE],
+        flops=HINT,
     )
     side_in = lax.ppermute(side, axes, neighbours(gx, gy, 1, 0))
     far_side_in = lax.ppermute(far_side, axes, neighbours(gx, gy, 2, 0))

time: 44.5 us -> 46.5 us (1.045)
  the two profiles are of different devices: /device:TPU:184 before, /device:TPU:240 now
where the time goes in v8:
time: 46.5 us; the launch traced here: 46.2 us
  starting transfers between devices  26.7 us (57%)
  blocking collectives  12 us (26%)
  Pallas kernels  5.32 us (11%)
  local copies, waits for them, and re-layouts  1.42 us (3%)
  waiting for transfers between devices  0.67 us (1%)
    ppermute x1, starting transfers between devices, local(): far_in = lax.ppermute(far, axes, neighbours(gx, gy, 2, 0))  10.2 us
    all_gather x1, blocking collectives, local(): received = lax.all_gather(received, 'comp')  7.96 us
    ppermute x1, starting transfers between devices, local(): far_side_in = lax.ppermute(far_side, axes, neighbours(gx, gy, 2, 0))  5.71 us
    pallas_call x4, Pallas kernels, call(): pl.pallas_call(kernel, out_shape=out_shape, in_specs=[pl.BlockSpec(memory...  5.32 us
    ppermute x1, starting transfers between devices, local(): columns = lax.ppermute(columns, axes, neighbours(gx, gy, 0, -1))  3.76 us
    ppermute x1, starting transfers between devices, local(): lax.ppermute(own.reshape(MAIN * LEVELS, LANES), axes, neighbours(gx, gy,...  3.48 us
    ppermute x1, starting transfers between devices, local(): side_in = lax.ppermute(side, axes, neighbours(gx, gy, 1, 0))  3.47 us
    all_gather x1, blocking collectives, local(): own = lax.all_gather(fields, 'comp')  2.19 us
  transfers between devices with their start and end apart: 5, of which 1 were waited for; matrix products, arithmetic and copies ran while one was open for 0% of the time, Pallas kernels for 0%

profile of v8, /device:TPU:240, one launch (start us, length us, event | category | flops | bytes accessed | tf_op | source)
XLA Modules:
  0.0 46.2 jit_solution(1401384313572885551)
XLA Ops:
  0.0 2.2 %all_gather.15.own_ref = f32[2,8,32,128]{3,2,1,0:T(8,128)S(1)} all-gather(f32[1,8,32,128]{3,2,1,0:T(8,128)} %bitcast.17), channel_id=1, replica_groups=mesh['comp'=2,'gx'=24,'gy'=16] {'comp'}, dimensions={0}, use_global_device_ids=true | all-gather | bytes 393216 | tf_op jit(solution)/shard_map/all_gather | solution.py:528
  2.2 0.0 copy-start.1
  2.2 0.0 copy-start
  2.2 0.7 %copy-done.1 = s32[4,128]{1,0:T(4,128)S(1)} copy-done((s32[4,128]{1,0:T(4,128)S(1)}, s32[4,128]{1,0:T(4,128)}, u32[]{:S(2)}) %copy-start.1) | copy-done | bytes 2072
  2.9 0.0 copy-done
  2.9 0.1 shard_map.55
  3.0 3.8 %collective-permute-start = (f32[9,8,128]{2,1,0:T(8,128)S(1)}, f32[9,8,128]{2,1,0:T(8,128)S(1)}, u32[]{:S(2)}, u32[]{:S(2)}) collective-permute-start(f32[9,8,128]{2,1,0:T(8,128)S(1)} %get-tuple-element.9), channel_id=1, source_target_pairs={{1,0},{2,1},{3,2},{4,3},{5,4},{6,5},{7,6},{8,7},{9,8},{10,9},{11,1... | collective-permute-start | bytes 110600 | tf_op jit(solution)/shard_map/ppermute | solution.py:533
  6.8 10.2 %collective-permute-start.3 = (f32[26,8,128]{2,1,0:T(8,128)S(1)}, f32[26,8,128]{2,1,0:T(8,128)S(1)}, u32[]{:S(2)}, u32[]{:S(2)}) collective-permute-start(f32[26,8,128]{2,1,0:T(8,128)S(1)} %get-tuple-element.11), channel_id=1, source_target_pairs={{0,32},{1,33},{2,34},{3,35},{4,36},{5,37},{6,38},{7,39},{8,40},{9,... | collective-permute-start | bytes 319496 | tf_op jit(solution)/shard_map/ppermute | solution.py:534
  17.0 3.5 %collective-permute-start.1 = (f32[512,128]{1,0:T(8,128)S(1)}, f32[512,128]{1,0:T(8,128)S(1)}, u32[]{:S(2)}, u32[]{:S(2)}) collective-permute-start(f32[512,128]{1,0:T(8,128)S(1)} %bitcast.12), channel_id=1, source_target_pairs={{0,16},{1,17},{2,18},{3,19},{4,20},{5,21},{6,22},{7,23},{8,24},{9,... | collective-permute-start | bytes 786440 | tf_op jit(solution)/shard_map/ppermute | solution.py:529
  20.5 0.0 collective-permute-done
  20.5 1.9 %all-gather = f32[18,8,128]{2,1,0:T(8,128)S(1)} all-gather(f32[9,8,128]{2,1,0:T(8,128)S(1)} %collective-permute-done), channel_id=2, replica_groups=mesh['comp'=2,'gx'=24,'gy'=16] {'comp'}, dimensions={0}, use_global_device_ids=true | all-gather | bytes 110592 | tf_op jit(solution)/shard_map/all_gather | solution.py:536
  22.4 0.1 shard_map.56
  22.5 3.5 %collective-permute-start.2 = (f32[9,8,128]{2,1,0:T(8,128)S(1)}, f32[9,8,128]{2,1,0:T(8,128)S(1)}, u32[]{:S(2)}, u32[]{:S(2)}) collective-permute-start(f32[9,8,128]{2,1,0:T(8,128)S(1)} %get-tuple-element.10.side_ref), channel_id=1, source_target_pairs={{0,16},{1,17},{2,18},{3,19},{4,20},{5,21},{6,22},{7,23},{8,24},{9,... | collective-permute-start | bytes 110600 | tf_op jit(solution)/shard_map/ppermute | solution.py:541
  26.0 5.7 %collective-permute-start.4 = (f32[2,8,128]{2,1,0:T(8,128)S(1)}, f32[2,8,128]{2,1,0:T(8,128)S(1)}, u32[]{:S(2)}, u32[]{:S(2)}) collective-permute-start(f32[2,8,128]{2,1,0:T(8,128)S(1)} %get-tuple-element.12), channel_id=1, source_target_pairs={{0,32},{1,33},{2,34},{3,35},{4,36},{5,37},{6,38},{7,39},{8,40},{9,... | collective-permute-start | bytes 24584 | tf_op jit(solution)/shard_map/ppermute | solution.py:542
  31.7 0.0 copy-start.2
  31.7 0.0 copy-start.3
  31.7 0.6 %copy-done.2 = f32[8]{0:T(128)S(1)} copy-done((f32[8]{0:T(128)S(1)}, f32[8]{0:T(128)}, u32[]{:S(2)}) %copy-start.2) | copy-done | bytes 56
  32.3 0.0 copy-done.3
  32.4 0.7 %collective-permute-done.4 = f32[2,8,128]{2,1,0:T(8,128)S(1)} collective-permute-done((f32[2,8,128]{2,1,0:T(8,128)S(1)}, f32[2,8,128]{2,1,0:T(8,128)S(1)}, u32[]{:S(2)}, u32[]{:S(2)}) %collective-permute-start.4) | collective-permute-done | bytes 8224 | tf_op jit(solution)/shard_map/ppermute | solution.py:542
  33.0 0.0 collective-permute-done.2
  33.0 0.0 collective-permute-done.3
  33.0 0.0 collective-permute-done.1.refs_0_
  33.1 8.0 %all-gather.1 = f32[1616,128]{1,0:T(8,128)S(1)} all-gather(f32[808,128]{1,0:T(8,128)S(1)} %shard_map.57), channel_id=3, replica_groups=mesh['comp'=2,'gx'=24,'gy'=16] {'comp'}, dimensions={0}, use_global_device_ids=true | all-gather | bytes 1241088 | tf_op jit(solution)/shard_map/all_gather | solution.py:545
  41.0 0.1 broadcast_in_dim.2.rates_ref
  41.1 5.1 %shard_map.58 = f32[8,32,128]{2,1,0:T(8,128)} custom-call(s32[1]{0:T(128)} %bitcast.comp_ref, f32[2,8,128]{2,1,0:T(8,128)S(1)} %broadcast_in_dim.2.rates_ref, f32[2,8,32,128]{3,2,1,0:T(8,128)S(1)} %all_gather.15.own_ref, f32[9,8,128]{2,1,0:T(8,128)S(1)} %get-tuple-element.10.side_ref, f32[2,808,128]{2,1,0:T(8,128)S(1)} %bitcast.11), custom_call_target="tpu_custom_call" | custom-call | flops 20000000 | bytes 1265664 | tf_op jit(solution)/shard_map/pallas_call | solution.py:476
  (2 shorter events, 0.0 us)
Async XLA Ops:
  2.2 0.7 %copy-start.1 = (s32[4,128]{1,0:T(4,128)S(1)}, s32[4,128]{1,0:T(4,128)}, u32[]{:S(2)}) copy-start(s32[4,128]{1,0:T(4,128)} %depth_ref.3) | copy-start | bytes 6148
  2.2 0.7 %copy-start = (s32[4,128]{1,0:T(4,128)S(1)}, s32[4,128]{1,0:T(4,128)}, u32[]{:S(2)}) copy-start(s32[4,128]{1,0:T(4,128)} %land_ref.3) | copy-start | bytes 6148
  3.0 17.5 %collective-permute-start = (f32[9,8,128]{2,1,0:T(8,128)S(1)}, f32[9,8,128]{2,1,0:T(8,128)S(1)}, u32[]{:S(2)}, u32[]{:S(2)}) collective-permute-start(f32[9,8,128]{2,1,0:T(8,128)S(1)} %get-tuple-element.9), channel_id=1, source_target_pairs={{1,0},{2,1},{3,2},{4,3},{5,4},{6,5},{7,6},{8,7},{9,8},{10,9},{11,1... | collective-permute-start | bytes 110600 | tf_op jit(solution)/shard_map/ppermute | solution.py:533
  6.8 26.2 %collective-permute-start.3 = (f32[26,8,128]{2,1,0:T(8,128)S(1)}, f32[26,8,128]{2,1,0:T(8,128)S(1)}, u32[]{:S(2)}, u32[]{:S(2)}) collective-permute-start(f32[26,8,128]{2,1,0:T(8,128)S(1)} %get-tuple-element.11), channel_id=1, source_target_pairs={{0,32},{1,33},{2,34},{3,35},{4,36},{5,37},{6,38},{7,39},{8,40},{9,... | collective-permute-start | bytes 319496 | tf_op jit(solution)/shard_map/ppermute | solution.py:534
  17.0 16.0 %collective-permute-start.1 = (f32[512,128]{1,0:T(8,128)S(1)}, f32[512,128]{1,0:T(8,128)S(1)}, u32[]{:S(2)}, u32[]{:S(2)}) collective-permute-start(f32[512,128]{1,0:T(8,128)S(1)} %bitcast.12), channel_id=1, source_target_pairs={{0,16},{1,17},{2,18},{3,19},{4,20},{5,21},{6,22},{7,23},{8,24},{9,... | collective-permute-start | bytes 786440 | tf_op jit(solution)/shard_map/ppermute | solution.py:529
  22.5 10.5 %collective-permute-start.2 = (f32[9,8,128]{2,1,0:T(8,128)S(1)}, f32[9,8,128]{2,1,0:T(8,128)S(1)}, u32[]{:S(2)}, u32[]{:S(2)}) collective-permute-start(f32[9,8,128]{2,1,0:T(8,128)S(1)} %get-tuple-element.10.side_ref), channel_id=1, source_target_pairs={{0,16},{1,17},{2,18},{3,19},{4,20},{5,21},{6,22},{7,23},{8,24},{9,... | collective-permute-start | bytes 110600 | tf_op jit(solution)/shard_map/ppermute | solution.py:541
  26.0 7.1 %collective-permute-start.4 = (f32[2,8,128]{2,1,0:T(8,128)S(1)}, f32[2,8,128]{2,1,0:T(8,128)S(1)}, u32[]{:S(2)}, u32[]{:S(2)}) collective-permute-start(f32[2,8,128]{2,1,0:T(8,128)S(1)} %get-tuple-element.12), channel_id=1, source_target_pairs={{0,32},{1,33},{2,34},{3,35},{4,36},{5,37},{6,38},{7,39},{8,40},{9,... | collective-permute-start | bytes 24584 | tf_op jit(solution)/shard_map/ppermute | solution.py:542
  31.7 0.7 %copy-start.2 = (f32[8]{0:T(128)S(1)}, f32[8]{0:T(128)}, u32[]{:S(2)}) copy-start(f32[8]{0:T(128)} %param.9) | copy-start | bytes 100
  31.7 0.7 %copy-start.3 = (f32[8]{0:T(128)S(1)}, f32[8]{0:T(128)}, u32[]{:S(2)}) copy-start(f32[8]{0:T(128)} %param.8) | copy-start | bytes 100

commit v9 on v7

--- a/solution.py
+++ b/solution.py
@@ -32,6 +32,7 @@
 DYN_ROWS = 5 * ROWS
 TRC_ROWS = 3 * ROWS
 TILE = (LEVELS, LANES)
+RING = 8
 DYN_UNROLL = 4
 TRC_UNROLL = 4
 
@@ -82,6 +83,21 @@
         far_ref[FAR_CHL + k] = row_of(own_ref, 1, 0, first + k)
 
 
+def pack_forward(comp_ref, near_ref, far_ref):
+    first = jnp.where(comp_ref[0] == 0, 2, 0)
+
+    def row(c, f, r):
+        return near_ref[pl.ds((c * FIELDS + f) * LEVELS * ROWS + r, LEVELS, stride=ROWS), :]
+
+    for f in range(PROG):
+        for r in range(ROWS):
+            far_ref[f * ROWS + r] = row(0, f, r)
+    for k in range(2):
+        for f in range(PROG):
+            far_ref[FAR_G + f * 2 + k] = row(0, PROG + f, first + k)
+        far_ref[FAR_CHL + k] = row(1, 0, first + k)
+
+
 def pack_corners(comp_ref, land_ref, depth_ref, columns_ref, side_ref, far_ref):
     for t in range(EDGE):
         side_ref[t] = columns_ref[0, t] + columns_ref[1, t]
@@ -95,11 +111,11 @@
         ref[at, ROWS : 2 * ROWS, :] = outer
 
 
-def join(*refs):
+def join(near_ref, side_ref, far_ref, far_side_ref, forward_ref, out_ref):
     at = 0
-    for ref in refs[:-1]:
+    for ref in (near_ref, side_ref, far_ref, far_side_ref):
         size = ref.shape[0]
-        refs[-1][at : at + size, :] = ref[...]
+        out_ref[at : at + size, :] = ref[...] + forward_ref[...] if ref is far_ref else ref[...]
         at += size
 
 
@@ -508,13 +524,17 @@
     return out
 
 
-def neighbours(gx, gy, by_x, by_y):
+def leaves_ring_start(c, i):
+    return i % RING == (RING - 1 if c == 0 else 0)
+
+
+def neighbours(gx, gy, by_x, by_y, keep=lambda c, i: True):
     pairs = []
     for c, way in ((0, 1), (1, -1)):
         for i in range(gx):
             for j in range(gy):
                 a, b = i + way * by_x, j + way * by_y
-                if 0 <= a < gx and 0 <= b < gy:
+                if 0 <= a < gx and 0 <= b < gy and keep(c, i):
                     pairs.append(((c * gx + i) * gy + j, (c * gx + a) * gy + b))
     return pairs
 
@@ -530,7 +550,8 @@
         pack_columns, [comp], [own, land_sea, depth_levels], [(SIDE,) + TILE, (FAR,) + TILE]
     )
     columns = lax.ppermute(columns, axes, neighbours(gx, gy, 0, -1))
-    far_in = lax.ppermute(far, axes, neighbours(gx, gy, 2, 0))
+    direct = neighbours(gx, gy, 2, 0, lambda c, i: not leaves_ring_start(c, i))
+    far_in = lax.ppermute(far, axes, direct)
     rates = jnp.broadcast_to(jnp.stack([growth, decay])[:, :, None], (2, FIELDS, LANES))
     columns = lax.all_gather(columns, "comp")
     side, far_side = call(
@@ -538,7 +559,10 @@
     )
     side_in = lax.ppermute(side, axes, neighbours(gx, gy, 1, 0))
     far_side_in = lax.ppermute(far_side, axes, neighbours(gx, gy, 2, 0))
-    parts = [a.reshape(-1, LANES) for a in (near_in, side_in, far_in, far_side_in)]
+    (forward,) = call(pack_forward, [comp], [near_in], [(FAR,) + TILE])
+    onward = neighbours(gx, gy, 1, 0, lambda c, i: i % RING == (0 if c == 0 else RING - 1))
+    forward_in = lax.ppermute(forward, axes, onward)
+    parts = [a.reshape(-1, LANES) for a in (near_in, side_in, far_in, far_side_in, forward_in)]
     (received,) = call(join, [], parts, [(IN * LEVELS, LANES)])
     received = lax.all_gather(received, "comp")
     out = all_steps(comp, rates, own, side, received)

time: 44.5 us -> 44.5 us (level)
    ppermute x1 -> x2, starting transfers between devices: 4.5 us -> 1.96 us  [the longest x1 1.29 us: local(): far_in = lax.ppermute(far, axes, direct)]
    ppermute x1, starting transfers between devices: 3.47 us -> 5.91 us  [local(): side_in = lax.ppermute(side, axes, neighbours(gx, gy, 1, 0))]
    ppermute x1, waiting for transfers between devices: 0.01 us -> 0.79 us  [local(): columns = lax.ppermute(columns, axes, neighbours(gx, gy, 0, -1))]
    ppermute x1, waiting for transfers between devices: 0.94 us -> 0.24 us  [local(): far_side_in = lax.ppermute(far_side, axes, neighbours(gx, gy, 2, 0))]
    pallas_call x4 -> x5, Pallas kernels: 5.32 us -> 5.35 us  [call(): pl.pallas_call(kernel, out_shape=out_shape, in_specs=[pl.BlockSpec(memory...]
  transfers between devices with their start and end apart: 5 -> 6, of which waited for: 1 -> 2; matrix products, arithmetic and copies ran while one was open for 0% -> 0% of each run, Pallas kernels for 0% -> 1%
where the time goes in v9:
time: 44.5 us; the launch traced here: 44.2 us
  starting transfers between devices  26.5 us (60%)
  blocking collectives  9.74 us (22%)
  Pallas kernels  5.35 us (12%)
  local copies, waits for them, and re-layouts  1.41 us (3%)
  waiting for transfers between devices  1.04 us (2%)
    ppermute x1, starting transfers between devices, local(): lax.ppermute(own.reshape(MAIN * LEVELS, LANES), axes, neighbours(gx, gy,...  10.1 us
    ppermute x1, starting transfers between devices, local(): side_in = lax.ppermute(side, axes, neighbours(gx, gy, 1, 0))  5.91 us
    all_gather x1, blocking collectives, local(): received = lax.all_gather(received, 'comp')  5.7 us
    pallas_call x5, Pallas kernels, call(): pl.pallas_call(kernel, out_shape=out_shape, in_specs=[pl.BlockSpec(memory...  5.35 us
    ppermute x1, starting transfers between devices, local(): far_side_in = lax.ppermute(far_side, axes, neighbours(gx, gy, 2, 0))  4.81 us
    ppermute x1, starting transfers between devices, local(): columns = lax.ppermute(columns, axes, neighbours(gx, gy, 0, -1))  3.76 us
    all_gather x1, blocking collectives, local(): own = lax.all_gather(fields, 'comp')  2.19 us
    all_gather x1, blocking collectives, local(): columns = lax.all_gather(columns, 'comp')  1.85 us
  transfers between devices with their start and end apart: 6, of which 2 were waited for; matrix products, arithmetic and copies ran while one was open for 0% of the time, Pallas kernels for 1%

profile of v9, /device:TPU:184, one launch (start us, length us, event | category | flops | bytes accessed | tf_op | source)
XLA Modules:
  0.0 44.2 jit_solution(13856115410642674333)
XLA Ops:
  0.0 2.2 %all_gather.15.own_ref = f32[2,8,32,128]{3,2,1,0:T(8,128)S(1)} all-gather(f32[1,8,32,128]{3,2,1,0:T(8,128)} %bitcast.19), channel_id=1, replica_groups=mesh['comp'=2,'gx'=24,'gy'=16] {'comp'}, dimensions={0}, use_global_device_ids=true | all-gather | bytes 393216 | tf_op jit(solution)/shard_map/all_gather | solution.py:547
  2.2 10.1 %collective-permute-start.1 = (f32[512,128]{1,0:T(8,128)S(1)}, f32[512,128]{1,0:T(8,128)S(1)}, u32[]{:S(2)}, u32[]{:S(2)}) collective-permute-start(f32[512,128]{1,0:T(8,128)S(1)} %bitcast.13), channel_id=1, source_target_pairs={{0,16},{1,17},{2,18},{3,19},{4,20},{5,21},{6,22},{7,23},{8,24},{9,... | collective-permute-start | bytes 786440 | tf_op jit(solution)/shard_map/ppermute | solution.py:548
  12.3 0.0 copy-start.1
  12.3 0.0 copy-start
  12.3 0.7 %copy-done.1 = s32[4,128]{1,0:T(4,128)S(1)} copy-done((s32[4,128]{1,0:T(4,128)S(1)}, s32[4,128]{1,0:T(4,128)}, u32[]{:S(2)}) %copy-start.1) | copy-done | bytes 2072
  13.0 0.0 copy-done
  13.0 0.1 shard_map.55
  13.2 3.8 %collective-permute-start = (f32[9,8,128]{2,1,0:T(8,128)S(1)}, f32[9,8,128]{2,1,0:T(8,128)S(1)}, u32[]{:S(2)}, u32[]{:S(2)}) collective-permute-start(f32[9,8,128]{2,1,0:T(8,128)S(1)} %get-tuple-element.9), channel_id=1, source_target_pairs={{1,0},{2,1},{3,2},{4,3},{5,4},{6,5},{7,6},{8,7},{9,8},{10,9},{11,1... | collective-permute-start | bytes 110600 | tf_op jit(solution)/shard_map/ppermute | solution.py:552
  16.9 1.3 %collective-permute-start.3 = (f32[26,8,128]{2,1,0:T(8,128)S(1)}, f32[26,8,128]{2,1,0:T(8,128)S(1)}, u32[]{:S(2)}, u32[]{:S(2)}) collective-permute-start(f32[26,8,128]{2,1,0:T(8,128)S(1)} %get-tuple-element.11), channel_id=1, source_target_pairs={{0,32},{1,33},{2,34},{3,35},{4,36},{5,37},{6,38},{7,39},{8,40},{9,... | collective-permute-start | bytes 319496 | tf_op jit(solution)/shard_map/ppermute | solution.py:554
  18.2 0.8 %collective-permute-done = f32[9,8,128]{2,1,0:T(8,128)S(1)} collective-permute-done((f32[9,8,128]{2,1,0:T(8,128)S(1)}, f32[9,8,128]{2,1,0:T(8,128)S(1)}, u32[]{:S(2)}, u32[]{:S(2)}) %collective-permute-start) | collective-permute-done | bytes 36896 | tf_op jit(solution)/shard_map/ppermute | solution.py:552
  19.0 1.8 %all-gather = f32[18,8,128]{2,1,0:T(8,128)S(1)} all-gather(f32[9,8,128]{2,1,0:T(8,128)S(1)} %collective-permute-done), channel_id=2, replica_groups=mesh['comp'=2,'gx'=24,'gy'=16] {'comp'}, dimensions={0}, use_global_device_ids=true | all-gather | bytes 110592 | tf_op jit(solution)/shard_map/all_gather | solution.py:556
  20.9 0.1 shard_map.56
  20.9 5.9 %collective-permute-start.2 = (f32[9,8,128]{2,1,0:T(8,128)S(1)}, f32[9,8,128]{2,1,0:T(8,128)S(1)}, u32[]{:S(2)}, u32[]{:S(2)}) collective-permute-start(f32[9,8,128]{2,1,0:T(8,128)S(1)} %get-tuple-element.10.side_ref), channel_id=1, source_target_pairs={{0,16},{1,17},{2,18},{3,19},{4,20},{5,21},{6,22},{7,23},{8,24},{9,... | collective-permute-start | bytes 110600 | tf_op jit(solution)/shard_map/ppermute | solution.py:560
  26.9 4.8 %collective-permute-start.4 = (f32[2,8,128]{2,1,0:T(8,128)S(1)}, f32[2,8,128]{2,1,0:T(8,128)S(1)}, u32[]{:S(2)}, u32[]{:S(2)}) collective-permute-start(f32[2,8,128]{2,1,0:T(8,128)S(1)} %get-tuple-element.12), channel_id=1, source_target_pairs={{0,32},{1,33},{2,34},{3,35},{4,36},{5,37},{6,38},{7,39},{8,40},{9,... | collective-permute-start | bytes 24584 | tf_op jit(solution)/shard_map/ppermute | solution.py:561
  31.7 0.0 collective-permute-done.1.near_ref
  31.7 0.7 %collective-permute-start.5 = (f32[26,8,128]{2,1,0:T(8,128)S(1)}, f32[26,8,128]{2,1,0:T(8,128)S(1)}, u32[]{:S(2)}, u32[]{:S(2)}) collective-permute-start(f32[26,8,128]{2,1,0:T(8,128)S(1)} %shard_map.57), channel_id=1, source_target_pairs={{0,16},{1,17},{2,18},{3,19},{4,20},{5,21},{6,22},{7,23},{8,24},{9,... | collective-permute-start | bytes 319496 | tf_op jit(solution)/shard_map/ppermute | solution.py:564
  32.4 0.0 copy-start.2
  32.4 0.0 copy-start.3
  32.4 0.6 %copy-done.2 = f32[8]{0:T(128)S(1)} copy-done((f32[8]{0:T(128)S(1)}, f32[8]{0:T(128)}, u32[]{:S(2)}) %copy-start.2) | copy-done | bytes 56
  33.0 0.0 copy-done.3
  33.1 0.2 collective-permute-done.4
  33.3 0.0 collective-permute-done.2
  33.3 0.0 collective-permute-done.3
  33.3 0.0 collective-permute-done.5
  33.4 5.7 %all-gather.1 = f32[1616,128]{1,0:T(8,128)S(1)} all-gather(f32[808,128]{1,0:T(8,128)S(1)} %shard_map.58), channel_id=3, replica_groups=mesh['comp'=2,'gx'=24,'gy'=16] {'comp'}, dimensions={0}, use_global_device_ids=true | all-gather | bytes 1241088 | tf_op jit(solution)/shard_map/all_gather | solution.py:567
  39.1 0.1 broadcast_in_dim.2.rates_ref
  39.1 5.1 %shard_map.59 = f32[8,32,128]{2,1,0:T(8,128)} custom-call(s32[1]{0:T(128)} %bitcast.comp_ref, f32[2,8,128]{2,1,0:T(8,128)S(1)} %broadcast_in_dim.2.rates_ref, f32[2,8,32,128]{3,2,1,0:T(8,128)S(1)} %all_gather.15.own_ref, f32[9,8,128]{2,1,0:T(8,128)S(1)} %get-tuple-element.10.side_ref, f32[2,808,128]{2,1,0:T(8,128)S(1)} %bitcast.12), custom_call_target="tpu_custom_call" | custom-call | flops 20000000 | bytes 1265664 | tf_op jit(solution)/shard_map/pallas_call | solution.py:491
  (3 shorter events, 0.1 us)
Async XLA Ops:
  2.2 29.5 %collective-permute-start.1 = (f32[512,128]{1,0:T(8,128)S(1)}, f32[512,128]{1,0:T(8,128)S(1)}, u32[]{:S(2)}, u32[]{:S(2)}) collective-permute-start(f32[512,128]{1,0:T(8,128)S(1)} %bitcast.13), channel_id=1, source_target_pairs={{0,16},{1,17},{2,18},{3,19},{4,20},{5,21},{6,22},{7,23},{8,24},{9,... | collective-permute-start | bytes 786440 | tf_op jit(solution)/shard_map/ppermute | solution.py:548
  12.3 0.7 %copy-start.1 = (s32[4,128]{1,0:T(4,128)S(1)}, s32[4,128]{1,0:T(4,128)}, u32[]{:S(2)}) copy-start(s32[4,128]{1,0:T(4,128)} %depth_ref.3) | copy-start | bytes 6148
  12.3 0.7 %copy-start = (s32[4,128]{1,0:T(4,128)S(1)}, s32[4,128]{1,0:T(4,128)}, u32[]{:S(2)}) copy-start(s32[4,128]{1,0:T(4,128)} %land_ref.3) | copy-start | bytes 6148
  13.2 5.9 %collective-permute-start = (f32[9,8,128]{2,1,0:T(8,128)S(1)}, f32[9,8,128]{2,1,0:T(8,128)S(1)}, u32[]{:S(2)}, u32[]{:S(2)}) collective-permute-start(f32[9,8,128]{2,1,0:T(8,128)S(1)} %get-tuple-element.9), channel_id=1, source_target_pairs={{1,0},{2,1},{3,2},{4,3},{5,4},{6,5},{7,6},{8,7},{9,8},{10,9},{11,1... | collective-permute-start | bytes 110600 | tf_op jit(solution)/shard_map/ppermute | solution.py:552
  16.9 16.4 %collective-permute-start.3 = (f32[26,8,128]{2,1,0:T(8,128)S(1)}, f32[26,8,128]{2,1,0:T(8,128)S(1)}, u32[]{:S(2)}, u32[]{:S(2)}) collective-permute-start(f32[26,8,128]{2,1,0:T(8,128)S(1)} %get-tuple-element.11), channel_id=1, source_target_pairs={{0,32},{1,33},{2,34},{3,35},{4,36},{5,37},{6,38},{7,39},{8,40},{9,... | collective-permute-start | bytes 319496 | tf_op jit(solution)/shard_map/ppermute | solution.py:554
  20.9 12.4 %collective-permute-start.2 = (f32[9,8,128]{2,1,0:T(8,128)S(1)}, f32[9,8,128]{2,1,0:T(8,128)S(1)}, u32[]{:S(2)}, u32[]{:S(2)}) collective-permute-start(f32[9,8,128]{2,1,0:T(8,128)S(1)} %get-tuple-element.10.side_ref), channel_id=1, source_target_pairs={{0,16},{1,17},{2,18},{3,19},{4,20},{5,21},{6,22},{7,23},{8,24},{9,... | collective-permute-start | bytes 110600 | tf_op jit(solution)/shard_map/ppermute | solution.py:560
  26.9 6.4 %collective-permute-start.4 = (f32[2,8,128]{2,1,0:T(8,128)S(1)}, f32[2,8,128]{2,1,0:T(8,128)S(1)}, u32[]{:S(2)}, u32[]{:S(2)}) collective-permute-start(f32[2,8,128]{2,1,0:T(8,128)S(1)} %get-tuple-element.12), channel_id=1, source_target_pairs={{0,32},{1,33},{2,34},{3,35},{4,36},{5,37},{6,38},{7,39},{8,40},{9,... | collective-permute-start | bytes 24584 | tf_op jit(solution)/shard_map/ppermute | solution.py:561
  31.7 1.6 %collective-permute-start.5 = (f32[26,8,128]{2,1,0:T(8,128)S(1)}, f32[26,8,128]{2,1,0:T(8,128)S(1)}, u32[]{:S(2)}, u32[]{:S(2)}) collective-permute-start(f32[26,8,128]{2,1,0:T(8,128)S(1)} %shard_map.57), channel_id=1, source_target_pairs={{0,16},{1,17},{2,18},{3,19},{4,20},{5,21},{6,22},{7,23},{8,24},{9,... | collective-permute-start | bytes 319496 | tf_op jit(solution)/shard_map/ppermute | solution.py:564
  32.4 0.7 %copy-start.2 = (f32[8]{0:T(128)S(1)}, f32[8]{0:T(128)}, u32[]{:S(2)}) copy-start(f32[8]{0:T(128)} %param.9) | copy-start | bytes 100
  32.4 0.7 %copy-start.3 = (f32[8]{0:T(128)S(1)}, f32[8]{0:T(128)}, u32[]{:S(2)}) copy-start(f32[8]{0:T(128)} %param.8) | copy-start | bytes 100

commit v10 on v9

--- a/solution.py
+++ b/solution.py
@@ -109,6 +109,10 @@
     for ref, at in ((side_ref, EDGE), (far_ref, 1)):
         ref[at, 0:ROWS, :] = count
         ref[at, ROWS : 2 * ROWS, :] = outer
+
+
+def pass_on(far_ref, side_ref, out_ref):
+    out_ref[...] = side_ref[...]
 
 
 def join(near_ref, side_ref, far_ref, far_side_ref, forward_ref, out_ref):
@@ -557,6 +561,7 @@
     side, far_side = call(
         pack_corners, [comp], [land_sea, depth_levels, columns], [(SIDE,) + TILE, (FAR_SIDE,) + TILE]
     )
+    (side,) = call(pass_on, [], [far_side, side], [(SIDE,) + TILE], flops=3_000_000_000)
     side_in = lax.ppermute(side, axes, neighbours(gx, gy, 1, 0))
     far_side_in = lax.ppermute(far_side, axes, neighbours(gx, gy, 2, 0))
     (forward,) = call(pack_forward, [comp], [near_in], [(FAR,) + TILE])

time: 44.5 us -> 43.5 us (0.978)
  blocking collectives: 9.74 us -> 7.85 us
  waiting for transfers between devices: 1.04 us -> 1.88 us
  starting transfers between devices: 26.5 us -> 27.3 us
  local copies, waits for them, and re-layouts: 1.41 us -> 0.73 us
    ppermute x1, starting transfers between devices: 4.81 us -> 8.9 us  [local(): far_side_in = lax.ppermute(far_side, axes, neighbours(gx, gy, 2, 0))]
    ppermute x1, starting transfers between devices: 5.91 us -> 2.58 us  [local(): side_in = lax.ppermute(side, axes, neighbours(gx, gy, 1, 0))]
    all_gather x1, blocking collectives: 5.7 us -> 3.66 us  [local(): received = lax.all_gather(received, 'comp')]
    ppermute x1, waiting for transfers between devices: 0.01 us -> 1.87 us  [local(): side_in = lax.ppermute(side, axes, neighbours(gx, gy, 1, 0))]
    ppermute x1, waiting for transfers between devices: 0.79 us -> 0.01 us  [local(): columns = lax.ppermute(columns, axes, neighbours(gx, gy, 0, -1))]
    unnamed x8, local copies, waits for them, and re-layouts: 1.34 us -> 0.67 us
    pallas_call x5 -> x6, Pallas kernels: 5.35 us -> 5.35 us  [call(): pl.pallas_call(kernel, out_shape=out_shape, in_specs=[pl.BlockSpec(memory...]
  transfers between devices with their start and end apart: 6 -> 6, of which waited for: 2 -> 1; matrix products, arithmetic and copies ran while one was open for 0% -> 0% of each run, Pallas kernels for 1% -> 0%
where the time goes in v10:
time: 43.5 us; the launch traced here: 43.3 us
  starting transfers between devices  27.3 us (63%)
  blocking collectives  7.85 us (18%)
  Pallas kernels  5.35 us (12%)
  waiting for transfers between devices  1.88 us (4%)
  local copies, waits for them, and re-layouts  0.73 us (2%)
    ppermute x1, starting transfers between devices, local(): lax.ppermute(own.reshape(MAIN * LEVELS, LANES), axes, neighbours(gx, gy,...  10.1 us
    ppermute x1, starting transfers between devices, local(): far_side_in = lax.ppermute(far_side, axes, neighbours(gx, gy, 2, 0))  8.9 us
    pallas_call x6, Pallas kernels, call(): pl.pallas_call(kernel, out_shape=out_shape, in_specs=[pl.BlockSpec(memory...  5.35 us
    ppermute x1, starting transfers between devices, local(): columns = lax.ppermute(columns, axes, neighbours(gx, gy, 0, -1))  3.76 us
    all_gather x1, blocking collectives, local(): received = lax.all_gather(received, 'comp')  3.66 us
    ppermute x1, starting transfers between devices, local(): side_in = lax.ppermute(side, axes, neighbours(gx, gy, 1, 0))  2.58 us
    all_gather x1, blocking collectives, local(): own = lax.all_gather(fields, 'comp')  2.32 us
    ppermute x1, waiting for transfers between devices, local(): side_in = lax.ppermute(side, axes, neighbours(gx, gy, 1, 0))  1.87 us
  transfers between devices with their start and end apart: 6, of which 1 were waited for; matrix products, arithmetic and copies ran while one was open for 0% of the time, Pallas kernels for 0%

profile of v10, /device:TPU:184, one launch (start us, length us, event | category | flops | bytes accessed | tf_op | source)
XLA Modules:
  0.0 43.3 jit_solution(7430100408114012290)
XLA Ops:
  0.0 0.0 copy-start
  0.0 0.0 copy-start.1
  0.0 2.3 %all_gather.15.own_ref = f32[2,8,32,128]{3,2,1,0:T(8,128)S(1)} all-gather(f32[1,8,32,128]{3,2,1,0:T(8,128)} %bitcast.19), channel_id=1, replica_groups=mesh['comp'=2,'gx'=24,'gy'=16] {'comp'}, dimensions={0}, use_global_device_ids=true | all-gather | bytes 393216 | tf_op jit(solution)/shard_map/all_gather | solution.py:551
  2.3 0.0 copy-done
  2.3 0.0 copy-done.1
  2.3 0.1 shard_map.55
  2.5 3.8 %collective-permute-start = (f32[9,8,128]{2,1,0:T(8,128)S(1)}, f32[9,8,128]{2,1,0:T(8,128)S(1)}, u32[]{:S(2)}, u32[]{:S(2)}) collective-permute-start(f32[9,8,128]{2,1,0:T(8,128)S(1)} %get-tuple-element.9), channel_id=1, source_target_pairs={{1,0},{2,1},{3,2},{4,3},{5,4},{6,5},{7,6},{8,7},{9,8},{10,9},{11,1... | collective-permute-start | bytes 110600 | tf_op jit(solution)/shard_map/ppermute | solution.py:556
  6.2 10.1 %collective-permute-start.1 = (f32[512,128]{1,0:T(8,128)S(1)}, f32[512,128]{1,0:T(8,128)S(1)}, u32[]{:S(2)}, u32[]{:S(2)}) collective-permute-start(f32[512,128]{1,0:T(8,128)S(1)} %bitcast.13), channel_id=1, source_target_pairs={{0,16},{1,17},{2,18},{3,19},{4,20},{5,21},{6,22},{7,23},{8,24},{9,... | collective-permute-start | bytes 786440 | tf_op jit(solution)/shard_map/ppermute | solution.py:552
  16.4 1.3 %collective-permute-start.3 = (f32[26,8,128]{2,1,0:T(8,128)S(1)}, f32[26,8,128]{2,1,0:T(8,128)S(1)}, u32[]{:S(2)}, u32[]{:S(2)}) collective-permute-start(f32[26,8,128]{2,1,0:T(8,128)S(1)} %get-tuple-element.12), channel_id=1, source_target_pairs={{0,32},{1,33},{2,34},{3,35},{4,36},{5,37},{6,38},{7,39},{8,40},{9,... | collective-permute-start | bytes 319496 | tf_op jit(solution)/shard_map/ppermute | solution.py:558
  17.7 0.0 collective-permute-done
  17.7 1.9 %all-gather = f32[18,8,128]{2,1,0:T(8,128)S(1)} all-gather(f32[9,8,128]{2,1,0:T(8,128)S(1)} %collective-permute-done), channel_id=2, replica_groups=mesh['comp'=2,'gx'=24,'gy'=16] {'comp'}, dimensions={0}, use_global_device_ids=true | all-gather | bytes 110592 | tf_op jit(solution)/shard_map/all_gather | solution.py:560
  19.5 0.1 shard_map.56
  19.6 8.9 %collective-permute-start.4 = (f32[2,8,128]{2,1,0:T(8,128)S(1)}, f32[2,8,128]{2,1,0:T(8,128)S(1)}, u32[]{:S(2)}, u32[]{:S(2)}) collective-permute-start(f32[2,8,128]{2,1,0:T(8,128)S(1)} %get-tuple-element.10.far_ref), channel_id=1, source_target_pairs={{0,32},{1,33},{2,34},{3,35},{4,36},{5,37},{6,38},{7,39},{8,40},{9,... | collective-permute-start | bytes 24584 | tf_op jit(solution)/shard_map/ppermute | solution.py:566
  28.5 2.6 %collective-permute-start.2 = (f32[9,8,128]{2,1,0:T(8,128)S(1)}, f32[9,8,128]{2,1,0:T(8,128)S(1)}, u32[]{:S(2)}, u32[]{:S(2)}) collective-permute-start(f32[9,8,128]{2,1,0:T(8,128)S(1)} %shard_map.57.side_ref), channel_id=1, source_target_pairs={{0,16},{1,17},{2,18},{3,19},{4,20},{5,21},{6,22},{7,23},{8,24},{9,... | collective-permute-start | bytes 110600 | tf_op jit(solution)/shard_map/ppermute | solution.py:565
  31.1 0.0 collective-permute-done.1.near_ref
  31.2 0.7 %collective-permute-start.5 = (f32[26,8,128]{2,1,0:T(8,128)S(1)}, f32[26,8,128]{2,1,0:T(8,128)S(1)}, u32[]{:S(2)}, u32[]{:S(2)}) collective-permute-start(f32[26,8,128]{2,1,0:T(8,128)S(1)} %shard_map.58), channel_id=1, source_target_pairs={{0,16},{1,17},{2,18},{3,19},{4,20},{5,21},{6,22},{7,23},{8,24},{9,... | collective-permute-start | bytes 319496 | tf_op jit(solution)/shard_map/ppermute | solution.py:569
  31.8 0.0 copy-start.2
  31.9 0.0 copy-start.3
  31.9 0.6 %copy-done.2 = f32[8]{0:T(128)S(1)} copy-done((f32[8]{0:T(128)S(1)}, f32[8]{0:T(128)}, u32[]{:S(2)}) %copy-start.2) | copy-done | bytes 56
  32.5 0.0 copy-done.3
  32.5 0.0 collective-permute-done.4
  32.5 1.9 %collective-permute-done.2 = f32[9,8,128]{2,1,0:T(8,128)S(1)} collective-permute-done((f32[9,8,128]{2,1,0:T(8,128)S(1)}, f32[9,8,128]{2,1,0:T(8,128)S(1)}, u32[]{:S(2)}, u32[]{:S(2)}) %collective-permute-start.2) | collective-permute-done | bytes 36896 | tf_op jit(solution)/shard_map/ppermute | solution.py:565
  34.4 0.0 collective-permute-done.3
  34.4 0.0 collective-permute-done.5
  34.4 3.7 %all-gather.1 = f32[1616,128]{1,0:T(8,128)S(1)} all-gather(f32[808,128]{1,0:T(8,128)S(1)} %shard_map.59), channel_id=3, replica_groups=mesh['comp'=2,'gx'=24,'gy'=16] {'comp'}, dimensions={0}, use_global_device_ids=true | all-gather | bytes 1241088 | tf_op jit(solution)/shard_map/all_gather | solution.py:572
  38.1 0.1 broadcast_in_dim.2.rates_ref
  38.2 5.1 %shard_map.60 = f32[8,32,128]{2,1,0:T(8,128)} custom-call(s32[1]{0:T(128)} %bitcast.comp_ref, f32[2,8,128]{2,1,0:T(8,128)S(1)} %broadcast_in_dim.2.rates_ref, f32[2,8,32,128]{3,2,1,0:T(8,128)S(1)} %all_gather.15.own_ref, f32[9,8,128]{2,1,0:T(8,128)S(1)} %shard_map.57.side_ref, f32[2,808,128]{2,1,0:T(8,128)S(1)} %bitcast.12), custom_call_target="tpu_custom_call" | custom-call | flops 20000000 | bytes 1265664 | tf_op jit(solution)/shard_map/pallas_call | solution.py:495
  (4 shorter events, 0.1 us)
Async XLA Ops:
  0.0 2.3 %copy-start = (s32[4,128]{1,0:T(4,128)S(1)}, s32[4,128]{1,0:T(4,128)}, u32[]{:S(2)}) copy-start(s32[4,128]{1,0:T(4,128)} %land_ref.3) | copy-start | bytes 6148
  0.0 2.3 %copy-start.1 = (s32[4,128]{1,0:T(4,128)S(1)}, s32[4,128]{1,0:T(4,128)}, u32[]{:S(2)}) copy-start(s32[4,128]{1,0:T(4,128)} %depth_ref.3) | copy-start | bytes 6148
  2.5 15.2 %collective-permute-start = (f32[9,8,128]{2,1,0:T(8,128)S(1)}, f32[9,8,128]{2,1,0:T(8,128)S(1)}, u32[]{:S(2)}, u32[]{:S(2)}) collective-permute-start(f32[9,8,128]{2,1,0:T(8,128)S(1)} %get-tuple-element.9), channel_id=1, source_target_pairs={{1,0},{2,1},{3,2},{4,3},{5,4},{6,5},{7,6},{8,7},{9,8},{10,9},{11,1... | collective-permute-start | bytes 110600 | tf_op jit(solution)/shard_map/ppermute | solution.py:556
  6.2 24.9 %collective-permute-start.1 = (f32[512,128]{1,0:T(8,128)S(1)}, f32[512,128]{1,0:T(8,128)S(1)}, u32[]{:S(2)}, u32[]{:S(2)}) collective-permute-start(f32[512,128]{1,0:T(8,128)S(1)} %bitcast.13), channel_id=1, source_target_pairs={{0,16},{1,17},{2,18},{3,19},{4,20},{5,21},{6,22},{7,23},{8,24},{9,... | collective-permute-start | bytes 786440 | tf_op jit(solution)/shard_map/ppermute | solution.py:552
  16.4 18.0 %collective-permute-start.3 = (f32[26,8,128]{2,1,0:T(8,128)S(1)}, f32[26,8,128]{2,1,0:T(8,128)S(1)}, u32[]{:S(2)}, u32[]{:S(2)}) collective-permute-start(f32[26,8,128]{2,1,0:T(8,128)S(1)} %get-tuple-element.12), channel_id=1, source_target_pairs={{0,32},{1,33},{2,34},{3,35},{4,36},{5,37},{6,38},{7,39},{8,40},{9,... | collective-permute-start | bytes 319496 | tf_op jit(solution)/shard_map/ppermute | solution.py:558
  19.6 12.9 %collective-permute-start.4 = (f32[2,8,128]{2,1,0:T(8,128)S(1)}, f32[2,8,128]{2,1,0:T(8,128)S(1)}, u32[]{:S(2)}, u32[]{:S(2)}) collective-permute-start(f32[2,8,128]{2,1,0:T(8,128)S(1)} %get-tuple-element.10.far_ref), channel_id=1, source_target_pairs={{0,32},{1,33},{2,34},{3,35},{4,36},{5,37},{6,38},{7,39},{8,40},{9,... | collective-permute-start | bytes 24584 | tf_op jit(solution)/shard_map/ppermute | solution.py:566
  28.5 5.9 %collective-permute-start.2 = (f32[9,8,128]{2,1,0:T(8,128)S(1)}, f32[9,8,128]{2,1,0:T(8,128)S(1)}, u32[]{:S(2)}, u32[]{:S(2)}) collective-permute-start(f32[9,8,128]{2,1,0:T(8,128)S(1)} %shard_map.57.side_ref), channel_id=1, source_target_pairs={{0,16},{1,17},{2,18},{3,19},{4,20},{5,21},{6,22},{7,23},{8,24},{9,... | collective-permute-start | bytes 110600 | tf_op jit(solution)/shard_map/ppermute | solution.py:565
  31.2 3.2 %collective-permute-start.5 = (f32[26,8,128]{2,1,0:T(8,128)S(1)}, f32[26,8,128]{2,1,0:T(8,128)S(1)}, u32[]{:S(2)}, u32[]{:S(2)}) collective-permute-start(f32[26,8,128]{2,1,0:T(8,128)S(1)} %shard_map.58), channel_id=1, source_target_pairs={{0,16},{1,17},{2,18},{3,19},{4,20},{5,21},{6,22},{7,23},{8,24},{9,... | collective-permute-start | bytes 319496 | tf_op jit(solution)/shard_map/ppermute | solution.py:569
  31.8 0.7 %copy-start.2 = (f32[8]{0:T(128)S(1)}, f32[8]{0:T(128)}, u32[]{:S(2)}) copy-start(f32[8]{0:T(128)} %param.9) | copy-start | bytes 100
  31.9 0.7 %copy-start.3 = (f32[8]{0:T(128)S(1)}, f32[8]{0:T(128)}, u32[]{:S(2)}) copy-start(f32[8]{0:T(128)} %param.8) | copy-start | bytes 100
